TPU v7x, 32 devices: a whole 2x2x4 slice. The times are simulated.
32 devices in a mesh: ctx: 8 (over y, x, core), wt: 4 (over z).
Axes of the slice: x: 2, y: 2, z: 4, core: 2. Of those that a mesh axis runs over, the one named last changes fastest.
Arguments:
- x_in: bfloat16 [4, 2048, 512], P(None, 'ctx'), may hold values from -13 to 13
- grad_out: bfloat16 [4, 2048, 512], P(None, 'ctx'), may hold values from -6 to 6
- seg_ids: int32 [4, 2048], replicated, may hold values from 0 to 2, as said below
- norm1_gain: float32 [512], replicated, may hold values from 0.1 to 1.9
- norm1_bias: float32 [512], replicated, may hold values from -1.75 to 1.75
- q_weight: bfloat16 [512, 512], P(None, 'wt'), may hold values from -0.375 to 0.375
- q_bias: float32 [512], P('wt'), may hold values from -3 to 3
- k_weight: bfloat16 [512, 512], P(None, 'wt'), may hold values from -0.25 to 0.25
- v_weight: bfloat16 [512, 512], P(None, 'wt'), may hold values from -0.25 to 0.25
- v_bias: float32 [512], P('wt'), may hold values from -3 to 3
- out_weight: bfloat16 [512, 512], P('wt'), may hold values from -0.5 to 0.5
- out_bias: float32 [512], replicated, may hold values from -3 to 3
- norm2_gain: float32 [512], replicated, may hold values from 0.1 to 1.9
- norm2_bias: float32 [512], replicated, may hold values from -1.75 to 1.75
- up_weight: bfloat16 [512, 2048], P(None, 'wt'), may hold values from -0.25 to 0.25
- up_bias: float32 [2048], P('wt'), may hold values from -1.75 to 1.75
- down_weight: bfloat16 [2048, 512], P('wt'), may hold values from -0.1875 to 0.1875
- down_bias: float32 [512], replicated, may hold values from -3 to 3
Outputs:
- layer_out: float32 [4, 2048, 512], P(None, 'ctx')
- input_grad: float32 [4, 2048, 512], P(None, 'ctx')
- norm1_gain_grad: float32 [512], P('wt')
- norm1_bias_grad: float32 [512], P('wt')
- q_weight_grad: float32 [512, 512], P(None, 'wt')
- q_bias_grad: float32 [512], P('wt')
- k_weight_grad: float32 [512, 512], P(None, 'wt')
- v_weight_grad: float32 [512, 512], P(None, 'wt')
- v_bias_grad: float32 [512], P('wt')
- out_weight_grad: float32 [512, 512], P('wt')
- out_bias_grad: float32 [512], P('wt')
- norm2_gain_grad: float32 [512], P('wt')
- norm2_bias_grad: float32 [512], P('wt')
- up_weight_grad: float32 [512, 2048], P(None, 'wt')
- up_bias_grad: float32 [2048], P('wt')
- down_weight_grad: float32 [2048, 512], P('wt')
- down_bias_grad: float32 [512], P('wt')
Inputs may be any that keep to these rules, and one draw needn't show every extreme that they name: `seg_ids`: in each micro-batch the segment numbers never fall along the tokens; there are three documents, each present, and the middle one covers tokens on every index of ctx.
All inputs are finite; a program needn't handle non-finite values.
Results may differ from a plain program's by a relative error of at most 0.02.
Values may be sent and summed in bfloat16 or wider, within the bound.
A program may use at most 192 MiB of HBM per device.

v0:
```python
import jax
import jax.numpy as jnp
from jax import lax
from jax.sharding import PartitionSpec as P

HEAD_DIM = 64
BLOCK = 16
LEVELS = 10
FINE = 3


EPSILON = 1e-05
NEGATIVE = -1e30
LOG_TWO = 0.6931471805599453


def from_behind(block, axis, distance):
    devices = range(lax.axis_size(axis))
    route = [(i - distance, i) for i in devices if i - distance in devices]
    return lax.ppermute(block, axis, route)


def shortened(array):

    def short(part):
        return part.astype(jnp.bfloat16) if part.dtype == jnp.float32 else part

    return jax.tree.map(short, array)


def matmul(left, right):
    return jnp.dot(left, right, preferred_element_type=jnp.float32)


def norm_forward(source, gain, shift):
    centre = jnp.mean(source, axis=-1, keepdims=True)
    centred = source - centre
    variance = jnp.mean(centred * centred, axis=-1, keepdims=True)
    inverse = lax.rsqrt(variance + EPSILON)
    normed = centred * inverse
    return (normed * gain + shift, normed, inverse)


def norm_backward(upstream, normed, inverse, gain):
    scaled = upstream * gain
    first_mean = jnp.mean(scaled, axis=-1, keepdims=True)
    second_mean = jnp.mean(scaled * normed, axis=-1, keepdims=True)
    return inverse * (scaled - first_mean - normed * second_mean)


def cell_means(source, cell_size):
    grouped = source.reshape(source.shape[0] // cell_size, cell_size, source.shape[1])
    return jnp.mean(grouped, axis=1, dtype=jnp.float32).astype(jnp.bfloat16)


def spread_back(upstream, cell_size):
    cell_count, columns = upstream.shape
    shared = jnp.broadcast_to((upstream / cell_size)[:, None, :], (cell_count, cell_size, columns))
    return shared.reshape(cell_count * cell_size, columns)


def band_rows(table, start, groups):
    rows = lax.dynamic_slice_in_dim(table, start, BLOCK * (groups + 1), 0)
    stacked = rows.reshape(groups + 1, BLOCK, table.shape[1])
    return jnp.concatenate([stacked[:-1], stacked[1:]], axis=1)


def unband(d_band, table_rows, start, groups):
    columns = d_band.shape[2]
    lower_half = jnp.pad(d_band[:, :BLOCK], ((0, 1), (0, 0), (0, 0)))
    upper_half = jnp.pad(d_band[:, BLOCK:], ((1, 0), (0, 0), (0, 0)))
    flat = (lower_half + upper_half).reshape(BLOCK * (groups + 1), columns)
    return lax.dynamic_update_slice_in_dim(
        jnp.zeros((table_rows, columns), jnp.float32), flat, start, 0
    )


def level_mask(level_at, base_pos, start, per_group, offset, seg_row, tok_dev):
    cell_size = 2**level_at
    span = BLOCK * cell_size
    token_at = jnp.arange(tok_dev, dtype=jnp.int32)[:, None]
    slot_at = jnp.arange(2 * BLOCK, dtype=jnp.int32)[None, :]
    begin = base_pos + cell_size * (start + BLOCK * (token_at // per_group) + slot_at)
    position = offset + token_at
    lower = span * (position // span - 1)
    if level_at == 0:
        upper = position + 1
    else:
        half_span = span // 2
        upper = half_span * (position // half_span - 1)
    inside = (begin >= 0) & (begin >= lower) & (begin + cell_size <= upper)
    last_index = seg_row.shape[0] - 1
    firsts = jnp.take(seg_row, jnp.clip(begin, 0, last_index))
    lasts = jnp.take(seg_row, jnp.clip(begin + cell_size - 1, 0, last_index))
    seg_query = jnp.take(seg_row, position)
    return inside & (firsts == seg_query) & (lasts == seg_query)


def micro_step(source_rows, upstream_rows, seg_row, params, offset, row_start, share):
    (
        norm1_gain,
        norm1_bias,
        q_weight,
        q_bias,
        k_weight,
        v_weight,
        v_bias,
        out_weight,
        out_bias,
        norm2_gain,
        norm2_bias,
        up_weight,
        up_bias,
        down_weight,
        down_bias,
    ) = params
    tok_dev = source_rows.shape[0]
    head_width = q_weight.shape[1]
    local_heads = head_width // HEAD_DIM
    score_scale = HEAD_DIM ** (-0.5)
    tail_len = BLOCK * 2 ** (FINE - 1)
    width = 2 * BLOCK
    source = source_rows.astype(jnp.float32)
    normed1, hat_one, inverse_one = norm_forward(source, norm1_gain, norm1_bias)
    normed1_low = normed1.astype(jnp.bfloat16)
    queries = (matmul(normed1_low, q_weight) + q_bias).astype(jnp.bfloat16)
    keys_own = matmul(normed1_low, k_weight).astype(jnp.bfloat16)
    values_own = (matmul(normed1_low, v_weight) + v_bias).astype(jnp.bfloat16)
    paired = jnp.concatenate([keys_own, values_own], axis=1)
    tail_rows = from_behind(paired[tok_dev - tail_len :], "ctx", 1)
    window = jnp.concatenate([tail_rows, paired], axis=0)
    all_cells = lax.all_gather(cell_means(paired, 2**FINE), "ctx", axis=0, tiled=True)
    base_count = all_cells.shape[0]
    query_heads = queries.reshape(tok_dev, local_heads, HEAD_DIM)
    levels = []
    for level_at in range(LEVELS):
        cell_size = 2**level_at
        span = BLOCK * cell_size
        groups = max(tok_dev // span, 1)
        per_group = tok_dev // groups
        if level_at < FINE:
            table = window if level_at == 0 else cell_means(window, cell_size)
            base_pos = offset - tail_len
            start = tail_len // cell_size - BLOCK
        else:
            cells = all_cells if level_at == FINE else cell_means(all_cells, 2 ** (level_at - FINE))
            table = jnp.pad(cells, ((BLOCK, 2 * BLOCK), (0, 0)))
            base_pos = -BLOCK * cell_size
            start = BLOCK * (offset // span)
        band = band_rows(table, start, groups)
        key_band = band[:, :, :head_width].reshape(groups, width, local_heads, HEAD_DIM)
        value_band = band[:, :, head_width:].reshape(groups, width, local_heads, HEAD_DIM)
        allowed = level_mask(level_at, base_pos, start, per_group, offset, seg_row, tok_dev)
        query_groups = query_heads.reshape(groups, per_group, local_heads, HEAD_DIM)
        levels.append(
            (table.shape[0], start, groups, per_group, key_band, value_band, allowed, query_groups)
        )

    def scores_of():
        parts = []
        for level_at in range(LEVELS):
            table_rows, start, groups, per_group, key_band, value_band, allowed, query_groups = (
                levels[level_at]
            )
            raw = jnp.einsum(
                "nqhd,nkhd->hnqk", query_groups, key_band, preferred_element_type=jnp.float32
            )
            raw = raw.reshape(local_heads, tok_dev, width) * score_scale
            parts.append(jnp.where(allowed[None], raw + level_at * LOG_TWO, NEGATIVE))
        return jnp.concatenate(parts, axis=-1)

    scores = scores_of()
    row_top = jnp.max(scores, axis=-1, keepdims=True)
    exponent = jnp.exp(scores - row_top)
    row_total = jnp.sum(exponent, axis=-1, keepdims=True)
    log_total = row_top + jnp.log(row_total)
    probs_low = (exponent / row_total).astype(jnp.bfloat16)
    mixed = jnp.zeros((tok_dev, local_heads, HEAD_DIM), jnp.float32)
    for level_at in range(LEVELS):
        table_rows, start, groups, per_group, key_band, value_band, allowed, query_groups = levels[
            level_at
        ]
        level_probs = probs_low[:, :, level_at * width : (level_at + 1) * width].reshape(
            local_heads, groups, per_group, width
        )
        mixed = mixed + jnp.einsum(
            "hnqk,nkhd->nqhd", level_probs, value_band, preferred_element_type=jnp.float32
        ).reshape(tok_dev, local_heads, HEAD_DIM)
    mixed_low = mixed.reshape(tok_dev, head_width).astype(jnp.bfloat16)
    attended = matmul(mixed_low, out_weight)
    attended = lax.psum(attended, "wt")
    middle = source + attended + out_bias
    normed2, hat_two, inverse_two = norm_forward(middle, norm2_gain, norm2_bias)
    normed2_low = normed2.astype(jnp.bfloat16)
    pre_active = matmul(normed2_low, up_weight) + up_bias
    sigmoid_pre = jax.nn.sigmoid(pre_active)
    hidden_low = (pre_active * sigmoid_pre).astype(jnp.bfloat16)
    branch = matmul(hidden_low, down_weight)
    branch = lax.psum(branch.astype(jnp.bfloat16), "wt").astype(jnp.float32)
    result = middle + branch + down_bias
    grad_two = upstream_rows.astype(jnp.float32)
    d_down = jnp.einsum("tf,td->fd", hidden_low, upstream_rows, preferred_element_type=jnp.float32)
    d_hidden = jnp.einsum(
        "td,fd->tf", upstream_rows, down_weight, preferred_element_type=jnp.float32
    ).astype(jnp.bfloat16)
    slope = sigmoid_pre * (1.0 + pre_active * (1.0 - sigmoid_pre))
    d_up_low = (d_hidden.astype(jnp.float32) * slope).astype(jnp.bfloat16)
    d_up_weight = jnp.einsum("td,tf->df", normed2_low, d_up_low, preferred_element_type=jnp.float32)
    d_up_bias = jnp.sum(d_up_low.astype(jnp.float32), axis=0)
    d_normed2 = jnp.einsum("tf,df->td", d_up_low, up_weight, preferred_element_type=jnp.float32)
    d_normed2 = lax.psum(d_normed2, "wt")
    grad_one = grad_two + norm_backward(d_normed2, hat_two, inverse_two, norm2_gain)
    grad_one_low = grad_one.astype(jnp.bfloat16)
    d_out_weight = jnp.einsum(
        "th,td->hd", mixed_low, grad_one_low, preferred_element_type=jnp.float32
    )
    d_mixed = jnp.einsum(
        "td,hd->th", grad_one_low, out_weight, preferred_element_type=jnp.float32
    ).astype(jnp.bfloat16)
    d_heads = d_mixed.reshape(tok_dev, local_heads, HEAD_DIM)
    probs = jnp.exp(scores_of() - log_total)
    parts = []
    for level_at in range(LEVELS):
        table_rows, start, groups, per_group, key_band, value_band, allowed, query_groups = levels[
            level_at
        ]
        d_groups = d_heads.reshape(groups, per_group, local_heads, HEAD_DIM)
        level_d = jnp.einsum(
            "nqhd,nkhd->hnqk", d_groups, value_band, preferred_element_type=jnp.float32
        )
        parts.append(level_d.reshape(local_heads, tok_dev, width))
    d_probs = jnp.concatenate(parts, axis=-1)
    centre = jnp.sum(probs * d_probs, axis=-1, keepdims=True)
    d_scores = (probs * (d_probs - centre)).astype(jnp.bfloat16)
    d_queries = jnp.zeros((tok_dev, local_heads, HEAD_DIM), jnp.float32)
    d_tables = []
    for level_at in range(LEVELS):
        table_rows, start, groups, per_group, key_band, value_band, allowed, query_groups = levels[
            level_at
        ]
        d_groups = d_heads.reshape(groups, per_group, local_heads, HEAD_DIM)
        level_scores = d_scores[:, :, level_at * width : (level_at + 1) * width].reshape(
            local_heads, groups, per_group, width
        )
        level_probs = probs_low[:, :, level_at * width : (level_at + 1) * width].reshape(
            local_heads, groups, per_group, width
        )
        d_queries = d_queries + jnp.einsum(
            "hnqk,nkhd->nqhd", level_scores, key_band, preferred_element_type=jnp.float32
        ).reshape(tok_dev, local_heads, HEAD_DIM)
        d_key_band = (
            jnp.einsum(
                "hnqk,nqhd->nkhd", level_scores, query_groups, preferred_element_type=jnp.float32
            )
            * score_scale
        )
        d_value_band = jnp.einsum(
            "hnqk,nqhd->nkhd", level_probs, d_groups, preferred_element_type=jnp.float32
        )
        d_band = jnp.concatenate(
            [
                d_key_band.reshape(groups, width, head_width),
                d_value_band.reshape(groups, width, head_width),
            ],
            axis=2,
        )
        d_tables.append(unband(d_band, table_rows, start, groups))
    d_queries = d_queries * score_scale
    d_window = d_tables[0]
    for level_at in range(1, FINE):
        d_window = d_window + spread_back(d_tables[level_at], 2**level_at)
    d_cells = d_tables[FINE][BLOCK : BLOCK + base_count]
    for level_at in range(FINE + 1, LEVELS):
        level_count = base_count // 2 ** (level_at - FINE)
        d_cells = d_cells + spread_back(
            d_tables[level_at][BLOCK : BLOCK + level_count], 2 ** (level_at - FINE)
        )
    own_cells = lax.psum_scatter(
        d_cells.astype(jnp.bfloat16), "ctx", scatter_dimension=0, tiled=True
    ).astype(jnp.float32)
    returned = from_behind(d_window[:tail_len].astype(jnp.bfloat16), "ctx", -1).astype(jnp.float32)
    d_paired = (
        d_window[tail_len:]
        + spread_back(own_cells, 2**FINE)
        + jnp.pad(returned, ((tok_dev - tail_len, 0), (0, 0)))
    )
    d_queries_low = d_queries.reshape(tok_dev, head_width).astype(jnp.bfloat16)
    d_keys_low = d_paired[:, :head_width].astype(jnp.bfloat16)
    d_values_low = d_paired[:, head_width:].astype(jnp.bfloat16)
    d_q_weight = jnp.einsum(
        "td,th->dh", normed1_low, d_queries_low, preferred_element_type=jnp.float32
    )
    d_k_weight = jnp.einsum(
        "td,th->dh", normed1_low, d_keys_low, preferred_element_type=jnp.float32
    )
    d_v_weight = jnp.einsum(
        "td,th->dh", normed1_low, d_values_low, preferred_element_type=jnp.float32
    )
    d_q_bias = jnp.sum(d_queries_low.astype(jnp.float32), axis=0)
    d_v_bias = jnp.sum(d_values_low.astype(jnp.float32), axis=0)
    d_normed1 = (
        jnp.einsum("th,dh->td", d_queries_low, q_weight, preferred_element_type=jnp.float32)
        + jnp.einsum("th,dh->td", d_keys_low, k_weight, preferred_element_type=jnp.float32)
        + jnp.einsum("th,dh->td", d_values_low, v_weight, preferred_element_type=jnp.float32)
    )
    d_normed1 = lax.psum(d_normed1.astype(jnp.bfloat16), "wt").astype(jnp.float32)
    d_source = grad_one + norm_backward(d_normed1, hat_one, inverse_one, norm1_gain)

    def rows_of(array_in):
        return lax.dynamic_slice_in_dim(array_in, row_start, share, 0)

    d_normed1_rows = rows_of(d_normed1)
    d_normed2_rows = rows_of(d_normed2)
    small = (
        jnp.sum(d_normed1_rows * rows_of(hat_one), axis=0),
        jnp.sum(d_normed1_rows, axis=0),
        jnp.sum(rows_of(grad_one), axis=0),
        jnp.sum(d_normed2_rows * rows_of(hat_two), axis=0),
        jnp.sum(d_normed2_rows, axis=0),
        jnp.sum(rows_of(grad_two), axis=0),
    )
    large = (
        d_q_weight,
        d_q_bias,
        d_k_weight,
        d_v_weight,
        d_v_bias,
        d_out_weight,
        d_up_weight,
        d_up_bias,
        d_down,
    )
    return (result, d_source, large, small)


def shards(
    x_in,
    grad_out,
    seg_ids,
    norm1_gain,
    norm1_bias,
    q_weight,
    q_bias,
    k_weight,
    v_weight,
    v_bias,
    out_weight,
    out_bias,
    norm2_gain,
    norm2_bias,
    up_weight,
    up_bias,
    down_weight,
    down_bias,
):
    tok_dev = x_in.shape[1]
    offset = lax.axis_index("ctx") * tok_dev
    runs = x_in.shape[0]
    share = tok_dev // lax.axis_size("wt")
    row_start = lax.axis_index("wt") * share
    params = (
        norm1_gain,
        norm1_bias,
        q_weight,
        q_bias,
        k_weight,
        v_weight,
        v_bias,
        out_weight,
        out_bias,
        norm2_gain,
        norm2_bias,
        up_weight,
        up_bias,
        down_weight,
        down_bias,
    )
    results = []
    source_grads = []
    large_total = None
    small_total = None
    for run_index in range(runs):
        source_rows = lax.dynamic_index_in_dim(x_in, run_index, 0, keepdims=False)
        upstream_rows = lax.dynamic_index_in_dim(grad_out, run_index, 0, keepdims=False)
        seg_row = lax.dynamic_index_in_dim(seg_ids, run_index, 0, keepdims=False)
        result, d_source, large, small = micro_step(
            source_rows, upstream_rows, seg_row, params, offset, row_start, share
        )
        results.append(result)
        source_grads.append(d_source)
        if large_total is None:
            large_total = large
            small_total = small
        else:
            large_total = jax.tree.map(jnp.add, large_total, large)
            small_total = jax.tree.map(jnp.add, small_total, small)
    layer_rows = jnp.stack(results, axis=0)
    grad_rows = jnp.stack(source_grads, axis=0)
    large_total = jax.tree.map(
        lambda part: part.astype(jnp.float32), lax.psum(shortened(large_total), "ctx")
    )
    small_total = lax.psum(small_total, ("ctx", "wt"))
    piece_len = small_total[0].shape[0] // lax.axis_size("wt")
    small_out = [
        lax.dynamic_slice_in_dim(member, lax.axis_index("wt") * piece_len, piece_len)
        for member in small_total
    ]
    return (
        layer_rows,
        grad_rows,
        small_out[0],
        small_out[1],
        large_total[0],
        large_total[1],
        large_total[2],
        large_total[3],
        large_total[4],
        large_total[5],
        small_out[2],
        small_out[3],
        small_out[4],
        large_total[6],
        large_total[7],
        large_total[8],
        small_out[5],
    )


def solution(mesh):
    in_specs = (
        P(None, "ctx", None),
        P(None, "ctx", None),
        P(),
        P(),
        P(),
        P(None, "wt"),
        P("wt"),
        P(None, "wt"),
        P(None, "wt"),
        P("wt"),
        P("wt", None),
        P(),
        P(),
        P(),
        P(None, "wt"),
        P("wt"),
        P("wt", None),
        P(),
    )
    out_specs = (
        P(None, "ctx", None),
        P(None, "ctx", None),
        P("wt"),
        P("wt"),
        P(None, "wt"),
        P("wt"),
        P(None, "wt"),
        P(None, "wt"),
        P("wt"),
        P("wt", None),
        P("wt"),
        P("wt"),
        P("wt"),
        P(None, "wt"),
        P("wt"),
        P("wt", None),
        P("wt"),
    )
    return jax.shard_map(shards, mesh=mesh, in_specs=in_specs, out_specs=out_specs, check_vma=False)
```

profile of v0, /device:TPU:0, one launch (start us, length us, event | category | flops | bytes accessed | tf_op | source)
XLA Modules:
  0.0 7931.5 jit_solution(2078046245471543254)
XLA Ops:
  36.2 80.4 %gather_fusion.2 = s32[8192]{0:T(1024)} fusion(s32[2048]{0:T(1024)S(1)} %bitcast.1685, s32[8192]{0:T(1024)S(1)} %broadcast_clamp_fusion.17), kind=kCustom, calls=%fused_computation.2.clone | custom fusion | bytes 98304 | tf_op jit(solution)/shard_map/jit(_take)/gather | solution.py:93
  197.0 80.4 %gather_fusion.3 = s32[8192]{0:T(1024)} fusion(s32[2048]{0:T(1024)S(1)} %bitcast.1686, s32[8192]{0:T(1024)S(1)} %broadcast_clamp_fusion.16), kind=kCustom, calls=%fused_computation.3.clone | custom fusion | bytes 98304 | tf_op jit(solution)/shard_map/jit(_take)/gather | solution.py:94
  277.4 80.4 %gather_fusion.23 = s32[8192]{0:T(1024)} fusion(s32[2048]{0:T(1024)S(1)} %bitcast.1666, s32[8192]{0:T(1024)S(1)} %broadcast_clamp_fusion.16), kind=kCustom, calls=%fused_computation.22.clone | custom fusion | bytes 98304 | tf_op jit(solution)/shard_map/jit(_take)/gather | solution.py:94
  360.2 80.4 %gather_fusion.42 = s32[8192]{0:T(1024)} fusion(s32[2048]{0:T(1024)S(1)} %bitcast.1645, s32[8192]{0:T(1024)S(1)} %broadcast_clamp_fusion.17), kind=kCustom, calls=%fused_computation.40.clone | custom fusion | bytes 98304 | tf_op jit(solution)/shard_map/jit(_take)/gather | solution.py:93
  523.4 80.4 %gather_fusion.62 = s32[8192]{0:T(1024)} fusion(s32[2048]{0:T(1024)S(1)} %bitcast.1625, s32[8192]{0:T(1024)S(1)} %broadcast_clamp_fusion.17), kind=kCustom, calls=%fused_computation.59.clone | custom fusion | bytes 98304 | tf_op jit(solution)/shard_map/jit(_take)/gather | solution.py:93
  603.8 80.4 %gather_fusion.63 = s32[8192]{0:T(1024)} fusion(s32[2048]{0:T(1024)S(1)} %bitcast.1626, s32[8192]{0:T(1024)S(1)} %broadcast_clamp_fusion.16), kind=kCustom, calls=%fused_computation.60.clone | custom fusion | bytes 98304 | tf_op jit(solution)/shard_map/jit(_take)/gather | solution.py:94
  686.2 80.4 %gather_fusion = s32[8192]{0:T(1024)} fusion(s32[2048]{0:T(1024)S(1)} %bitcast.1687, s32[8192]{0:T(1024)S(1)} %broadcast_clamp_fusion.18), kind=kCustom, calls=%fused_computation.clone | custom fusion | bytes 98304 | tf_op jit(solution)/shard_map/jit(_take)/gather | solution.py:93
  1009.2 80.4 %gather_fusion.4 = s32[8192]{0:T(1024)} fusion(s32[2048]{0:T(1024)S(1)} %bitcast.1688, s32[8192]{0:T(1024)S(1)} %broadcast_clamp_fusion.15), kind=kCustom, calls=%fused_computation.4.clone | custom fusion | bytes 98304 | tf_op jit(solution)/shard_map/jit(_take)/gather | solution.py:93
  1089.6 80.4 %gather_fusion.24 = s32[8192]{0:T(1024)} fusion(s32[2048]{0:T(1024)S(1)} %bitcast.1668, s32[8192]{0:T(1024)S(1)} %broadcast_clamp_fusion.15), kind=kCustom, calls=%fused_computation.23.clone | custom fusion | bytes 98304 | tf_op jit(solution)/shard_map/jit(_take)/gather | solution.py:93
  1170.1 80.4 %gather_fusion.5 = s32[8192]{0:T(1024)} fusion(s32[2048]{0:T(1024)S(1)} %bitcast.1689, s32[8192]{0:T(1024)S(1)} %broadcast_clamp_fusion.14), kind=kCustom, calls=%fused_computation.5.clone | custom fusion | bytes 98304 | tf_op jit(solution)/shard_map/jit(_take)/gather | solution.py:94
  1411.3 80.4 %gather_fusion.45 = s32[8192]{0:T(1024)} fusion(s32[2048]{0:T(1024)S(1)} %bitcast.1649, s32[8192]{0:T(1024)S(1)} %broadcast_clamp_fusion.14), kind=kCustom, calls=%fused_computation.43.clone | custom fusion | bytes 98304 | tf_op jit(solution)/shard_map/jit(_take)/gather | solution.py:94
  1572.0 80.4 %gather_fusion.65 = s32[8192]{0:T(1024)} fusion(s32[2048]{0:T(1024)S(1)} %bitcast.1629, s32[8192]{0:T(1024)S(1)} %broadcast_clamp_fusion.14), kind=kCustom, calls=%fused_computation.62.clone | custom fusion | bytes 98304 | tf_op jit(solution)/shard_map/jit(_take)/gather | solution.py:94
  1654.1 80.4 %gather_fusion.6 = s32[8192]{0:T(1024)} fusion(s32[2048]{0:T(1024)S(1)} %bitcast.1690, s32[8192]{0:T(1024)S(1)} %broadcast_clamp_fusion.13), kind=kCustom, calls=%fused_computation.6.clone | custom fusion | bytes 98304 | tf_op jit(solution)/shard_map/jit(_take)/gather | solution.py:93
  1734.5 80.4 %gather_fusion.26 = s32[8192]{0:T(1024)} fusion(s32[2048]{0:T(1024)S(1)} %bitcast.1670, s32[8192]{0:T(1024)S(1)} %broadcast_clamp_fusion.13), kind=kCustom, calls=%fused_computation.25.clone | custom fusion | bytes 98304 | tf_op jit(solution)/shard_map/jit(_take)/gather | solution.py:93
  1815.0 80.5 %gather_fusion.7 = s32[8192]{0:T(1024)} fusion(s32[2048]{0:T(1024)S(1)} %bitcast.1691, s32[8192]{0:T(1024)S(1)} %broadcast_clamp_fusion.12), kind=kCustom, calls=%fused_computation.7.clone | custom fusion | bytes 98304 | tf_op jit(solution)/shard_map/jit(_take)/gather | solution.py:94
  1895.5 80.4 %gather_fusion.27 = s32[8192]{0:T(1024)} fusion(s32[2048]{0:T(1024)S(1)} %bitcast.1671, s32[8192]{0:T(1024)S(1)} %broadcast_clamp_fusion.12), kind=kCustom, calls=%fused_computation.26.clone | custom fusion | bytes 98304 | tf_op jit(solution)/shard_map/jit(_take)/gather | solution.py:94
  2056.3 80.4 %gather_fusion.47 = s32[8192]{0:T(1024)} fusion(s32[2048]{0:T(1024)S(1)} %bitcast.1651, s32[8192]{0:T(1024)S(1)} %broadcast_clamp_fusion.12), kind=kCustom, calls=%fused_computation.45.clone | custom fusion | bytes 98304 | tf_op jit(solution)/shard_map/jit(_take)/gather | solution.py:94
  2136.7 80.5 %gather_fusion.66 = s32[8192]{0:T(1024)} fusion(s32[2048]{0:T(1024)S(1)} %bitcast.1630, s32[8192]{0:T(1024)S(1)} %broadcast_clamp_fusion.13), kind=kCustom, calls=%fused_computation.63.clone | custom fusion | bytes 98304 | tf_op jit(solution)/shard_map/jit(_take)/gather | solution.py:93
  2217.3 80.5 %gather_fusion.67 = s32[8192]{0:T(1024)} fusion(s32[2048]{0:T(1024)S(1)} %bitcast.1631, s32[8192]{0:T(1024)S(1)} %broadcast_clamp_fusion.12), kind=kCustom, calls=%fused_computation.64.clone | custom fusion | bytes 98304 | tf_op jit(solution)/shard_map/jit(_take)/gather | solution.py:94
  2299.0 80.4 %gather_fusion.8 = s32[8192]{0:T(1024)} fusion(s32[2048]{0:T(1024)S(1)} %bitcast.1692, s32[8192]{0:T(1024)S(1)} %broadcast_clamp_fusion.11), kind=kCustom, calls=%fused_computation.8.clone | custom fusion | bytes 98304 | tf_op jit(solution)/shard_map/jit(_take)/gather | solution.py:93
  2620.4 80.5 %gather_fusion.48 = s32[8192]{0:T(1024)} fusion(s32[2048]{0:T(1024)S(1)} %bitcast.1652, s32[8192]{0:T(1024)S(1)} %broadcast_clamp_fusion.11), kind=kCustom, calls=%fused_computation.46.clone | custom fusion | bytes 98304 | tf_op jit(solution)/shard_map/jit(_take)/gather | solution.py:93
  2700.9 80.5 %gather_fusion.49 = s32[8192]{0:T(1024)} fusion(s32[2048]{0:T(1024)S(1)} %bitcast.1653, s32[8192]{0:T(1024)S(1)} %broadcast_clamp_fusion.10), kind=kCustom, calls=%fused_computation.47.clone | custom fusion | bytes 98304 | tf_op jit(solution)/shard_map/jit(_take)/gather | solution.py:94
  2781.4 80.4 %gather_fusion.68 = s32[8192]{0:T(1024)} fusion(s32[2048]{0:T(1024)S(1)} %bitcast.1632, s32[8192]{0:T(1024)S(1)} %broadcast_clamp_fusion.11), kind=kCustom, calls=%fused_computation.65.clone | custom fusion | bytes 98304 | tf_op jit(solution)/shard_map/jit(_take)/gather | solution.py:93
  2861.8 80.4 %gather_fusion.69 = s32[8192]{0:T(1024)} fusion(s32[2048]{0:T(1024)S(1)} %bitcast.1633, s32[8192]{0:T(1024)S(1)} %broadcast_clamp_fusion.10), kind=kCustom, calls=%fused_computation.66.clone | custom fusion | bytes 98304 | tf_op jit(solution)/shard_map/jit(_take)/gather | solution.py:94
  3033.7 80.4 %gather_fusion.30 = s32[8192]{0:T(1024)} fusion(s32[2048]{0:T(1024)S(1)} %bitcast.1674, s32[8192]{0:T(1024)S(1)} %broadcast_clamp_fusion.9), kind=kCustom, calls=%fused_computation.29.clone | custom fusion | bytes 98304 | tf_op jit(solution)/shard_map/jit(_take)/gather | solution.py:93
  3114.2 80.4 %gather_fusion.11 = s32[8192]{0:T(1024)} fusion(s32[2048]{0:T(1024)S(1)} %bitcast.1695, s32[8192]{0:T(1024)S(1)} %broadcast_clamp_fusion.8), kind=kCustom, calls=%fused_computation.11.clone | custom fusion | bytes 98304 | tf_op jit(solution)/shard_map/jit(_take)/gather | solution.py:94
  3275.0 80.4 %gather_fusion.50 = s32[8192]{0:T(1024)} fusion(s32[2048]{0:T(1024)S(1)} %bitcast.1654, s32[8192]{0:T(1024)S(1)} %broadcast_clamp_fusion.9), kind=kCustom, calls=%fused_computation.48.clone | custom fusion | bytes 98304 | tf_op jit(solution)/shard_map/jit(_take)/gather | solution.py:93
  3355.4 80.4 %gather_fusion.51 = s32[8192]{0:T(1024)} fusion(s32[2048]{0:T(1024)S(1)} %bitcast.1655, s32[8192]{0:T(1024)S(1)} %broadcast_clamp_fusion.8), kind=kCustom, calls=%fused_computation.49.clone | custom fusion | bytes 98304 | tf_op jit(solution)/shard_map/jit(_take)/gather | solution.py:94
  3435.8 80.5 %gather_fusion.70 = s32[8192]{0:T(1024)} fusion(s32[2048]{0:T(1024)S(1)} %bitcast.1634, s32[8192]{0:T(1024)S(1)} %broadcast_clamp_fusion.9), kind=kCustom, calls=%fused_computation.67.clone | custom fusion | bytes 98304 | tf_op jit(solution)/shard_map/jit(_take)/gather | solution.py:93
  3598.5 80.5 %gather_fusion.12 = s32[8192]{0:T(1024)} fusion(s32[2048]{0:T(1024)S(1)} %bitcast.1696, s32[8192]{0:T(1024)S(1)} %broadcast_clamp_fusion.7), kind=kCustom, calls=%fused_computation.12.clone | custom fusion | bytes 98304 | tf_op jit(solution)/shard_map/jit(_take)/gather | solution.py:93
  3679.0 80.4 %gather_fusion.32 = s32[8192]{0:T(1024)} fusion(s32[2048]{0:T(1024)S(1)} %bitcast.1676, s32[8192]{0:T(1024)S(1)} %broadcast_clamp_fusion.7), kind=kCustom, calls=%fused_computation.31.clone | custom fusion | bytes 98304 | tf_op jit(solution)/shard_map/jit(_take)/gather | solution.py:93
  3839.8 80.4 %gather_fusion.33 = s32[8192]{0:T(1024)} fusion(s32[2048]{0:T(1024)S(1)} %bitcast.1677, s32[8192]{0:T(1024)S(1)} %broadcast_clamp_fusion.6), kind=kCustom, calls=%fused_computation.32.clone | custom fusion | bytes 98304 | tf_op jit(solution)/shard_map/jit(_take)/gather | solution.py:94
  3920.3 80.4 %gather_fusion.52 = s32[8192]{0:T(1024)} fusion(s32[2048]{0:T(1024)S(1)} %bitcast.1656, s32[8192]{0:T(1024)S(1)} %broadcast_clamp_fusion.7), kind=kCustom, calls=%fused_computation.50.clone | custom fusion | bytes 98304 | tf_op jit(solution)/shard_map/jit(_take)/gather | solution.py:93
  4081.1 80.4 %gather_fusion.72 = s32[8192]{0:T(1024)} fusion(s32[2048]{0:T(1024)S(1)} %bitcast.1636, s32[8192]{0:T(1024)S(1)} %broadcast_clamp_fusion.7), kind=kCustom, calls=%fused_computation.69.clone | custom fusion | bytes 98304 | tf_op jit(solution)/shard_map/jit(_take)/gather | solution.py:93
  4243.3 80.4 %gather_fusion.14 = s32[8192]{0:T(1024)} fusion(s32[2048]{0:T(1024)S(1)} %bitcast.1698, s32[8192]{0:T(1024)S(1)} %broadcast_clamp_fusion.5), kind=kCustom, calls=%fused_computation.14.clone | custom fusion | bytes 98304 | tf_op jit(solution)/shard_map/jit(_take)/gather | solution.py:93
  4404.3 80.4 %gather_fusion.15 = s32[8192]{0:T(1024)} fusion(s32[2048]{0:T(1024)S(1)} %bitcast.1699, s32[8192]{0:T(1024)S(1)} %broadcast_clamp_fusion.4), kind=kCustom, calls=%fused_computation.15.clone | custom fusion | bytes 98304 | tf_op jit(solution)/shard_map/jit(_take)/gather | solution.py:94
  4484.7 80.4 %gather_fusion.35 = s32[8192]{0:T(1024)} fusion(s32[2048]{0:T(1024)S(1)} %bitcast.1679, s32[8192]{0:T(1024)S(1)} %broadcast_clamp_fusion.4), kind=kCustom, calls=%fused_computation.34.clone | custom fusion | bytes 98304 | tf_op jit(solution)/shard_map/jit(_take)/gather | solution.py:94
  4565.1 80.4 %gather_fusion.54 = s32[8192]{0:T(1024)} fusion(s32[2048]{0:T(1024)S(1)} %bitcast.1658, s32[8192]{0:T(1024)S(1)} %broadcast_clamp_fusion.5), kind=kCustom, calls=%fused_computation.52.clone | custom fusion | bytes 98304 | tf_op jit(solution)/shard_map/jit(_take)/gather | solution.py:93
  4725.9 80.4 %gather_fusion.74 = s32[8192]{0:T(1024)} fusion(s32[2048]{0:T(1024)S(1)} %bitcast.1638, s32[8192]{0:T(1024)S(1)} %broadcast_clamp_fusion.5), kind=kCustom, calls=%fused_computation.71.clone | custom fusion | bytes 98304 | tf_op jit(solution)/shard_map/jit(_take)/gather | solution.py:93
  4806.3 80.5 %gather_fusion.75 = s32[8192]{0:T(1024)} fusion(s32[2048]{0:T(1024)S(1)} %bitcast.1639, s32[8192]{0:T(1024)S(1)} %broadcast_clamp_fusion.4), kind=kCustom, calls=%fused_computation.72.clone | custom fusion | bytes 98304 | tf_op jit(solution)/shard_map/jit(_take)/gather | solution.py:94
  4888.6 80.4 %gather_fusion.16 = s32[8192]{0:T(1024)} fusion(s32[2048]{0:T(1024)S(1)} %bitcast.1700, s32[8192]{0:T(1024)S(1)} %broadcast_clamp_fusion.3), kind=kCustom, calls=%fused_computation.16.clone | custom fusion | bytes 98304 | tf_op jit(solution)/shard_map/jit(_take)/gather | solution.py:93
  5210.4 80.4 %gather_fusion.56 = s32[8192]{0:T(1024)} fusion(s32[2048]{0:T(1024)S(1)} %bitcast.1660, s32[8192]{0:T(1024)S(1)} %broadcast_clamp_fusion.3), kind=kCustom, calls=%fused_computation.54.clone | custom fusion | bytes 98304 | tf_op jit(solution)/shard_map/jit(_take)/gather | solution.py:93
  5371.1 80.8 %gather_fusion.76 = s32[8192]{0:T(1024)} fusion(s32[2048]{0:T(1024)S(1)} %bitcast.1640, s32[8192]{0:T(1024)S(1)} %broadcast_clamp_fusion.3), kind=kCustom, calls=%fused_computation.73.clone | custom fusion | bytes 98304 | tf_op jit(solution)/shard_map/jit(_take)/gather | solution.py:93
  5533.8 80.4 %gather_fusion.18 = s32[8192]{0:T(1024)} fusion(s32[2048]{0:T(1024)S(1)} %bitcast.1702, s32[8192]{0:T(1024)S(1)} %broadcast_clamp_fusion.1), kind=kCustom, calls=%fused_computation.18.clone | custom fusion | bytes 98304 | tf_op jit(solution)/shard_map/jit(_take)/gather | solution.py:93
  5614.2 80.4 %gather_fusion.38 = s32[8192]{0:T(1024)} fusion(s32[2048]{0:T(1024)S(1)} %bitcast.1682, s32[8192]{0:T(1024)S(1)} %broadcast_clamp_fusion.1), kind=kCustom, calls=%fused_computation.37.clone | custom fusion | bytes 98304 | tf_op jit(solution)/shard_map/jit(_take)/gather | solution.py:93
  5855.6 80.4 %gather_fusion.58 = s32[8192]{0:T(1024)} fusion(s32[2048]{0:T(1024)S(1)} %bitcast.1662, s32[8192]{0:T(1024)S(1)} %broadcast_clamp_fusion.1), kind=kCustom, calls=%fused_computation.56.clone | custom fusion | bytes 98304 | tf_op jit(solution)/shard_map/jit(_take)/gather | solution.py:93
  6593.5 86.6 %all-reduce.133.cloned.1.call-done = (f32[256,512]{1,0:T(8,128)}, f32[256,512]{1,0:T(8,128)}, f32[256,512]{1,0:T(8,128)}, f32[256,512]{1,0:T(8,128)}) async-done(((f32[256,512]{1,0:T(8,128)}, f32[256,512]{1,0:T(8,128)}, f32[256,512]{1,0:T(8,128)}, f32[256,512]{1,0:T(8,128)}), (f32[256,512]{1,0:T(8,128)}, f32[256,512]{1,0:T(8,128)}, f32[256,512]{1,0:T(8,128)}, ...) | async-done | bytes 2097168 | tf_op jit(solution)/shard_map/psum | solution.py:191
  7782.3 84.7 %all-reduce.137.cloned.1.call-done = (bf16[256,512]{1,0:T(8,128)(2,1)}, bf16[256,512]{1,0:T(8,128)(2,1)}, bf16[256,512]{1,0:T(8,128)(2,1)}, bf16[256,512]{1,0:T(...) async-done(((bf16[256,512]{1,0:T(8,128)(2,1)}, bf16[256,512]{1,0:T(8,128)(2,1)}, ...) | async-done | bytes 2097168 | tf_op jit(solution)/shard_map/psum | solution.py:199
  (3129 shorter events, 4036.4 us)
Async XLA Ops:
  7.2 6679.1 %copy-start = (bf16[512,512]{1,0:T(8,128)(2,1)S(1)}, bf16[512,512]{1,0:T(8,128)(2,1)}, u32[]{:S(2)}) copy-start(bf16[512,512]{1,0:T(8,128)(2,1)} %param.38) | copy-start | bytes 1572868
  7.2 6673.0 %all-reduce.133.cloned.1.call-start = ((), (), s32[]{:S(2)}) async-start(), calls=%async_computation.9 | async-start | bytes 4194304 | tf_op jit(solution)/shard_map/psum | solution.py:191
  13.7 6453.8 %collective-permute-start.3 = (bf16[64,256]{1,0:T(8,128)(2,1)}, bf16[64,256]{1,0:T(8,128)(2,1)}, u32[]{:S(2)}, u32[]{:S(2)}) collective-permute-start(bf16[64,256]{1,0:T(8,128)(2,1)} %fusion.623), channel_id=1, source_target_pairs={{0,4},{4,8},{8,12},{12,16},{16,20},{20,24},{24,28},{1,5},{5,9},{9,... | collective-permute-start | bytes 98312 | tf_op jit(solution)/shard_map/ppermute | solution.py:20
  17.8 6451.3 %collective-permute-start.2 = (bf16[64,256]{1,0:T(8,128)(2,1)}, bf16[64,256]{1,0:T(8,128)(2,1)}, u32[]{:S(2)}, u32[]{:S(2)}) collective-permute-start(bf16[64,256]{1,0:T(8,128)(2,1)} %fusion.624), channel_id=1, source_target_pairs={{0,4},{4,8},{8,12},{12,16},{16,20},{20,24},{24,28},{1,5},{5,9},{9,... | collective-permute-start | bytes 98312 | tf_op jit(solution)/shard_map/ppermute | solution.py:20
  23.4 6447.1 %collective-permute-start.1 = (bf16[64,256]{1,0:T(8,128)(2,1)}, bf16[64,256]{1,0:T(8,128)(2,1)}, u32[]{:S(2)}, u32[]{:S(2)}) collective-permute-start(bf16[64,256]{1,0:T(8,128)(2,1)} %fusion.625), channel_id=1, source_target_pairs={{0,4},{4,8},{8,12},{12,16},{16,20},{20,24},{24,28},{1,5},{5,9},{9,... | collective-permute-start | bytes 98312 | tf_op jit(solution)/shard_map/ppermute | solution.py:20
  26.4 6450.8 %collective-permute-start = (bf16[64,256]{1,0:T(8,128)(2,1)}, bf16[64,256]{1,0:T(8,128)(2,1)}, u32[]{:S(2)}, u32[]{:S(2)}) collective-permute-start(bf16[64,256]{1,0:T(8,128)(2,1)} %fusion.626), channel_id=1, source_target_pairs={{0,4},{4,8},{8,12},{12,16},{16,20},{20,24},{24,28},{1,5},{5,9},{9,... | collective-permute-start | bytes 98312 | tf_op jit(solution)/shard_map/ppermute | solution.py:20
  30.6 86.0 %copy-start.666 = (s32[256]{0:T(256)}, s32[256]{0:T(256)S(1)}, u32[]{:S(2)}) copy-start(s32[256]{0:T(256)S(1)} %get-tuple-element.565) | copy-start | bytes 3076
  31.3 165.8 %copy-start.29 = (s32[1,2048]{1,0:T(1,128)}, s32[1,2048]{1,0:T(1,128)S(1)}, u32[]{:S(2)}) copy-start(s32[1,2048]{1,0:T(1,128)S(1)} %get-tuple-element.369) | copy-start | bytes 24580
  31.3 246.2 %copy-start.20 = (s32[1,2048]{1,0:T(1,128)}, s32[1,2048]{1,0:T(1,128)S(1)}, u32[]{:S(2)}) copy-start(s32[1,2048]{1,0:T(1,128)S(1)} %get-tuple-element.368) | copy-start | bytes 24580
  31.3 85.3 %copy-start.663 = (s32[1024]{0:T(1024)}, s32[1024]{0:T(1024)S(1)}, u32[]{:S(2)}) copy-start(s32[1024]{0:T(1024)S(1)} %pad_clamp_fusion) | copy-start | bytes 12292
  1572.0 81.7 %copy-start.676 = (s32[256]{0:T(256)S(1)}, s32[256]{0:T(256)}, u32[]{:S(2)}) copy-start(s32[256]{0:T(256)} %get-tuple-element.567) | copy-start | bytes 3076
  2861.8 91.2 %copy-start.668 = (s32[256]{0:T(256)S(1)}, s32[256]{0:T(256)}, u32[]{:S(2)}) copy-start(s32[256]{0:T(256)} %get-tuple-element.587) | copy-start | bytes 3076
  5451.9 81.6 %copy-start.672 = (s32[256]{0:T(256)S(1)}, s32[256]{0:T(256)}, u32[]{:S(2)}) copy-start(s32[256]{0:T(256)} %get-tuple-element.583) | copy-start | bytes 3076
  6096.8 81.7 %copy-start.67 = (bf16[256,256]{1,0:T(8,128)(2,1)S(1)}, bf16[256,256]{1,0:T(8,128)(2,1)}, u32[]{:S(2)}) copy-start(bf16[256,256]{1,0:T(8,128)(2,1)} %copy-done.62) | copy-start | bytes 393220
  6177.7 343.0 %copy-start.85 = (bf16[256,128]{0,1:T(8,128)(2,1)}, bf16[256,128]{0,1:T(8,128)(2,1)S(1)}, u32[]{:S(2)}) copy-start(bf16[256,128]{0,1:T(8,128)(2,1)S(1)} %fusion.63) | copy-start | bytes 196612
  6192.3 369.2 %copy-start.89 = (bf16[256,128]{0,1:T(8,128)(2,1)}, bf16[256,128]{0,1:T(8,128)(2,1)S(1)}, u32[]{:S(2)}) copy-start(bf16[256,128]{0,1:T(8,128)(2,1)S(1)} %fusion.61) | copy-start | bytes 196612
  6206.2 377.0 %copy-start.87 = (bf16[256,128]{0,1:T(8,128)(2,1)}, bf16[256,128]{0,1:T(8,128)(2,1)S(1)}, u32[]{:S(2)}) copy-start(bf16[256,128]{0,1:T(8,128)(2,1)S(1)} %fusion.59) | copy-start | bytes 196612
  6376.1 81.9 %copy-start.526 = (pred[256,32]{1,0:T(8,128)(4,1)S(1)}, pred[256,32]{1,0:T(8,128)(4,1)}, u32[]{:S(2)}) copy-start(pred[256,32]{1,0:T(8,128)(4,1)} %get-tuple-element.469) | copy-start | bytes 24580
  6376.9 82.5 %copy-start.527 = (pred[256,32]{1,0:T(8,128)(4,1)S(1)}, pred[256,32]{1,0:T(8,128)(4,1)}, u32[]{:S(2)}) copy-start(pred[256,32]{1,0:T(8,128)(4,1)} %get-tuple-element.465) | copy-start | bytes 24580
  6376.9 85.9 %copy-start.580 = (bf16[2,32,128]{2,1,0:T(8,128)(2,1)S(1)}, bf16[2,32,128]{2,1,0:T(8,128)(2,1)}, u32[]{:S(2)}) copy-start(bf16[2,32,128]{2,1,0:T(8,128)(2,1)} %get-tuple-element.379) | copy-start | bytes 49156
  6377.7 85.8 %copy-start.617 = (bf16[1,32,128]{2,1,0:T(8,128)(2,1)S(1)}, bf16[1,32,128]{2,1,0:T(8,128)(2,1)}, u32[]{:S(2)}) copy-start(bf16[1,32,128]{2,1,0:T(8,128)(2,1)} %get-tuple-element.425) | copy-start | bytes 24580
  6377.7 86.5 %copy-start.618 = (bf16[1,32,128]{2,1,0:T(8,128)(2,1)S(1)}, bf16[1,32,128]{2,1,0:T(8,128)(2,1)}, u32[]{:S(2)}) copy-start(bf16[1,32,128]{2,1,0:T(8,128)(2,1)} %get-tuple-element.427) | copy-start | bytes 24580
  6377.7 87.2 %copy-start.619 = (bf16[1,32,128]{2,1,0:T(8,128)(2,1)S(1)}, bf16[1,32,128]{2,1,0:T(8,128)(2,1)}, u32[]{:S(2)}) copy-start(bf16[1,32,128]{2,1,0:T(8,128)(2,1)} %get-tuple-element.429) | copy-start | bytes 24580
  6378.3 87.2 %copy-start.620 = (bf16[1,32,128]{2,1,0:T(8,128)(2,1)S(1)}, bf16[1,32,128]{2,1,0:T(8,128)(2,1)}, u32[]{:S(2)}) copy-start(bf16[1,32,128]{2,1,0:T(8,128)(2,1)} %get-tuple-element.431) | copy-start | bytes 24580
  6378.3 87.9 %copy-start.621 = (bf16[1,32,128]{2,1,0:T(8,128)(2,1)S(1)}, bf16[1,32,128]{2,1,0:T(8,128)(2,1)}, u32[]{:S(2)}) copy-start(bf16[1,32,128]{2,1,0:T(8,128)(2,1)} %get-tuple-element.433) | copy-start | bytes 24580
  6378.3 89.2 %copy-start.139 = (bf16[256,128]{1,0:T(8,128)(2,1)S(1)}, bf16[256,128]{1,0:T(8,128)(2,1)}, u32[]{:S(2)}) copy-start(bf16[256,128]{1,0:T(8,128)(2,1)} %copy-done.136) | copy-start | bytes 196612
  6378.3 89.2 %copy-start.149 = (bf16[256,128]{1,0:T(8,128)(2,1)S(1)}, bf16[256,128]{1,0:T(8,128)(2,1)}, u32[]{:S(2)}) copy-start(bf16[256,128]{1,0:T(8,128)(2,1)} %copy-done.146) | copy-start | bytes 196612
  6396.8 102.2 %copy-start.462 = (bf16[2,32,2,64]{3,2,1,0:T(2,128)(2,1)}, bf16[2,32,2,64]{3,2,1,0:T(2,128)(2,1)S(1)}, u32[]{:S(2)}) copy-start(bf16[2,32,2,64]{3,2,1,0:T(2,128)(2,1)S(1)} %reshape.4113) | copy-start | bytes 49156
  6397.6 102.7 %copy-start.496 = (bf16[32,2,64]{2,1,0:T(2,128)(2,1)}, bf16[32,2,64]{2,1,0:T(2,128)(2,1)S(1)}, u32[]{:S(2)}) copy-start(bf16[32,2,64]{2,1,0:T(2,128)(2,1)S(1)} %reshape.4116) | copy-start | bytes 24580
  6589.6 90.6 %copy-start.39 = (bf16[4,256,512]{2,1,0:T(8,128)(2,1)S(1)}, bf16[4,256,512]{2,1,0:T(8,128)(2,1)}, u32[]{:S(2)}) copy-start(bf16[4,256,512]{2,1,0:T(8,128)(2,1)} %param.22) | copy-start | bytes 3145732
  6589.6 90.6 %copy-start.631 = (f32[512]{0:T(512)S(1)}, f32[512]{0:T(512)}, u32[]{:S(2)}) copy-start(f32[512]{0:T(512)} %param.33) | copy-start | bytes 6148
  6590.7 91.6 %copy-start.313 = (bf16[256,128]{1,0:T(8,128)(2,1)}, bf16[256,128]{1,0:T(8,128)(2,1)S(1)}, u32[]{:S(2)}) copy-start(bf16[256,128]{1,0:T(8,128)(2,1)S(1)} %add_convert_fusion.11) | copy-start | bytes 196612
  6591.7 193.9 %all-reduce.131.cloned.1.call-start = ((), (), s32[]{:S(2)}) async-start(), calls=%async_computation.8 | async-start | bytes 4194304 | tf_op jit(solution)/shard_map/psum | solution.py:211
  6698.5 915.8 %reduce-scatter.5.cloned.1.call-start = ((), (), s32[]{:S(2)}) async-start(), calls=%async_computation.4 | async-start | bytes 147456 | tf_op jit(solution)/shard_map/reduce_scatter | solution.py:278
  7220.1 411.1 %collective-permute-start.5 = (bf16[64,256]{1,0:T(8,128)(2,1)}, bf16[64,256]{1,0:T(8,128)(2,1)}, u32[]{:S(2)}, u32[]{:S(2)}) collective-permute-start(bf16[64,256]{1,0:T(8,128)(2,1)} %slice.2934), channel_id=1, source_target_pairs={{4,0},{8,4},{12,8},{16,12},{20,16},{24,20},{28,24},{5,1},{9,5},{13... | collective-permute-start | bytes 98312 | tf_op jit(solution)/shard_map/ppermute | solution.py:20
  7271.0 359.5 %reduce-scatter.7.cloned.1.call-start = ((), (), s32[]{:S(2)}) async-start(), calls=%async_computation.5 | async-start | bytes 147456 | tf_op jit(solution)/shard_map/reduce_scatter | solution.py:278
  7305.1 310.0 %collective-permute-start.4 = (bf16[64,256]{1,0:T(8,128)(2,1)}, bf16[64,256]{1,0:T(8,128)(2,1)}, u32[]{:S(2)}, u32[]{:S(2)}) collective-permute-start(bf16[64,256]{1,0:T(8,128)(2,1)} %slice.2935), channel_id=1, source_target_pairs={{4,0},{8,4},{12,8},{16,12},{20,16},{24,20},{28,24},{5,1},{9,5},{13... | collective-permute-start | bytes 98312 | tf_op jit(solution)/shard_map/ppermute | solution.py:20
  7398.8 268.7 %collective-permute-start.6 = (bf16[64,256]{1,0:T(8,128)(2,1)}, bf16[64,256]{1,0:T(8,128)(2,1)}, u32[]{:S(2)}, u32[]{:S(2)}) collective-permute-start(bf16[64,256]{1,0:T(8,128)(2,1)} %slice.2933), channel_id=1, source_target_pairs={{4,0},{8,4},{12,8},{16,12},{20,16},{24,20},{28,24},{5,1},{9,5},{13... | collective-permute-start | bytes 98312 | tf_op jit(solution)/shard_map/ppermute | solution.py:20
  7476.9 227.0 %collective-permute-start.7 = (bf16[64,256]{1,0:T(8,128)(2,1)}, bf16[64,256]{1,0:T(8,128)(2,1)}, u32[]{:S(2)}, u32[]{:S(2)}) collective-permute-start(bf16[64,256]{1,0:T(8,128)(2,1)} %slice.2932), channel_id=1, source_target_pairs={{4,0},{8,4},{12,8},{16,12},{20,16},{24,20},{28,24},{5,1},{9,5},{13... | collective-permute-start | bytes 98312 | tf_op jit(solution)/shard_map/ppermute | solution.py:20
  7593.0 73.6 reduce-scatter.9.cloned.1.call-start
  7598.8 104.4 %reduce-scatter.11.cloned.1.call-start = ((), (), s32[]{:S(2)}) async-start(), calls=%async_computation.7 | async-start | bytes 147456 | tf_op jit(solution)/shard_map/reduce_scatter | solution.py:278
  7603.5 171.5 %all-reduce.135.cloned.1.call-start = ((), (), s32[]{:S(2)}) async-start(), calls=%async_computation.10 | async-start | bytes 3145728 | tf_op jit(solution)/shard_map/psum | solution.py:400
  7714.3 152.7 %all-reduce.137.cloned.1.call-start = ((), (), s32[]{:S(2)}) async-start(), calls=%async_computation.11 | async-start | bytes 4194304 | tf_op jit(solution)/shard_map/psum | solution.py:199
  7780.1 90.2 %copy-start.640 = (f32[256]{0:T(256)S(1)}, f32[256]{0:T(256)}, u32[]{:S(2)}) copy-start(f32[256]{0:T(256)} %copy-done.639) | copy-start | bytes 3076
  7780.1 90.2 %copy-start.650 = (f32[256]{0:T(256)S(1)}, f32[256]{0:T(256)}, u32[]{:S(2)}) copy-start(f32[256]{0:T(256)} %copy-done.649) | copy-start | bytes 3076
  7780.1 90.2 %copy-start.652 = (f32[256]{0:T(256)S(1)}, f32[256]{0:T(256)}, u32[]{:S(2)}) copy-start(f32[256]{0:T(256)} %copy-done.651) | copy-start | bytes 3076
  7780.1 90.2 %copy-start.654 = (f32[256]{0:T(256)S(1)}, f32[256]{0:T(256)}, u32[]{:S(2)}) copy-start(f32[256]{0:T(256)} %copy-done.653) | copy-start | bytes 3076
  7780.1 90.2 %copy-start.656 = (f32[256]{0:T(256)S(1)}, f32[256]{0:T(256)}, u32[]{:S(2)}) copy-start(f32[256]{0:T(256)} %copy-done.655) | copy-start | bytes 3076
  (672 other events, 11982.7 us)
Sparse Core Ops, SparseCore 0:
  6591.8 88.3 all-reduce.132
  6698.7 86.9 all-reduce.130
  7271.1 33.6 reduce-scatter.4
  7593.2 37.2 reduce-scatter.6
  7633.3 33.3 reduce-scatter.8
  7669.8 33.3 reduce-scatter.10
  7714.4 60.5 all-reduce.134
  7778.2 88.7 all-reduce.136
where the time goes:
time: 7960 us; the launch traced here: 7930 us
  local copies, waits for them, and re-layouts  6920 us (87%)
  waiting for transfers between devices  343 us (4%)
  matrix products  327 us (4%)
  other arithmetic  216 us (3%)
  blocking collectives  86.6 us (1%)
    gather x80, local copies, waits for them, and re-layouts, level_mask(): firsts = jnp.take(seg_row, jnp.clip(begin, 0, last_index))  3250 us
    gather x72, local copies, waits for them, and re-layouts, level_mask(): lasts = jnp.take(seg_row, jnp.clip(begin + cell_size - 1, 0, last_index))  2920 us
  transfers between devices with their start and end apart: 16, of which 7 were waited for; matrix products, arithmetic and copies ran while one was open for 86% of the time, Pallas kernels for 0%

commit v1 on v0

v1 whole, which is shorter than its diff:
```python
import functools

import jax
import jax.numpy as jnp
from jax import lax
from jax.experimental import pallas as pl
from jax.experimental.pallas import tpu as pltpu
from jax.sharding import PartitionSpec as P

HEAD_DIM = 64
BLOCK = 16
LEVELS = 10
FINE = 3
EPSILON = 1e-05
NEGATIVE = -1e30
LOG_TWO = 0.6931471805599453
LANES = 128
BF16 = jnp.bfloat16
F32 = jnp.float32


def dot(left, right, dims):
    return lax.dot_general(left, right, (dims, ((), ())), preferred_element_type=F32)


def dot_nn(left, right):
    return dot(left, right, ((1,), (0,)))


def dot_nt(left, right):
    return dot(left, right, ((1,), (1,)))


def dot_tn(left, right):
    return dot(left, right, ((0,), (0,)))


def norm_parts(source):
    centre = jnp.mean(source, axis=-1, keepdims=True)
    centred = source - centre
    variance = jnp.mean(centred * centred, axis=-1, keepdims=True)
    inverse = lax.rsqrt(variance + EPSILON)
    return centred * inverse, inverse


def norm_backward(upstream, normed, inverse, gain):
    scaled = upstream * gain
    first_mean = jnp.mean(scaled, axis=-1, keepdims=True)
    second_mean = jnp.mean(scaled * normed, axis=-1, keepdims=True)
    return inverse * (scaled - first_mean - normed * second_mean)


def iota(shape, axis):
    return lax.broadcasted_iota(jnp.int32, shape, axis)


class Geometry:
    def __init__(self, ctx, wt, tok_dev):
        self.ctx, self.wt, self.tok_dev = ctx, wt, tok_dev
        tokens = ctx * tok_dev
        self.levels = len([l for l in range(LEVELS) if BLOCK * 2**l < tokens])
        self.own_cells = [tok_dev // 2**l if l <= FINE else 0 for l in range(self.levels)]
        self.tile = tok_dev // 2
        self.tile_slots = [BLOCK + self.tile] + [BLOCK * 4 >> (l - 1) if l < FINE else BLOCK for l in range(1, self.levels)]
        self.slots = sum(self.tile_slots)
        self.slot_at = [sum(self.tile_slots[:l]) for l in range(self.levels + 1)]
        self.far = self.levels - (FINE + 2)
        self.near = FINE + 2


def pool_matrix():
    parts = []
    for level, count in ((1, 128), (2, 64), (3, 32)):
        hit = (iota((count, 256), 1) >> level) == iota((count, 256), 0)
        parts.append(jnp.where(hit, 1.0 / 2**level, 0.0))
    return jnp.concatenate(parts, axis=0).astype(BF16)


def coarse_matrix():
    row, column = iota((32, 32), 0), iota((32, 32), 1)
    out = jnp.zeros((32, 32), F32)
    first = 0
    for level, count in ((4, 16), (5, 8), (6, 4), (7, 2), (8, 1)):
        up = level - FINE
        hit = (row >= first) & (row < first + count) & ((column >> up) == row - first)
        out = jnp.where(hit, 1.0 / 2**up, out)
        first += count
    return out.astype(BF16)


def far_matrix(geo, me):
    parts = []
    first = 0
    for step in range(geo.far):
        up = step + 1
        each = BLOCK >> up
        row, column = iota((BLOCK, geo.ctx * BLOCK), 0), iota((BLOCK, geo.ctx * BLOCK), 1)
        group = (me >> up) - 1
        device = (group << up) + (row >> (4 - up))
        wanted = device * BLOCK + first + (row & (each - 1))
        parts.append(jnp.where((column == wanted) & (group >= 0), 1.0, 0.0))
        first += each
    return jnp.concatenate(parts, axis=0).astype(BF16)


def mask_bias(geo, me, segs, tile):
    first_pos = me * geo.tok_dev + tile * geo.tile
    seg_one = jnp.sum((segs < 1).astype(jnp.int32), axis=1, keepdims=True)
    seg_two = jnp.sum((segs < 2).astype(jnp.int32), axis=1, keepdims=True)
    position = first_pos + iota((1, geo.tile), 1)
    begins = jnp.where(position >= seg_two, seg_two, jnp.where(position >= seg_one, seg_one, 0))
    parts = []
    for level in range(geo.levels):
        size, shift = 2**level, level + 4
        count = geo.tile_slots[level]
        span = BLOCK * size
        if level <= FINE:
            base = first_pos - span
        else:
            base = (((me * geo.tok_dev) >> shift) - 1) << shift
        begin = base + size * iota((count, geo.tile), 0)
        lower = jnp.maximum(((position >> shift) - 1) << shift, begins)
        if level == 0:
            upper = position + 1
        else:
            upper = ((position >> (shift - 1)) - 1) << (shift - 1)
        valid = (begin >= lower) & (begin + size <= upper)
        parts.append(jnp.where(valid, level * LOG_TWO, NEGATIVE))
    return jnp.concatenate(parts, axis=0)


def both_heads(pair):
    lane = iota(pair.shape, 1)
    zero = jnp.zeros_like(pair)
    return jnp.concatenate([jnp.where(lane < HEAD_DIM, pair, zero), jnp.where(lane >= HEAD_DIM, pair, zero)], axis=0)


def own_lanes(stacked):
    rows = stacked.shape[0] // 2
    lane = iota((rows, stacked.shape[1]), 1)
    return jnp.where(lane < HEAD_DIM, stacked[:rows], stacked[rows:])


def project(geo, x, gain, shift, wa, extra, n1, q, own, cells, near, far):
    normed, _ = norm_parts(x[...].astype(F32))
    n1[...] = (normed * gain[...] + shift[...]).astype(BF16)
    pool, coarse = pool_matrix(), coarse_matrix()

    def shard(w, carry):
        out = dot_nn(n1[...], wa[w, :, : 3 * LANES])
        bias = extra[w, 1:2, :]
        q[w] = ((out[:, :LANES] + bias[:, :LANES]).astype(BF16) * 0.125).astype(BF16)
        kv = jnp.concatenate(
            [out[:, LANES : 2 * LANES], out[:, 2 * LANES :] + bias[:, LANES : 2 * LANES]], axis=1
        ).astype(BF16)
        own[w] = kv
        fine = dot_nn(pool, kv).astype(BF16)
        cells[w] = fine
        rough = dot_nn(coarse, fine[192:224]).astype(BF16)
        near[w, 0:16] = kv[240:256]
        near[w, 16:32] = fine[112:128]
        near[w, 32:48] = fine[176:192]
        near[w, 48:64] = fine[208:224]
        near[w, 64:80] = rough[0:16]
        far[w] = rough[16:32]
        return carry

    lax.fori_loop(0, geo.wt, shard, 0)


def tables(geo, me, own, cells, near_in, far_in, table):
    pick = far_matrix(geo, me)

    def shard(w, carry):
        rough = dot_nn(pick, far_in[w]).astype(BF16)
        at = geo.slot_at
        table[w, 0, 0:16] = near_in[w, 0:16]
        table[w, 0, 16:144] = own[w, 0:128]
        table[w, 1, 0:144] = own[w, 112:256]
        table[w, 0, at[1] : at[1] + 16] = near_in[w, 16:32]
        table[w, 0, at[1] + 16 : at[2]] = cells[w, 0:48]
        table[w, 1, at[1] : at[2]] = cells[w, 48:112]
        table[w, 0, at[2] : at[2] + 16] = near_in[w, 32:48]
        table[w, 0, at[2] + 16 : at[3]] = cells[w, 128:144]
        table[w, 1, at[2] : at[3]] = cells[w, 144:176]
        table[w, 0, at[3] : at[4]] = near_in[w, 48:64]
        table[w, 1, at[3] : at[4]] = cells[w, 192:208]
        for tile in (0, 1):
            table[w, tile, at[4] : at[5]] = near_in[w, 64:80]
            table[w, tile, at[5] :] = rough
        return carry

    lax.fori_loop(0, geo.wt, shard, 0)


def attend(geo, q, table, bias, probs, mixed):
    def shard(w, carry):
        for tile in (0, 1):
            rows = slice(tile * geo.tile, (tile + 1) * geo.tile)
            both = both_heads(q[w, rows, :])
            level_bias = bias[tile]
            scores = dot_nt(table[w, tile, :, :LANES], both)
            scores = scores + jnp.concatenate([level_bias, level_bias], axis=1)
            top = jnp.max(scores, axis=0, keepdims=True)
            exponent = jnp.exp(scores - top)
            total = jnp.sum(exponent, axis=0, keepdims=True)
            low = (exponent * (1.0 / total)).astype(BF16)
            probs[w, tile] = low
            mixed[w, rows, :] = own_lanes(dot_tn(low, table[w, tile, :, LANES:])).astype(BF16)
        return carry

    lax.fori_loop(0, geo.wt, shard, 0)


def attend_back(geo, q, table, probs, d_mixed, d_queries, d_table):
    def shard(w, carry):
        for tile in (0, 1):
            rows = slice(tile * geo.tile, (tile + 1) * geo.tile)
            both = both_heads(q[w, rows, :])
            d_both = both_heads(d_mixed[w, rows, :])
            low = probs[w, tile]
            d_probs = dot_nt(table[w, tile, :, LANES:], d_both)
            wide = low.astype(F32)
            product = wide * d_probs
            centre = jnp.sum(product, axis=0, keepdims=True)
            d_scores = (product - wide * centre).astype(BF16)
            d_table[w, tile, :, :LANES] = dot_nn(d_scores, both)
            d_table[w, tile, :, LANES:] = dot_nn(low, d_both)
            back = own_lanes(dot_tn(d_scores, table[w, tile, :, :LANES]))
            d_queries[w, rows, :] = (back * 0.125).astype(BF16)
        return carry

    lax.fori_loop(0, geo.wt, shard, 0)


def return_cells(geo, me, d_table, near, far):
    pick = far_matrix(geo, me)
    at = geo.slot_at

    def shard(w, carry):
        near[w, 0:16] = d_table[w, 0, 0:16].astype(BF16)
        near[w, 16:32] = d_table[w, 0, at[1] : at[1] + 16].astype(BF16)
        near[w, 32:48] = d_table[w, 0, at[2] : at[2] + 16].astype(BF16)
        near[w, 48:64] = d_table[w, 0, at[3] : at[4]].astype(BF16)
        near[w, 64:80] = (d_table[w, 0, at[4] : at[5]] + d_table[w, 1, at[4] : at[5]]).astype(BF16)
        rough = (d_table[w, 0, at[5] :] + d_table[w, 1, at[5] :]).astype(BF16)
        far[w] = dot_tn(pick, rough).astype(BF16)
        return carry

    lax.fori_loop(0, geo.wt, shard, 0)


def own_gradients(geo, w, d_table, near_back, far_back):
    at = geo.slot_at
    first, second = d_table.at[w, 0], d_table.at[w, 1]
    back = near_back[w].astype(F32)
    tokens = jnp.concatenate(
        [first[16:128], first[128:144] + second[0:16], second[16:128], second[128:144] + back[0:16]], axis=0
    )
    rough = jnp.concatenate([back[64:80], far_back], axis=0)
    fine = dot_tn(coarse_matrix(), rough.astype(BF16))
    level3 = jnp.concatenate([second[at[3] : at[4]], back[48:64]], axis=0) + fine
    cells = jnp.concatenate(
        [
            first[at[1] + 16 : at[2]],
            second[at[1] : at[2]],
            back[16:32],
            first[at[2] + 16 : at[3]],
            second[at[2] : at[3]],
            back[32:48],
            level3,
        ],
        axis=0,
    )
    return tokens + dot_tn(pool_matrix(), cells.astype(BF16))


def forward_rest(geo, x, out_shift, gain, shift, wa, extra, up, down, down_shift, mixed, middle, n2, hidden, slope, result):
    middle[...] = x[...].astype(F32) + out_shift[...]

    def shard(w, carry):
        middle[...] += dot_nt(mixed[w], wa[w, :, 3 * LANES :])
        return carry

    lax.fori_loop(0, geo.wt, shard, 0)
    normed, _ = norm_parts(middle[...])
    n2[...] = (normed * gain[...] + shift[...]).astype(BF16)
    result[...] = middle[...] + down_shift[...]

    def ff(w, carry):
        pre = dot_nn(n2[...], up[w]) + extra[w, 0:1, :]
        gate = jax.nn.sigmoid(pre)
        hidden[w] = (pre * gate).astype(BF16)
        slope[w] = gate * (1.0 + pre * (1.0 - gate))
        result[...] += dot_nn(hidden[w], down[w])
        return carry

    lax.fori_loop(0, geo.wt, ff, 0)


def feed_back(geo, g2, gain, wa, up, down, middle, n2, hidden, slope, mixed, g1, d_mixed, sums, grads, total):
    total[...] = jnp.zeros_like(total)

    def ff(w, carry):
        d_hidden = dot_nt(g2[...], down[w]).astype(BF16).astype(F32)
        d_up = (d_hidden * slope[w]).astype(BF16)
        sums[w, 0:1, :] = jnp.sum(d_up.astype(F32), axis=0, keepdims=True)
        grads[2, w] = dot_tn(hidden[w], g2[...]).astype(BF16)
        grads[1, w] = dot_tn(n2[...], d_up).astype(BF16)
        total[...] += dot_nt(d_up, up[w])
        return carry

    lax.fori_loop(0, geo.wt, ff, 0)
    normed, inverse = norm_parts(middle[...])
    d_normed = total[...]
    wide = g2[...].astype(F32)
    first = wide + norm_backward(d_normed, normed, inverse, gain[...])
    g1[...] = first
    low = first.astype(BF16)

    def add(column, row):
        for w in range(geo.wt):
            sums[w, 2 + column // 4 : 3 + column // 4, (column % 4) * LANES : (column % 4 + 1) * LANES] = row[
                :, w * LANES : (w + 1) * LANES
            ]

    add(2, jnp.sum(first, axis=0, keepdims=True))
    add(3, jnp.sum(d_normed * normed, axis=0, keepdims=True))
    add(4, jnp.sum(d_normed, axis=0, keepdims=True))
    add(5, jnp.sum(wide, axis=0, keepdims=True))

    def out(w, carry):
        d_mixed[w] = dot_nn(low, wa[w, :, 3 * LANES :]).astype(BF16)
        grads[0, w, :, 3 * LANES :] = dot_tn(low, mixed[w]).astype(BF16)
        return carry

    lax.fori_loop(0, geo.wt, out, 0)


def project_back(geo, x, gain, wa, n1, g1, d_queries, d_table, near_back, far_back, sums, grads, total, d_source):
    total[...] = jnp.zeros_like(total)

    def shard(w, carry):
        far = far_back[w, 0].astype(F32)
        for step in range(1, far_back.shape[1]):
            far = far + far_back[w, step].astype(F32)
        kv = own_gradients(geo, w, d_table, near_back, far).astype(BF16)
        d_qkv = jnp.concatenate([d_queries[w], kv], axis=1)
        sums[w, 1:2, :LANES] = jnp.sum(d_qkv[:, :LANES].astype(F32), axis=0, keepdims=True)
        sums[w, 1:2, LANES : 2 * LANES] = jnp.sum(d_qkv[:, 2 * LANES :].astype(F32), axis=0, keepdims=True)
        grads[w, :, : 3 * LANES] = dot_tn(n1[...], d_qkv).astype(BF16)
        total[...] += dot_nt(d_qkv, wa[w, :, : 3 * LANES])
        return carry

    lax.fori_loop(0, geo.wt, shard, 0)
    normed, inverse = norm_parts(x[...].astype(F32))
    d_normed = total[...]
    d_source[...] = (g1[...] + norm_backward(d_normed, normed, inverse, gain[...])).astype(d_source.dtype)
    rows = (jnp.sum(d_normed * normed, axis=0, keepdims=True), jnp.sum(d_normed, axis=0, keepdims=True))
    for w in range(geo.wt):
        for column, row in enumerate(rows):
            sums[w, 2:3, column * LANES : (column + 1) * LANES] = row[:, w * LANES : (w + 1) * LANES]


def shards(
    x_in,
    grad_out,
    seg_ids,
    norm1_gain,
    norm1_bias,
    q_weight,
    q_bias,
    k_weight,
    v_weight,
    v_bias,
    out_weight,
    out_bias,
    norm2_gain,
    norm2_bias,
    up_weight,
    up_bias,
    down_weight,
    down_bias,
):
    ctx, wt = lax.axis_size("ctx"), lax.axis_size("wt")
    runs, tok_dev, width = x_in.shape
    geo = Geometry(ctx, wt, tok_dev)
    z = lax.axis_index("wt")
    me_out = lax.axis_index("ctx")
    x = lax.dynamic_index_in_dim(x_in, z, 0, keepdims=False)
    g2 = lax.dynamic_index_in_dim(grad_out, z, 0, keepdims=False)
    segs = lax.dynamic_index_in_dim(seg_ids, z, 0, keepdims=True)
    row = lambda v: v.reshape(1, -1)
    wa_own = jnp.concatenate([q_weight, k_weight, v_weight, out_weight.T], axis=1)
    extra_own = jnp.zeros((8, up_bias.shape[0]), F32)
    extra_own = extra_own.at[0].set(up_bias).at[1, :128].set(q_bias).at[1, 128:256].set(v_bias)
    wa, up, down, extra = (lax.all_gather(t, "wt") for t in (wa_own, up_weight, down_weight, extra_own))
    sds = jax.ShapeDtypeStruct
    params = pltpu.CompilerParams(vmem_limit_bytes=60 * 2**20)
    T = tok_dev

    def call(body, outs, *args):
        return pl.pallas_call(body, out_shape=outs, compiler_params=params)(*args)

    n1, q, own, cells, near, far = call(
        functools.partial(project, geo),
        [
            sds((T, width), BF16),
            sds((wt, T, LANES), BF16),
            sds((wt, T, 256), BF16),
            sds((wt, 224, 256), BF16),
            sds((wt, 80, 256), BF16),
            sds((wt, 16, 256), BF16),
        ],
        x, row(norm1_gain), row(norm1_bias), wa, extra,
    )
    near_in = lax.ppermute(near, "ctx", [(i, i + 1) for i in range(ctx - 1)])
    far_in = lax.all_gather(far, "ctx", axis=1).reshape(wt, ctx * 16, 256)

    def middle_body(x, g2, segs, out_b, n2g, n2b, wa, extra, up, down, down_b, q, own, cells, near_in, far_in,
                    result, g1, d_queries, d_table, near_out, far_out, sums, grads,
                    table, bias, probs, mixed, mid, n2, hidden, slope, d_mixed, total):
        me = lax.axis_index("ctx")
        bias[0] = mask_bias(geo, me, segs[...], 0)
        bias[1] = mask_bias(geo, me, segs[...], 1)
        tables(geo, me, own, cells, near_in, far_in, table)
        attend(geo, q, table, bias, probs, mixed)
        forward_rest(geo, x, out_b, n2g, n2b, wa, extra, up, down, down_b, mixed, mid, n2, hidden, slope, result)
        sums[...] = jnp.zeros_like(sums)
        feed_back(geo, g2, n2g, wa, up, down, mid, n2, hidden, slope, mixed, g1, d_mixed, sums, grads, total)
        attend_back(geo, q, table, probs, d_mixed, d_queries, d_table)
        return_cells(geo, me, d_table, near_out, far_out)

    S = geo.slots
    result, g1, d_queries, d_table, near_out, far_out, sums, grads = pl.pallas_call(
        middle_body,
        out_shape=[
            sds((T, width), F32),
            sds((T, width), F32),
            sds((wt, T, LANES), BF16),
            sds((wt, 2, S, 256), F32),
            sds((wt, 80, 256), BF16),
            sds((wt, ctx * 16, 256), BF16),
            sds((wt, 8, 512), F32),
            sds((3, wt, 512, 512), BF16),
        ],
        scratch_shapes=[
            pltpu.VMEM((wt, 2, S, 256), BF16),
            pltpu.VMEM((2, S, T // 2), F32),
            pltpu.VMEM((wt, 2, S, 256), BF16),
            pltpu.VMEM((wt, T, LANES), BF16),
            pltpu.VMEM((T, width), F32),
            pltpu.VMEM((T, width), BF16),
            pltpu.VMEM((wt, T, 512), BF16),
            pltpu.VMEM((wt, T, 512), F32),
            pltpu.VMEM((wt, T, LANES), BF16),
            pltpu.VMEM((T, width), F32),
        ],
        compiler_params=params,
    )(x, g2, segs, row(out_bias), row(norm2_gain), row(norm2_bias), wa, extra, up, down, row(down_bias), q, own, cells, near_in, far_in)
    near_back = lax.ppermute(near_out, "ctx", [(i + 1, i) for i in range(ctx - 1)])
    far_back = lax.psum_scatter(far_out, "ctx", scatter_dimension=1, tiled=True).reshape(wt, 1, 16, 256)

    def last_body(x, n1g, wa, n1, g1, d_queries, d_table, near_back, far_back, sums_in, grads_in, d_source, sums, grads, total):
        sums[...] = sums_in[...]
        grads[...] = grads_in[...]
        project_back(geo, x, n1g, wa, n1, g1, d_queries, d_table, near_back, far_back, sums, grads, total, d_source)

    d_source, sums, grads0 = pl.pallas_call(
        last_body,
        out_shape=[sds((T, width), F32), sds((wt, 8, 512), F32), sds((wt, 512, 512), BF16)],
        scratch_shapes=[pltpu.VMEM((T, width), F32)],
        compiler_params=params,
    )(x, row(norm1_gain), wa, n1, g1, d_queries, d_table, near_back, far_back, sums, grads[0])
    layer_rows = lax.all_gather(result.astype(BF16), "wt").astype(F32)
    grad_rows = lax.all_gather(d_source.astype(BF16), "wt").astype(F32)
    grads = jnp.stack([grads0, grads[1], grads[2]])
    mine = lax.psum(lax.psum_scatter(grads, "wt", scatter_dimension=1, tiled=True), "ctx").astype(F32)[:, 0]
    small = lax.psum(lax.psum_scatter(sums, "wt", scatter_dimension=0, tiled=True), "ctx")[0]
    d_a = mine[0]
    return (
        layer_rows,
        grad_rows,
        small[2, 0:128],
        small[2, 128:256],
        d_a[:, :128],
        small[1, :128],
        d_a[:, 128:256],
        d_a[:, 256:384],
        small[1, 128:256],
        d_a[:, 384:].T,
        small[2, 256:384],
        small[2, 384:512],
        small[3, 0:128],
        mine[1],
        small[0],
        mine[2],
        small[3, 128:256],
    )


def solution(mesh):
    in_specs = (
        P(None, "ctx", None),
        P(None, "ctx", None),
        P(),
        P(),
        P(),
        P(None, "wt"),
        P("wt"),
        P(None, "wt"),
        P(None, "wt"),
        P("wt"),
        P("wt", None),
        P(),
        P(),
        P(),
        P(None, "wt"),
        P("wt"),
        P("wt", None),
        P(),
    )
    out_specs = (
        P(None, "ctx", None),
        P(None, "ctx", None),
        P("wt"),
        P("wt"),
        P(None, "wt"),
        P("wt"),
        P(None, "wt"),
        P(None, "wt"),
        P("wt"),
        P("wt", None),
        P("wt"),
        P("wt"),
        P("wt"),
        P(None, "wt"),
        P("wt"),
        P("wt", None),
        P("wt"),
    )
    return jax.shard_map(shards, mesh=mesh, in_specs=in_specs, out_specs=out_specs, check_vma=False)
```

time: 7960 us -> 601 us (0.08)
  local copies, waits for them, and re-layouts: 6920 us -> 28.3 us
  matrix products: 327 us -> 0 us
  other arithmetic: 216 us -> 16.8 us
  waiting for transfers between devices: 343 us -> 450 us
    gather x156 -> x0, local copies, waits for them, and re-layouts: 6180 us -> none  [the longest x80 3250 us: level_mask(): firsts = jnp.take(seg_row, jnp.clip(begin, 0, last_index))]
    dot_general x312 -> x0, matrix products: 327 us -> none  [the longest x40 69.7 us: micro_step(): jnp.einsum('hnqk,nkhd->nqhd', level_scores, key_band, preferred_element_t...]
    reshape x260 -> x0, local copies, waits for them, and re-layouts: 285 us -> none  [the longest x60 103 us: micro_step(): d_queries = d_queries + jnp.einsum('hnqk,nkhd->nqhd', level_scores, key_b...]
    unnamed x8 -> x10, waiting for transfers between devices: 0.13 us -> 222 us
    psum x4 -> x1, waiting for transfers between devices: 271 us -> 58.9 us  [shards(): lax.psum(lax.psum_scatter(grads, 'wt', scatter_dimension=1, tiled=True),...]
    all_gather x0 -> x5, waiting for transfers between devices: none -> 128 us  [the longest x3 98.1 us: shards(): lax.all_gather(t, 'wt')]
    transpose x80 -> x1, local copies, waits for them, and re-layouts: 93.3 us -> 0.91 us  [shards(): d_a[:, 384:]]
    another operation x108 -> x0, local copies, waits for them, and re-layouts: 88.1 us -> none
  transfers between devices with their start and end apart: 16 -> 11, of which waited for: 7 -> 9; matrix products, arithmetic and copies ran while one was open for 86% -> 5% of each run, Pallas kernels for 0% -> 1%
where the time goes in v1:
time: 601 us; the launch traced here: 600 us
  waiting for transfers between devices  450 us (75%)
  blocking collectives  50.7 us (8%)
  Pallas kernels  36.8 us (6%)
  local copies, waits for them, and re-layouts  28.3 us (5%)
  other arithmetic  16.8 us (3%)
  between operations  14 us (2%)
    unnamed x10, waiting for transfers between devices  222 us
    all_gather x3, waiting for transfers between devices, shards(): lax.all_gather(t, 'wt')  98.1 us
    psum x1, waiting for transfers between devices, shards(): lax.psum(lax.psum_scatter(grads, 'wt', scatter_dimension=1, tiled=True),...  58.9 us
    all_gather x1, waiting for transfers between devices, shards(): grad_rows = lax.all_gather(d_source.astype(BF16), 'wt').astype(F32)  26.8 us
    psum x1, blocking collectives, shards(): lax.psum(lax.psum_scatter(sums, 'wt', scatter_dimension=0, tiled=True), '...  23.7 us
    reduce_scatter x1, waiting for transfers between devices, shards(): lax.psum_scatter(far_out, 'ctx', scatter_dimension=1, tiled=True)  23.5 us
    pallas_call x1, Pallas kernels, shards(): pl.pallas_call(middle_body, out_shape=[sds((T, width), F32), sds((T, widt...  23 us
    reduce_scatter x1, waiting for transfers between devices, shards(): lax.psum_scatter(sums, 'wt', scatter_dimension=0, tiled=True)  17.3 us
  transfers between devices with their start and end apart: 11, of which 9 were waited for; matrix products, arithmetic and copies ran while one was open for 5% of the time, Pallas kernels for 1%

profile of v1, /device:TPU:0, one launch (start us, length us, event | category | flops | bytes accessed | tf_op | source)
XLA Modules:
  0.0 600.1 jit_solution(139247772179533481)
XLA Ops:
  7.3 1.1 copy.40
  8.4 1.0 copy.41
  9.4 1.0 copy.42
  10.4 1.7 pad_maximum_fusion.1
  12.2 0.7 all-gather.14.cloned.1.call-update
  13.0 0.7 all-gather.16.cloned.1.call-update
  13.7 0.2 scatter.11
  14.0 0.2 scatter.14
  14.2 15.9 %all_gather.51.extra = f32[4,8,512]{2,1,0:T(8,128)} all-gather(f32[1,8,512]{2,1,0:T(8,128)S(1)} %scatter.14), channel_id=1, replica_groups=mesh['ctx'=8,'wt'=4] {'wt'}, dimensions={0}, use_global_device_ids=true | all-gather | bytes 81920 | tf_op jit(solution)/shard_map/all_gather | solution.py:397
  30.1 0.7 dynamic-slice_bitcast_fusion.1.x
  30.8 1.4 constant_dynamic-slice_fusion.segs
  32.2 29.4 %all-gather.12.cloned.1.call-done = bf16[2048,512]{0,1:T(8,128)(2,1)} async-done(((bf16[512,512]{0,1:T(8,128)(2,1)}), bf16[2048,512]{0,1:T(8,128)(2,1)}) %all-gather.12.cloned.1.call-update) | async-done | bytes 2097168 | tf_op jit(solution)/shard_map/all_gather | solution.py:397
  61.6 3.9 copy.43
  65.5 5.2 shard_map.305
  70.7 1.9 collective-permute-start
  72.6 1.7 dynamic-slice_bitcast_fusion.g2
  74.2 11.1 %all-gather.3.far_in = bf16[4,128,256]{2,1,0:T(8,128)(2,1)} all-gather(bf16[4,16,256]{2,1,0:T(8,128)(2,1)} %get-tuple-element.74), channel_id=5, replica_groups=mesh['ctx'=8,'wt'=4] {'ctx'}, dimensions={1}, use_global_device_ids=true | all-gather | bytes 294912 | tf_op jit(solution)/shard_map/all_gather | solution.py:418
  85.4 22.5 %all-gather.14.cloned.1.call-done = bf16[2048,512]{1,0:T(8,128)(2,1)} async-done(((bf16[512,512]{1,0:T(8,128)(2,1)}), bf16[2048,512]{1,0:T(8,128)(2,1)}) %all-gather.14.cloned.1.call-update) | async-done | bytes 2097168 | tf_op jit(solution)/shard_map/all_gather | solution.py:397
  107.9 46.3 %all-gather.16.cloned.1.call-done = bf16[2048,512]{1,0:T(8,128)(2,1)} async-done(((bf16[512,512]{1,0:T(8,128)(2,1)}), bf16[2048,512]{1,0:T(8,128)(2,1)}) %all-gather.16.cloned.1.call-update) | async-done | bytes 2097168 | tf_op jit(solution)/shard_map/all_gather | solution.py:397
  154.1 0.7 copy-done.3
  154.8 23.0 %shard_map.306 = (f32[256,512]{1,0:T(8,128)}, f32[256,512]{1,0:T(8,128)}, bf16[4,256,128]{2,1,0:T(8,128)(2,1)}, f32[4,2,304,256]{3,2,1,0:T(8,128)}, bf16[4,80,25...) custom-call(bf16[256,512]{1,0:T(8,128)(2,1)} %dynamic-slice_bitcast_fus, ...), custom_call_target="tpu_custom_call" | custom-call | tf_op jit(solution)/shard_map/pallas_call | solution.py:435
  177.9 1.3 collective-permute-start.1
  179.2 3.0 slice_bitcast_fusion.grads_in
  182.2 4.5 slice.115
  186.8 23.5 %reduce-scatter.6.cloned.1.call-done = bf16[4,16,256]{2,1,0:T(8,128)(2,1)} async-done(((bf16[4,128,256]{2,1,0:T(8,128)(2,1)}), bf16[4,16,256]{2,1,0:T(8,128)(2,1)}) %reduce-scatter.6.cloned.1.call-update) | async-done | bytes 32784 | tf_op jit(solution)/shard_map/reduce_scatter | solution.py:462
  210.3 8.6 %shard_map.307 = (f32[256,512]{1,0:T(8,128)}, f32[4,8,512]{2,1,0:T(8,128)}, bf16[4,512,512]{2,1,0:T(8,128)(2,1)}) custom-call(bf16[256,512]{1,0:T(8,128)(2,1)} %dynamic-slice_bitcast_fusion.1.x, f32[1,512]{1,0:T(1,128)} %bitcast.72, bf16[4,512,512]{2,1,0:T(8,128)(2,1)} %bitcast.62, bf16[256,512]{1,0:T(8,128)(2,1)} %get-tuple-element.76.n1, ...), custom_call_target="tpu_custom_call" | custom-call | tf_op jit(solution)/shard_map/pallas_call | solution.py:469
  218.9 6.0 %pad_maximum_fusion = bf16[3,4,512,512]{3,2,1,0:T(8,128)(2,1)} fusion(bf16[2,4,512,512]{3,2,1,0:T(8,128)(2,1)} %slice.115, bf16[1,4,512,512]{3,2,1,0:T(8,128)(2,1)} %bitcast.65), kind=kLoop, calls=%fused_computation | loop fusion | flops 3145728 | bytes 12582912 | tf_op jit(solution)/shard_map/stack | solution.py:477
  225.0 0.5 reduce-scatter.8.cloned.1.call-update
  225.6 0.4 copy-done.1
  226.0 0.7 convert_element_type.15
  226.7 0.0 all-gather.20.cloned.1.call-start
  226.8 0.7 convert_element_type.17
  227.6 0.6 dynamic-slice.23
  228.2 219.8 %all-reduce.7.cloned.1.call-done = bf16[3,4,512,512]{3,2,1,0:T(8,128)(2,1)} async-done(((bf16[3,4,512,512]{3,2,1,0:T(8,128)(2,1)}), bf16[3,4,512,512]{3,2,1,0:T(8,128)(2,1)}) %all-reduce.7.cloned.1.call-update) | async-done | bytes 6291472
  448.0 3.3 constant_dynamic-slice_fusion.1
  451.4 17.3 %reduce-scatter.8.cloned.1.call-done = f32[1,8,512]{2,1,0:T(8,128)} async-done(((f32[4,8,512]{2,1,0:T(8,128)}), f32[1,8,512]{2,1,0:T(8,128)}) %reduce-scatter.8.cloned.1.call-update) | async-done | bytes 16400 | tf_op jit(solution)/shard_map/reduce_scatter | solution.py:479
  468.7 23.7 %psum.14 = f32[1,8,512]{2,1,0:T(8,128)S(1)} all-reduce(f32[1,8,512]{2,1,0:T(8,128)} %reduce-scatter.8.cloned.1.call-done), channel_id=1, replica_groups=mesh['ctx'=8,'wt'=4] {'ctx'}, use_global_device_ids=true, to_apply=%region_2.3 | all-reduce | flops 4096 | bytes 32768 | tf_op jit(solution)/shard_map/psum | solution.py:479
  492.4 0.6 slice.143
  492.9 0.5 slice_bitcast_fusion.5
  493.5 3.5 all-gather.18.cloned.1.call-done
  497.0 2.8 convert
  499.8 26.8 %all-gather.20.cloned.1.call-done = bf16[1024,512]{1,0:T(8,128)(2,1)} async-done(((bf16[256,512]{1,0:T(8,128)(2,1)}), bf16[1024,512]{1,0:T(8,128)(2,1)}) %all-gather.20.cloned.1.call-update) | async-done | bytes 1048592 | tf_op jit(solution)/shard_map/all_gather | solution.py:476
  526.6 2.8 convert.1
  529.4 58.9 %all-reduce.5.cloned.1.call-done = bf16[3,1,512,512]{3,2,1,0:T(8,128)(2,1)} async-done(((bf16[3,1,512,512]{3,2,1,0:T(8,128)(2,1)}), bf16[3,1,512,512]{3,2,1,0:T(8,128)(2,1)}) %all-reduce.5.cloned.1.call-update) | async-done | bytes 1572880 | tf_op jit(solution)/shard_map/psum | solution.py:478
  588.4 1.8 convert_element_type.19
  590.2 1.6 slice_bitcast_fusion.1
  591.9 0.9 slice_bitcast_fusion.4
  592.8 0.8 copy.44
  (33 shorter events, 0.5 us)
Async XLA Ops:
  7.2 22.9 %copy-start = (bf16[4,256,512]{2,1,0:T(8,128)(2,1)S(1)}, bf16[4,256,512]{2,1,0:T(8,128)(2,1)}, u32[]{:S(2)}) copy-start(bf16[4,256,512]{2,1,0:T(8,128)(2,1)} %param.24) | copy-start | bytes 3145732
  7.2 6.5 %copy-start.5 = (f32[512]{0:T(512)S(1)}, f32[512]{0:T(512)}, u32[]{:S(2)}) copy-start(f32[512]{0:T(512)} %param.39) | copy-start | bytes 6148
  7.2 6.5 %copy-start.6 = (f32[128]{0:T(128)S(1)}, f32[128]{0:T(128)}, u32[]{:S(2)}) copy-start(f32[128]{0:T(128)} %param.30) | copy-start | bytes 1540
  7.2 6.7 %copy-start.7 = (f32[128]{0:T(128)S(1)}, f32[128]{0:T(128)}, u32[]{:S(2)}) copy-start(f32[128]{0:T(128)} %param.33) | copy-start | bytes 1540
  7.2 54.3 %all-gather.12.cloned.1.call-start = ((), (), s32[]{:S(2)}) async-start(), calls=%async_computation.5 | async-start | bytes 2621440 | tf_op jit(solution)/shard_map/all_gather | solution.py:397
  12.2 95.7 %all-gather.14.cloned.1.call-start = ((), (), s32[]{:S(2)}) async-start(), calls=%async_computation.6 | async-start | bytes 2621440 | tf_op jit(solution)/shard_map/all_gather | solution.py:397
  12.9 141.2 %all-gather.16.cloned.1.call-start = ((), (), s32[]{:S(2)}) async-start(), calls=%async_computation.7 | async-start | bytes 2621440 | tf_op jit(solution)/shard_map/all_gather | solution.py:397
  13.6 196.6 %reduce-scatter.6.cloned.1.call-start = ((), (), s32[]{:S(2)}) async-start(), calls=%async_computation.2 | async-start | bytes 294912 | tf_op jit(solution)/shard_map/reduce_scatter | solution.py:462
  70.7 83.4 %collective-permute-start = (bf16[4,80,256]{2,1,0:T(8,128)(2,1)}, bf16[4,80,256]{2,1,0:T(8,128)(2,1)S(1)}, u32[]{:S(2)}, u32[]{:S(2)}) collective-permute-start(bf16[4,80,256]{2,1,0:T(8,128)(2,1)} %get-tuple-element.73), channel_id=1, source_target_pairs={{0,4},{4,8},{8,12},{12,16},{16,20},{20,24},{24,28},{1,5},{5,9},{9,... | collective-permute-start | bytes 491528 | tf_op jit(solution)/shard_map/ppermute | solution.py:417
  154.1 0.7 copy-start.3
  177.8 270.2 %all-reduce.7.cloned.1.call-start = ((), (), s32[]{:S(2)}) async-start(), calls=%async_computation.10 | async-start | bytes 12582912
  177.9 8.9 %collective-permute-start.1 = (bf16[4,80,256]{2,1,0:T(8,128)(2,1)}, bf16[4,80,256]{2,1,0:T(8,128)(2,1)S(1)}, u32[]{:S(2)}, u32[]{:S(2)}) collective-permute-start(bf16[4,80,256]{2,1,0:T(8,128)(2,1)} %get-tuple-element.80), channel_id=1, source_target_pairs={{4,0},{8,4},{12,8},{16,12},{20,16},{24,20},{28,24},{5,1},{9,5},{13... | collective-permute-start | bytes 491528 | tf_op jit(solution)/shard_map/ppermute | solution.py:461
  186.8 23.5 %copy-start.4 = (bf16[4,80,256]{2,1,0:T(8,128)(2,1)}, bf16[4,80,256]{2,1,0:T(8,128)(2,1)S(1)}, u32[]{:S(2)}) copy-start(bf16[4,80,256]{2,1,0:T(8,128)(2,1)S(1)} %collective-permute-done.1.near_back) | copy-start | bytes 491524
  224.9 1.0 copy-start.1
  224.9 1.9 copy-start.2
  224.9 2.7 copy-start.8
  225.0 243.7 %reduce-scatter.8.cloned.1.call-start = ((), (), s32[]{:S(2)}) async-start(), calls=%async_computation.3 | async-start | bytes 81920 | tf_op jit(solution)/shard_map/reduce_scatter | solution.py:479
  225.6 271.5 %all-gather.18.cloned.1.call-start = ((), (), s32[]{:S(2)}) async-start(), calls=%async_computation.8 | async-start | bytes 1310720 | tf_op jit(solution)/shard_map/all_gather | solution.py:475
  226.7 299.9 %all-gather.20.cloned.1.call-start = ((), (), s32[]{:S(2)}) async-start(), calls=%async_computation.9 | async-start | bytes 1310720 | tf_op jit(solution)/shard_map/all_gather | solution.py:476
  227.6 360.8 %all-reduce.5.cloned.1.call-start = ((), (), s32[]{:S(2)}) async-start(), calls=%async_computation.4 | async-start | bytes 3145728 | tf_op jit(solution)/shard_map/psum | solution.py:478
Sparse Core Ops, SparseCore 0:
  12.3 49.2 all-gather.11
  63.1 44.6 all-gather.13
  109.4 44.6 all-gather.15
  177.9 32.2 reduce-scatter.5
  225.1 222.8 all-reduce.6
  450.7 17.8 reduce-scatter.7
  470.8 26.1 all-gather.17
  499.1 27.4 all-gather.19
  529.9 58.4 all-reduce.4

commit v2 on v1

v2 whole, which is shorter than its diff:
```python
import functools

import jax
import jax.numpy as jnp
from jax import lax
from jax.experimental import pallas as pl
from jax.experimental.pallas import tpu as pltpu
from jax.sharding import PartitionSpec as P

HEAD_DIM = 64
BLOCK = 16
LEVELS = 10
FINE = 3
EPSILON = 1e-05
NEGATIVE = -1e30
LOG_TWO = 0.6931471805599453
LANES = 128
BF16 = jnp.bfloat16
F32 = jnp.float32


def dot(left, right, dims):
    return lax.dot_general(left, right, (dims, ((), ())), preferred_element_type=F32)


def dot_nn(left, right):
    return dot(left, right, ((1,), (0,)))


def dot_nt(left, right):
    return dot(left, right, ((1,), (1,)))


def dot_tn(left, right):
    return dot(left, right, ((0,), (0,)))


def norm_parts(source):
    centre = jnp.mean(source, axis=-1, keepdims=True)
    centred = source - centre
    variance = jnp.mean(centred * centred, axis=-1, keepdims=True)
    inverse = lax.rsqrt(variance + EPSILON)
    return centred * inverse, inverse


def norm_backward(upstream, normed, inverse, gain):
    scaled = upstream * gain
    first_mean = jnp.mean(scaled, axis=-1, keepdims=True)
    second_mean = jnp.mean(scaled * normed, axis=-1, keepdims=True)
    return inverse * (scaled - first_mean - normed * second_mean)


def iota(shape, axis):
    return lax.broadcasted_iota(jnp.int32, shape, axis)


class Geometry:
    def __init__(self, ctx, wt, tok_dev):
        self.ctx, self.wt, self.tok_dev = ctx, wt, tok_dev
        tokens = ctx * tok_dev
        self.levels = len([l for l in range(LEVELS) if BLOCK * 2**l < tokens])
        self.own_cells = [tok_dev // 2**l if l <= FINE else 0 for l in range(self.levels)]
        self.tile = tok_dev // 2
        self.tile_slots = [BLOCK + self.tile] + [BLOCK * 4 >> (l - 1) if l < FINE else BLOCK for l in range(1, self.levels)]
        self.slots = sum(self.tile_slots)
        self.slot_at = [sum(self.tile_slots[:l]) for l in range(self.levels + 1)]
        self.far = self.levels - (FINE + 2)
        self.near = FINE + 2


def pool_matrix():
    parts = []
    for level, count in ((1, 128), (2, 64), (3, 32)):
        hit = (iota((count, 256), 1) >> level) == iota((count, 256), 0)
        parts.append(jnp.where(hit, 1.0 / 2**level, 0.0))
    return jnp.concatenate(parts, axis=0).astype(BF16)


def coarse_matrix():
    row, column = iota((32, 32), 0), iota((32, 32), 1)
    out = jnp.zeros((32, 32), F32)
    first = 0
    for level, count in ((4, 16), (5, 8), (6, 4), (7, 2), (8, 1)):
        up = level - FINE
        hit = (row >= first) & (row < first + count) & ((column >> up) == row - first)
        out = jnp.where(hit, 1.0 / 2**up, out)
        first += count
    return out.astype(BF16)


def far_matrix(geo, me):
    parts = []
    first = 0
    for step in range(geo.far):
        up = step + 1
        each = BLOCK >> up
        row, column = iota((BLOCK, geo.ctx * BLOCK), 0), iota((BLOCK, geo.ctx * BLOCK), 1)
        group = (me >> up) - 1
        device = (group << up) + (row >> (4 - up))
        wanted = device * BLOCK + first + (row & (each - 1))
        parts.append(jnp.where((column == wanted) & (group >= 0), 1.0, 0.0))
        first += each
    return jnp.concatenate(parts, axis=0).astype(BF16)


def mask_bias(geo, me, segs, tile):
    first_pos = me * geo.tok_dev + tile * geo.tile
    seg_one = jnp.sum((segs < 1).astype(jnp.int32), axis=1, keepdims=True)
    seg_two = jnp.sum((segs < 2).astype(jnp.int32), axis=1, keepdims=True)
    position = first_pos + iota((1, geo.tile), 1)
    begins = jnp.where(position >= seg_two, seg_two, jnp.where(position >= seg_one, seg_one, 0))
    parts = []
    for level in range(geo.levels):
        size, shift = 2**level, level + 4
        count = geo.tile_slots[level]
        span = BLOCK * size
        if level <= FINE:
            base = first_pos - span
        else:
            base = (((me * geo.tok_dev) >> shift) - 1) << shift
        begin = base + size * iota((count, geo.tile), 0)
        lower = jnp.maximum(((position >> shift) - 1) << shift, begins)
        if level == 0:
            upper = position + 1
        else:
            upper = ((position >> (shift - 1)) - 1) << (shift - 1)
        valid = (begin >= lower) & (begin + size <= upper)
        parts.append(jnp.where(valid, level * LOG_TWO, NEGATIVE))
    return jnp.concatenate(parts, axis=0)


def both_heads(pair):
    lane = iota(pair.shape, 1)
    zero = jnp.zeros_like(pair)
    return jnp.concatenate([jnp.where(lane < HEAD_DIM, pair, zero), jnp.where(lane >= HEAD_DIM, pair, zero)], axis=0)


def own_lanes(stacked):
    rows = stacked.shape[0] // 2
    lane = iota((rows, stacked.shape[1]), 1)
    return jnp.where(lane < HEAD_DIM, stacked[:rows], stacked[rows:])


def project(w, n1, weights, extra, q, own, cells, near, far):
    out = dot_nn(n1[...], weights[0, w, :, : 3 * LANES])
    bias = extra[w, 1:2, :]
    q[w] = ((out[:, :LANES] + bias[:, :LANES]).astype(BF16) * 0.125).astype(BF16)
    kv = jnp.concatenate(
        [out[:, LANES : 2 * LANES], out[:, 2 * LANES :] + bias[:, LANES : 2 * LANES]], axis=1
    ).astype(BF16)
    own[w] = kv
    fine = dot_nn(pool_matrix(), kv).astype(BF16)
    cells[w] = fine
    rough = dot_nn(coarse_matrix(), fine[192:224]).astype(BF16)
    near[w, 0:16] = kv[240:256]
    near[w, 16:32] = fine[112:128]
    near[w, 32:48] = fine[176:192]
    near[w, 48:64] = fine[208:224]
    near[w, 64:80] = rough[0:16]
    far[w] = rough[16:32]


def tables(geo, w, pick, own, cells, near_in, far_in, table):
    blocks = far_in[:, w].reshape(geo.ctx * BLOCK, 2 * LANES)
    rough = dot_nn(pick, blocks).astype(BF16)
    at = geo.slot_at
    table[w, 0, 0:16] = near_in[w, 0:16]
    table[w, 0, 16:144] = own[w, 0:128]
    table[w, 1, 0:144] = own[w, 112:256]
    table[w, 0, at[1] : at[1] + 16] = near_in[w, 16:32]
    table[w, 0, at[1] + 16 : at[2]] = cells[w, 0:48]
    table[w, 1, at[1] : at[2]] = cells[w, 48:112]
    table[w, 0, at[2] : at[2] + 16] = near_in[w, 32:48]
    table[w, 0, at[2] + 16 : at[3]] = cells[w, 128:144]
    table[w, 1, at[2] : at[3]] = cells[w, 144:176]
    table[w, 0, at[3] : at[4]] = near_in[w, 48:64]
    table[w, 1, at[3] : at[4]] = cells[w, 192:208]
    for tile in (0, 1):
        table[w, tile, at[4] : at[5]] = near_in[w, 64:80]
        table[w, tile, at[5] :] = rough


def attend(geo, w, tile, q, table, bias, probs, mixed):
    rows = slice(tile * geo.tile, (tile + 1) * geo.tile)
    both = both_heads(q[w, rows, :])
    level_bias = bias[tile]
    scores = dot_nt(table[w, tile, :, :LANES], both)
    scores = scores + jnp.concatenate([level_bias, level_bias], axis=1)
    top = jnp.max(scores, axis=0, keepdims=True)
    exponent = jnp.exp(scores - top)
    total = jnp.sum(exponent, axis=0, keepdims=True)
    low = (exponent * (1.0 / total)).astype(BF16)
    probs[w, tile] = low
    mixed[w, rows, :] = own_lanes(dot_tn(low, table[w, tile, :, LANES:])).astype(BF16)


def attend_back(geo, w, tile, q, table, probs, d_mixed, d_queries, d_table):
    rows = slice(tile * geo.tile, (tile + 1) * geo.tile)
    both = both_heads(q[w, rows, :])
    d_both = both_heads(d_mixed[w, rows, :])
    low = probs[w, tile]
    d_probs = dot_nt(table[w, tile, :, LANES:], d_both)
    wide = low.astype(F32)
    product = wide * d_probs
    centre = jnp.sum(product, axis=0, keepdims=True)
    d_scores = (product - wide * centre).astype(BF16)
    d_table[w, tile, :, :LANES] = dot_nn(d_scores, both)
    d_table[w, tile, :, LANES:] = dot_nn(low, d_both)
    back = own_lanes(dot_tn(d_scores, table[w, tile, :, :LANES]))
    d_queries[w, rows, :] = (back * 0.125).astype(BF16)


def return_cells(geo, w, pick, d_table, near, far):
    at = geo.slot_at
    near[w, 0:16] = d_table[w, 0, 0:16].astype(BF16)
    near[w, 16:32] = d_table[w, 0, at[1] : at[1] + 16].astype(BF16)
    near[w, 32:48] = d_table[w, 0, at[2] : at[2] + 16].astype(BF16)
    near[w, 48:64] = d_table[w, 0, at[3] : at[4]].astype(BF16)
    near[w, 64:80] = (d_table[w, 0, at[4] : at[5]] + d_table[w, 1, at[4] : at[5]]).astype(BF16)
    rough = (d_table[w, 0, at[5] :] + d_table[w, 1, at[5] :]).astype(BF16)
    far[:, w] = dot_tn(pick, rough).astype(BF16).reshape(geo.ctx, BLOCK, 2 * LANES)


def own_gradients(geo, w, d_table, near_back, far_back):
    at = geo.slot_at
    first, second = d_table.at[w, 0], d_table.at[w, 1]
    back = near_back[w].astype(F32)
    tokens = jnp.concatenate(
        [first[16:128], first[128:144] + second[0:16], second[16:128], second[128:144] + back[0:16]], axis=0
    )
    far = jnp.sum(far_back[:, w].astype(F32), axis=0)
    rough = jnp.concatenate([back[64:80], far], axis=0)
    fine = dot_tn(coarse_matrix(), rough.astype(BF16))
    level3 = jnp.concatenate([second[at[3] : at[4]], back[48:64]], axis=0) + fine
    cells = jnp.concatenate(
        [
            first[at[1] + 16 : at[2]],
            second[at[1] : at[2]],
            back[16:32],
            first[at[2] + 16 : at[3]],
            second[at[2] : at[3]],
            back[32:48],
            level3,
        ],
        axis=0,
    )
    return tokens + dot_tn(pool_matrix(), cells.astype(BF16))


def feed(w, n2, weights, extra, hidden, slope, result):
    pre = dot_nn(n2[...], weights[1, w]) + extra[w, 0:1, :]
    gate = jax.nn.sigmoid(pre)
    hidden[w] = (pre * gate).astype(BF16)
    slope[w] = gate * (1.0 + pre * (1.0 - gate))
    result[...] += dot_nn(hidden[w], weights[2, w])


def feed_back(w, g2, weights, n2, hidden, slope, sums, grads, total):
    d_hidden = dot_nt(g2[...], weights[2, w]).astype(BF16).astype(F32)
    d_up = (d_hidden * slope[w]).astype(BF16)
    sums[w, 0:1, :] = jnp.sum(d_up.astype(F32), axis=0, keepdims=True)
    grads[2, w] = dot_tn(hidden[w], g2[...]).astype(BF16)
    grads[1, w] = dot_tn(n2[...], d_up).astype(BF16)
    part = dot_nt(d_up, weights[1, w])
    total[...] = part if w == 0 else total[...] + part


def put_sums(geo, sums, column, row):
    at, lanes = 2 + column // 4, slice(column % 4 * LANES, (column % 4 + 1) * LANES)
    for w in range(geo.wt):
        sums[w, at : at + 1, lanes] = row[:, w * LANES : (w + 1) * LANES]


def project_back(geo, w, weights, n1, d_queries, d_table, near_back, far_back, sums, grads, total):
    kv = own_gradients(geo, w, d_table, near_back, far_back).astype(BF16)
    d_qkv = jnp.concatenate([d_queries[w], kv], axis=1)
    sums[w, 1:2, :LANES] = jnp.sum(d_qkv[:, :LANES].astype(F32), axis=0, keepdims=True)
    sums[w, 1:2, LANES : 2 * LANES] = jnp.sum(d_qkv[:, 2 * LANES :].astype(F32), axis=0, keepdims=True)
    grads[0, w, :, : 3 * LANES] = dot_tn(n1[...], d_qkv).astype(BF16)
    part = dot_nt(d_qkv, weights[0, w, :, : 3 * LANES])
    total[...] = part if w == 0 else total[...] + part


def remote(source, target, sent, landed, device):
    return pltpu.make_async_remote_copy(source, target, sent, landed, device_id=device, device_id_type=pl.DeviceIdType.MESH)


class Plane:
    def __init__(self, ctx, c, rows):
        self.ctx, self.c = ctx, c
        self.bits = ctx.bit_length() - 1
        self.each = rows // ctx
        plane_bits = self.bits - 1
        half = plane_bits // 2
        plane, core = c // 2, c % 2
        turned = plane // 2**half + plane % 2**half * 2 ** (plane_bits - half)
        self.places = (plane + core * 2**plane_bits, turned + core * 2**plane_bits)
        self.masks = (
            [2 << s for s in range(plane_bits)] + [1],
            [2 << (s + half) % plane_bits for s in range(plane_bits)] + [1],
        )

    def place(self, order):
        if isinstance(order, int):
            return self.places[order]
        return jnp.where(order == 0, self.places[0], self.places[1])

    def partner(self, order, stage):
        if isinstance(order, int):
            return self.flip(self.masks[order][stage])
        return jnp.where(order == 0, self.flip(self.masks[0][stage]), self.flip(self.masks[1][stage]))

    def flip(self, mask):
        return self.c + mask * (1 - 2 * (self.c // mask % 2))

    def block(self, order, stage, other=False):
        index = self.place(order) // 2**stage
        if other:
            index = index + 1 - 2 * (index % 2)
        size = self.each * 2**stage
        return pl.ds(pl.multiple_of(index * size, size), size)


def fused(geo, *refs):
    (
        x_hbm, g_hbm, segs, n1g, n1b, q_hbm, q_bias, k_hbm, v_hbm, v_bias, o_hbm, out_bias, n2g, n2b,
        up_hbm, up_bias, down_hbm, down_bias,
        out_result, out_source, out_grads, out_sums,
        weights, extra, x, g2, o_own, n1, q, own, cells, near_send, far_send, near_in, far_in,
        table, bias, probs, mixed, middle, n2, hidden, slope, result, total, g1, d_mixed, d_queries, d_table,
        near_give, far_give, near_back, far_back, grads, sums, gathered, source_all,
        from_left, from_right, reduced, sums_in, sums_all, sums_got,
        load_sem, store_sem, zw_send, zw_recv, pw_send, pw_recv, ex_send, ex_recv, halo_send, halo_recv,
        far_s, far_r, back_send, back_recv, farb_s, farb_r, rs_send, rs_recv, zl_send, zl_recv, zr_send, zr_recv,
        ag_send, ag_recv, out_send, out_recv, sm_send, sm_recv, sc_send, sc_recv,
        *landings,
    ) = refs
    C, W = geo.ctx, geo.wt
    c, z = lax.axis_index("ctx"), lax.axis_index("wt")
    plane = Plane(C, c, 512)
    B = plane.bits

    loads = [
        pltpu.make_async_copy(q_hbm, weights.at[0, z, :, pl.ds(0, LANES)], load_sem.at[0]),
        pltpu.make_async_copy(k_hbm, weights.at[0, z, :, pl.ds(LANES, LANES)], load_sem.at[1]),
        pltpu.make_async_copy(v_hbm, weights.at[0, z, :, pl.ds(2 * LANES, LANES)], load_sem.at[2]),
        pltpu.make_async_copy(o_hbm, o_own, load_sem.at[3]),
        pltpu.make_async_copy(up_hbm, weights.at[1, z], load_sem.at[4]),
        pltpu.make_async_copy(down_hbm, weights.at[2, z], load_sem.at[5]),
        pltpu.make_async_copy(x_hbm.at[z], x, load_sem.at[6]),
        pltpu.make_async_copy(g_hbm.at[z], g2, load_sem.at[7]),
    ]
    for copy in loads:
        copy.start()
    near_in[...] = jnp.zeros_like(near_in)
    far_in[...] = jnp.zeros_like(far_in)
    near_back[...] = jnp.zeros_like(near_back)
    far_back[...] = jnp.zeros_like(far_back)
    sums[...] = jnp.zeros_like(sums)
    extra[z] = jnp.zeros_like(extra[z])
    extra[z, 0:1, :] = up_bias[...]
    extra[z, 1:2, :LANES] = q_bias[...]
    extra[z, 1:2, LANES : 2 * LANES] = v_bias[...]

    barrier = pltpu.get_barrier_semaphore()
    for step in range(1, C):
        pl.semaphore_signal(barrier, inc=1, device_id=(lax.rem(c + step, C), z), device_id_type=pl.DeviceIdType.MESH)
    for step in range(1, W):
        pl.semaphore_signal(barrier, inc=1, device_id=(c, lax.rem(z + step, W)), device_id_type=pl.DeviceIdType.MESH)
    for copy in loads[:4]:
        copy.wait()
    weights[0, z, :, 3 * LANES :] = o_own[...].T
    pl.semaphore_wait(barrier, C + W - 2)

    def order_of(k, w):
        return (k + w) % 2

    def arrival(i):
        table_of = []
        for at in range(W):
            seen = []
            for step in range(1, W):
                seen += [w for w in (at - step, at + step) if 0 <= w < W]
            table_of.append(seen[i])
        w = jnp.int32(table_of[0])
        for at in range(1, W):
            w = jnp.where(z == at, table_of[at], w)
        return w

    arrivals = [arrival(i) for i in range(W - 1)]

    def weight_hop(k, w, to, side):
        rows = plane.block(order_of(k, w), 0)
        return remote(weights.at[k, w, rows], weights.at[k, w, rows], zw_send.at[k, w, side], zw_recv.at[k, w], (c, to))

    def weight_first(k):
        @pl.when(z > 0)
        def _():
            weight_hop(k, z, z - 1, 0).start()

        @pl.when(z < W - 1)
        def _():
            weight_hop(k, z, z + 1, 1).start()

    def weight_forward(k, w):
        to = jnp.where(w < z, z + 1, z - 1)
        return (to >= 0) & (to < W), weight_hop(k, w, to, 0)

    def weight_stage(k, w, s):
        order = order_of(k, w)
        rows = plane.block(order, s)
        return remote(
            weights.at[k, w, rows], weights.at[k, w, rows], pw_send.at[k, w, s], pw_recv.at[k, w, s],
            (plane.partner(order, s), z),
        )

    def weight_arrive(k):
        for w in arrivals:
            weight_hop(k, w, lax.rem(z + 1, W), 0).wait_recv()
            onward, copy = weight_forward(k, w)

            @pl.when(onward)
            def _():
                copy.start()

            weight_stage(k, w, 0).start()

    def weight_next(k, s):
        for w in arrivals:
            weight_stage(k, w, s).wait_recv()
            if s + 1 < B:
                weight_stage(k, w, s + 1).start()

    def weight_drain(k):
        @pl.when(z > 0)
        def _():
            weight_hop(k, z, z - 1, 0).wait_send()

        @pl.when(z < W - 1)
        def _():
            weight_hop(k, z, z + 1, 1).wait_send()

        for w in arrivals:
            onward, copy = weight_forward(k, w)

            @pl.when(onward)
            def _():
                copy.wait_send()

            for s in range(B):
                weight_stage(k, w, s).wait_send()

    def extra_copy(step):
        to = lax.rem(z + step, W)
        return remote(extra.at[z], extra.at[z], ex_send.at[step], ex_recv.at[step], (c, to))

    def extra_from(step):
        source = lax.rem(z + W - step, W)
        return remote(extra.at[source], extra.at[source], ex_send.at[step], ex_recv.at[step], (c, source))

    weight_first(0)
    for step in range(1, W):
        extra_copy(step).start()
    loads[4].wait()
    weight_first(1)
    loads[5].wait()
    weight_first(2)
    loads[6].wait()
    normed, _ = norm_parts(x[...].astype(F32))
    n1[...] = (normed * n1g[...] + n1b[...]).astype(BF16)
    bias[0] = mask_bias(geo, c, segs[pl.ds(z, 1), :], 0)
    bias[1] = mask_bias(geo, c, segs[pl.ds(z, 1), :], 1)
    pick = far_matrix(geo, c)
    weight_arrive(0)
    for s in range(B):
        weight_next(0, s)
        if s == 0:
            weight_arrive(1)
    for step in range(1, W):
        extra_from(step).wait_recv()

    for w in range(W):
        project(w, n1, weights, extra, q, own, cells, near_send, far_send)

    def halo(back):
        if back:
            return remote(near_give, near_back, back_send, back_recv, (c - 1, z))
        return remote(near_send, near_in, halo_send, halo_recv, (c + 1, z))

    def needs(source, target):
        need = jnp.bool_(False)
        for step in range(geo.far):
            size = 2 ** (step + 1)
            need = need | (target // size == source // size + 1)
        return need

    def far_copy(device):
        return remote(far_send, far_in.at[c], far_s.at[device], far_r.at[c], (device, z))

    def far_wait(device):
        return remote(far_send, far_in.at[device], far_s.at[device], far_r.at[device], (device, z))

    def give_copy(device):
        return remote(far_give.at[device], far_back.at[c], farb_s.at[device], farb_r.at[c], (device, z))

    def give_wait(device):
        return remote(far_give.at[device], far_back.at[device], farb_s.at[device], farb_r.at[device], (device, z))

    def each_after(action):
        for step in range(1, C):
            device = jnp.minimum(c + step, C - 1)

            @pl.when((c + step < C) & needs(c, device))
            def _():
                action(device)

    def each_before(action):
        for step in range(1, C):
            device = jnp.maximum(c - step, 0)

            @pl.when((c - step >= 0) & needs(device, c))
            def _():
                action(device)

    @pl.when(c < C - 1)
    def _():
        halo(False).start()

    each_after(lambda device: far_copy(device).start())
    weight_next(1, 0)
    weight_arrive(2)
    weight_next(1, 1)

    @pl.when(c > 0)
    def _():
        halo(False).wait_recv()

    each_before(lambda device: far_wait(device).wait_recv())

    for w in range(W):
        tables(geo, w, pick, own, cells, near_in, far_in, table)
        for tile in (0, 1):
            attend(geo, w, tile, q, table, bias, probs, mixed)
        if w == 0:
            weight_next(2, 0)
        if w == 1:
            for s in range(2, B):
                weight_next(1, s)
        if w == 2:
            for s in range(1, B - 1):
                weight_next(2, s)

    acc = x[...].astype(F32) + out_bias[...]
    for w in range(W):
        acc = acc + dot_nt(mixed[w], weights[0, w, :, 3 * LANES :])
    middle[...] = acc
    normed, _ = norm_parts(acc)
    n2[...] = (normed * n2g[...] + n2b[...]).astype(BF16)
    result[...] = acc + down_bias[...]
    weight_next(2, B - 1)
    for w in range(W):
        feed(w, n2, weights, extra, hidden, slope, result)
    gathered[z] = result[...].astype(BF16)

    def row_hop(at, w, to, side):
        rows = (gathered, source_all)[at]
        return remote(rows.at[w], rows.at[w], out_send.at[at, w, side], out_recv.at[at, w], (c, to))

    def rows_first(at):
        @pl.when(z > 0)
        def _():
            row_hop(at, z, z - 1, 0).start()

        @pl.when(z < W - 1)
        def _():
            row_hop(at, z, z + 1, 1).start()

    def row_forward(at, w):
        to = jnp.where(w < z, z + 1, z - 1)
        return (to >= 0) & (to < W), row_hop(at, w, to, 0)

    def rows_arrive(at, i):
        w = arrivals[i]
        row_hop(at, w, lax.rem(z + 1, W), 0).wait_recv()
        onward, copy = row_forward(at, w)

        @pl.when(onward)
        def _():
            copy.start()

    def rows_drain(at):
        @pl.when(z > 0)
        def _():
            row_hop(at, z, z - 1, 0).wait_send()

        @pl.when(z < W - 1)
        def _():
            row_hop(at, z, z + 1, 1).wait_send()

        for w in arrivals:
            onward, copy = row_forward(at, w)

            @pl.when(onward)
            def _():
                copy.wait_send()

    def reduce_copy(k, w, s):
        order = order_of(k, w)
        return remote(
            grads.at[k, w, plane.block(order, s, other=True)],
            landings[s].at[k, w],
            rs_send.at[k, w, s],
            rs_recv.at[k, w, s],
            (plane.partner(order, s), z),
        )

    def reduce_add(k, w, s):
        reduce_copy(k, w, s).wait_recv()
        rows = plane.block(order_of(k, w), s)
        grads[k, w, rows] = (grads[k, w, rows].astype(F32) + landings[s][k, w].astype(F32)).astype(BF16)
        if s > 0:
            reduce_copy(k, w, s - 1).start()

    def line_copy(k, w, right):
        rows = plane.block(order_of(k, w), 0)
        if right:
            return remote(grads.at[k, w, rows], from_left.at[k, w], zr_send.at[k, w], zr_recv.at[k, w], (c, z + 1))
        return remote(grads.at[k, w, rows], from_right.at[k, w], zl_send.at[k, w], zl_recv.at[k, w], (c, z - 1))

    def line_send(k, w):
        rows = plane.block(order_of(k, w), 0)

        @pl.when(w > z)
        def _():
            @pl.when(z > 0)
            def _():
                line_copy(k, w, True).wait_recv()
                grads[k, w, rows] = (grads[k, w, rows].astype(F32) + from_left[k, w].astype(F32)).astype(BF16)

            line_copy(k, w, True).start()

        @pl.when(w < z)
        def _():
            @pl.when(z < W - 1)
            def _():
                line_copy(k, w, False).wait_recv()
                grads[k, w, rows] = (grads[k, w, rows].astype(F32) + from_right[k, w].astype(F32)).astype(BF16)

            line_copy(k, w, False).start()

    def line_drain(k, w):
        @pl.when(w > z)
        def _():
            line_copy(k, w, True).wait_send()

        @pl.when(w < z)
        def _():
            line_copy(k, w, False).wait_send()

    def own_rows(k):
        return plane.block(order_of(k, z), 0)

    def line_end(k):
        rows = own_rows(k)
        total_now = grads[k, z, rows].astype(F32)

        @pl.when(z > 0)
        def _():
            line_copy(k, z, True).wait_recv()

        @pl.when(z < W - 1)
        def _():
            line_copy(k, z, False).wait_recv()

        left = jnp.where(z > 0, from_left[k, z].astype(F32), 0.0)
        right = jnp.where(z < W - 1, from_right[k, z].astype(F32), 0.0)
        reduced[k, rows] = (total_now + left + right).astype(BF16)
        gather_copy(k, 0).start()

    def gather_copy(k, s):
        order = order_of(k, z)
        rows = plane.block(order, s)
        return remote(reduced.at[k, rows], reduced.at[k, rows], ag_send.at[k, s], ag_recv.at[k, s], (plane.partner(order, s), z))

    def gather_next(k, s):
        gather_copy(k, s).wait_recv()
        if s + 1 < B:
            gather_copy(k, s + 1).start()

    line_order = []
    for step in range((W + 1) // 2):
        line_order += [W - 1 - step] + ([step] if step != W - 1 - step else [])

    rows_first(0)
    loads[7].wait()
    for w in range(W):
        feed_back(w, g2, weights, n2, hidden, slope, sums, grads, total)
        reduce_copy(2, w, B - 1).start()
        reduce_copy(1, w, B - 1).start()
        if w > 0:
            reduce_add(2, w - 1, B - 1)
            reduce_add(1, w - 1, B - 1)
    rows_arrive(0, 0)
    normed, inverse = norm_parts(middle[...])
    d_normed = total[...]
    wide = g2[...].astype(F32)
    first = wide + norm_backward(d_normed, normed, inverse, n2g[...])
    g1[...] = first
    low = first.astype(BF16)
    put_sums(geo, sums, 2, jnp.sum(first, axis=0, keepdims=True))
    put_sums(geo, sums, 3, jnp.sum(d_normed * normed, axis=0, keepdims=True))
    put_sums(geo, sums, 4, jnp.sum(d_normed, axis=0, keepdims=True))
    put_sums(geo, sums, 5, jnp.sum(wide, axis=0, keepdims=True))
    reduce_add(2, W - 1, B - 1)
    reduce_add(1, W - 1, B - 1)
    for w in range(W):
        d_mixed[w] = dot_nn(low, weights[0, w, :, 3 * LANES :]).astype(BF16)
        grads[0, w, :, 3 * LANES :] = dot_tn(low, mixed[w]).astype(BF16)
    for w in range(W):
        for tile in (0, 1):
            attend_back(geo, w, tile, q, table, probs, d_mixed, d_queries, d_table)
        return_cells(geo, w, pick, d_table, near_give, far_give)
        if w == 1:
            rows_arrive(0, 1)
        for s in range(B - 2, 0, -1):
            reduce_add(2, w, s)

    @pl.when(c > 0)
    def _():
        halo(True).start()

    each_before(lambda device: give_copy(device).start())
    for w in range(W):
        for s in range(B - 2, 0, -1):
            reduce_add(1, w, s)
    rows_arrive(0, 2)

    @pl.when(c < C - 1)
    def _():
        halo(True).wait_recv()

    each_after(lambda device: give_wait(device).wait_recv())
    for w in range(W):
        project_back(geo, w, weights, n1, d_queries, d_table, near_back, far_back, sums, grads, total)
        reduce_copy(0, w, B - 1).start()
        reduce_add(2, w, 0)
    normed, inverse = norm_parts(x[...].astype(F32))
    d_normed = total[...]
    source_all[z] = (g1[...] + norm_backward(d_normed, normed, inverse, n1g[...])).astype(BF16)
    rows_first(1)
    put_sums(geo, sums, 0, jnp.sum(d_normed * normed, axis=0, keepdims=True))
    put_sums(geo, sums, 1, jnp.sum(d_normed, axis=0, keepdims=True))

    def sums_copy(step):
        to = lax.rem(z + step, W)
        return remote(sums.at[to], sums_in.at[step], sm_send.at[step], sm_recv.at[step], (c, to))

    def sums_stage(s):
        return remote(sums_all.at[s], sums_got.at[s], sc_send.at[s], sc_recv.at[s], (plane.flip(1 << s), z))

    for step in range(1, W):
        sums_copy(step).start()
    for w in range(W):
        reduce_add(0, w, B - 1)
    for w in line_order:
        line_send(2, w)
    for w in range(W):
        reduce_add(1, w, 0)
    rows_arrive(1, 0)
    line_end(2)
    for w in line_order:
        line_send(1, w)
    total_sums = sums[z]
    for step in range(1, W):
        sums_copy(step).wait_recv()
        total_sums = total_sums + sums_in[step]
    sums_all[0] = total_sums
    for s in range(B):
        sums_stage(s).start()
        sums_stage(s).wait_recv()
        sums_all[s + 1] = sums_all[s] + sums_got[s]
    gather_next(2, 0)
    rows_arrive(1, 1)
    line_end(1)
    for w in range(W):
        for s in range(B - 2, 0, -1):
            reduce_add(0, w, s)
    for s in range(1, B):
        gather_next(2, s)
    gather_next(1, 0)
    for w in range(W):
        reduce_add(0, w, 0)
    for s in range(1, B):
        gather_next(1, s)
    for w in line_order:
        line_send(0, w)
    rows_arrive(1, 2)
    line_end(0)
    stores = [
        pltpu.make_async_copy(gathered, out_result, store_sem.at[0]),
        pltpu.make_async_copy(source_all, out_source, store_sem.at[1]),
        pltpu.make_async_copy(sums_all.at[B], out_sums, store_sem.at[2]),
        pltpu.make_async_copy(reduced.at[1], out_grads.at[1], store_sem.at[3]),
        pltpu.make_async_copy(reduced.at[2], out_grads.at[2], store_sem.at[4]),
        pltpu.make_async_copy(reduced.at[0], out_grads.at[0], store_sem.at[5]),
    ]
    for copy in stores[:5]:
        copy.start()
    for s in range(B):
        gather_next(0, s)
    stores[5].start()

    for k in range(3):
        weight_drain(k)
        for w in range(W):
            for s in range(B):
                reduce_copy(k, w, s).wait_send()
            line_drain(k, w)
        for s in range(B):
            gather_copy(k, s).wait_send()
    for at in (0, 1):
        rows_drain(at)
    for step in range(1, W):
        extra_copy(step).wait_send()
        sums_copy(step).wait_send()
    for s in range(B):
        sums_stage(s).wait_send()

    @pl.when(c < C - 1)
    def _():
        halo(False).wait_send()

    @pl.when(c > 0)
    def _():
        halo(True).wait_send()

    each_after(lambda device: far_copy(device).wait_send())
    each_before(lambda device: give_copy(device).wait_send())
    for copy in stores:
        copy.wait()


def unpack(result, source, grads, sums, *outs):
    (
        layer_out, input_grad, d_n1g, d_n1b, d_q, d_qb, d_k, d_v, d_vb, d_o, d_ob, d_n2g, d_n2b, d_up, d_upb, d_down, d_db,
    ) = outs
    layer_out[...] = result[...].astype(F32)
    input_grad[...] = source[...].astype(F32)
    wide = grads[0].astype(F32)
    d_q[...] = wide[:, :LANES]
    d_k[...] = wide[:, LANES : 2 * LANES]
    d_v[...] = wide[:, 2 * LANES : 3 * LANES]
    d_o[...] = wide[:, 3 * LANES :].T
    d_up[...] = grads[1].astype(F32)
    d_down[...] = grads[2].astype(F32)
    for at, out in enumerate((d_n1g, d_n1b, d_ob, d_n2g, d_n2b, d_db)):
        row, lane = 2 + at // 4, at % 4 * LANES
        out[...] = sums[row : row + 1, lane : lane + LANES]
    d_qb[...] = sums[1:2, :LANES]
    d_vb[...] = sums[1:2, LANES : 2 * LANES]
    d_upb[...] = sums[0:1, :]


def shards(
    x_in,
    grad_out,
    seg_ids,
    norm1_gain,
    norm1_bias,
    q_weight,
    q_bias,
    k_weight,
    v_weight,
    v_bias,
    out_weight,
    out_bias,
    norm2_gain,
    norm2_bias,
    up_weight,
    up_bias,
    down_weight,
    down_bias,
):
    C, W = lax.axis_size("ctx"), lax.axis_size("wt")
    runs, T, width = x_in.shape
    hidden = up_weight.shape[1]
    geo = Geometry(C, W, T)
    S, B = geo.slots, C.bit_length() - 1
    each = width // C
    assert runs == W and hidden == width and q_weight.shape[1] == LANES and T == 256
    sds = jax.ShapeDtypeStruct
    vmem, dma = pltpu.VMEM, pltpu.SemaphoreType.DMA
    row = lambda v: v.reshape(1, -1)
    pair = 2 * LANES
    scratch = [
        vmem((3, W, width, width), BF16),
        vmem((W, 8, width), F32),
        vmem((T, width), BF16),
        vmem((T, width), BF16),
        vmem((LANES, width), BF16),
        vmem((T, width), BF16),
        vmem((W, T, LANES), BF16),
        vmem((W, T, pair), BF16),
        vmem((W, 224, pair), BF16),
        vmem((W, 80, pair), BF16),
        vmem((W, 16, pair), BF16),
        vmem((W, 80, pair), BF16),
        vmem((C, W, 16, pair), BF16),
        vmem((W, 2, S, pair), BF16),
        vmem((2, S, geo.tile), F32),
        vmem((W, 2, S, pair), BF16),
        vmem((W, T, LANES), BF16),
        vmem((T, width), F32),
        vmem((T, width), BF16),
        vmem((W, T, hidden), BF16),
        vmem((W, T, hidden), F32),
        vmem((T, width), F32),
        vmem((T, width), F32),
        vmem((T, width), F32),
        vmem((W, T, LANES), BF16),
        vmem((W, T, LANES), BF16),
        vmem((W, 2, S, pair), F32),
        vmem((W, 80, pair), BF16),
        vmem((C, W, 16, pair), BF16),
        vmem((W, 80, pair), BF16),
        vmem((C, W, 16, pair), BF16),
        vmem((3, W, width, width), BF16),
        vmem((W, 8, width), F32),
        vmem((W, T, width), BF16),
        vmem((W, T, width), BF16),
        vmem((3, W, each, width), BF16),
        vmem((3, W, each, width), BF16),
        vmem((3, width, width), BF16),
        vmem((W, 8, width), F32),
        vmem((B + 1, 8, width), F32),
        vmem((B, 8, width), F32),
        dma((8,)),
        dma((6,)),
        dma((3, W, 2)),
        dma((3, W)),
        dma((3, W, B)),
        dma((3, W, B)),
        dma((W,)),
        dma((W,)),
        dma(()),
        dma(()),
        dma((C,)),
        dma((C,)),
        dma(()),
        dma(()),
        dma((C,)),
        dma((C,)),
        dma((3, W, B)),
        dma((3, W, B)),
        dma((3, W)),
        dma((3, W)),
        dma((3, W)),
        dma((3, W)),
        dma((3, B)),
        dma((3, B)),
        dma((2, W, 2)),
        dma((2, W)),
        dma((W,)),
        dma((W,)),
        dma((B,)),
        dma((B,)),
    ] + [vmem((3, W, each * 2**s, width), BF16) for s in range(B)]
    far, near = pl.BlockSpec(memory_space=pl.ANY), pl.BlockSpec(memory_space=pltpu.VMEM)
    result, source, grads, sums = pl.pallas_call(
        functools.partial(fused, geo),
        name="fused",
        out_shape=[sds((W, T, width), BF16), sds((W, T, width), BF16), sds((3, width, width), BF16), sds((8, width), F32)],
        in_specs=[far, far, near, near, near, far, near, far, far, near, far, near, near, near, far, near, far, near],
        out_specs=[far] * 4,
        scratch_shapes=scratch,
        compiler_params=pltpu.CompilerParams(collective_id=0, has_side_effects=True, vmem_limit_bytes=58 * 2**20),
    )(
        x_in, grad_out, seg_ids, row(norm1_gain), row(norm1_bias), q_weight, row(q_bias), k_weight, v_weight, row(v_bias),
        out_weight, row(out_bias), row(norm2_gain), row(norm2_bias), up_weight, row(up_bias), down_weight, row(down_bias),
    )
    part = width // W
    rows = lambda shape: pl.BlockSpec(shape, lambda i: (i, 0))
    still = lambda shape: pl.BlockSpec(shape, lambda i: (0, 0))
    one, wide = (sds((1, LANES), F32), still((1, LANES))), (sds((1, hidden), F32), still((1, hidden)))
    blocks = (sds((W, T, width), F32), pl.BlockSpec((1, T, width), lambda i: (i, 0, 0)))
    thin = (sds((width, LANES), F32), rows((part, LANES)))
    full = (sds((width, width), F32), rows((part, width)))
    turned = (sds((LANES, width), F32), pl.BlockSpec((LANES, part), lambda i: (0, i)))
    outs = [blocks, blocks, one, one, thin, one, thin, thin, one, turned, one, one, one, full, wide, full, one]
    values = pl.pallas_call(
        unpack,
        name="unpack",
        grid=(W,),
        out_shape=[o[0] for o in outs],
        in_specs=[blocks[1], blocks[1], pl.BlockSpec((3, part, width), lambda i: (0, i, 0)), still((8, width))],
        out_specs=[o[1] for o in outs],
    )(result, source, grads, sums)
    return tuple(v.reshape(-1) if v.shape[0] == 1 else v for v in values)


def solution(mesh):
    in_specs = (
        P(None, "ctx", None),
        P(None, "ctx", None),
        P(),
        P(),
        P(),
        P(None, "wt"),
        P("wt"),
        P(None, "wt"),
        P(None, "wt"),
        P("wt"),
        P("wt", None),
        P(),
        P(),
        P(),
        P(None, "wt"),
        P("wt"),
        P("wt", None),
        P(),
    )
    out_specs = (
        P(None, "ctx", None),
        P(None, "ctx", None),
        P("wt"),
        P("wt"),
        P(None, "wt"),
        P("wt"),
        P(None, "wt"),
        P(None, "wt"),
        P("wt"),
        P("wt", None),
        P("wt"),
        P("wt"),
        P("wt"),
        P(None, "wt"),
        P("wt"),
        P("wt", None),
        P("wt"),
    )
    return jax.shard_map(shards, mesh=mesh, in_specs=in_specs, out_specs=out_specs, check_vma=False)
```

time: 601 us -> 173 us (0.29)
  waiting for transfers between devices: 450 us -> 0 us
  Pallas kernels: 36.8 us -> 171 us
  blocking collectives: 50.7 us -> 0 us
  local copies, waits for them, and re-layouts: 28.3 us -> 0 us
  other arithmetic: 16.8 us -> 0 us
  between operations: 14 us -> 0.83 us
    unnamed x10 -> x0, waiting for transfers between devices: 222 us -> none
    pallas_call x3 -> x2, Pallas kernels: 36.8 us -> 171 us  [the longest x1 166 us: shards(): pl.pallas_call(functools.partial(fused, geo), name='fused', out_shape=[sd...]
    all_gather x5 -> x0, waiting for transfers between devices: 128 us -> none  [the longest x3 98.1 us: shards(): lax.all_gather(t, 'wt')]
    psum x1 -> x0, waiting for transfers between devices: 58.9 us -> none  [shards(): lax.psum(lax.psum_scatter(grads, 'wt', scatter_dimension=1, tiled=True),...]
    reduce_scatter x2 -> x0, waiting for transfers between devices: 40.8 us -> none  [the longest x1 23.5 us: shards(): lax.psum_scatter(far_out, 'ctx', scatter_dimension=1, tiled=True)]
    all_gather x2 -> x0, blocking collectives: 27 us -> none  [the longest x1 15.9 us: shards(): lax.all_gather(t, 'wt')]
    psum x1 -> x0, blocking collectives: 23.7 us -> none  [shards(): lax.psum(lax.psum_scatter(sums, 'wt', scatter_dimension=0, tiled=True), '...]
    convert_element_type x5 -> x0, other arithmetic: 8.97 us -> none  [the longest x2 3.57 us: shards(): grad_rows = lax.all_gather(d_source.astype(BF16), 'wt').astype(F32)]
  transfers between devices with their start and end apart: 11 -> 0, of which waited for: 9 -> 0; matrix products, arithmetic and copies ran while one was open for 5% -> 0% of each run, Pallas kernels for 1% -> 0%
where the time goes in v2:
time: 173 us; the launch traced here: 172 us
  Pallas kernels  171 us (99%)
    pallas_call x1, Pallas kernels, shards(): pl.pallas_call(functools.partial(fused, geo), name='fused', out_shape=[sd...  166 us
    pallas_call x1, Pallas kernels, shards(): pl.pallas_call(unpack, name='unpack', grid=(W,), out_shape=[o[0] for o in...  5.34 us

profile of v2, /device:TPU:0, one launch (start us, length us, event | category | flops | bytes accessed | tf_op | source)
XLA Modules:
  0.0 171.9 jit_solution(13892248897768678223)
XLA Ops:
  0.7 165.8 %fused.1 = (bf16[4,256,512]{2,1,0:T(8,128)(2,1)}, bf16[4,256,512]{2,1,0:T(8,128)(2,1)}, bf16[3,512,512]{2,1,0:T(8,128)(2,1)}, f32[8,512]{1,0:T(8,128)}) custom-call(bf16[4,256,512]{2,1,0:T(8,128)(2,1)} %refs_0_.1, bf16[4,256,512]{2,1,0:T(8,128)(2,1)} %refs_1_.1, s32[4,2048]{1,0:T(4,128)} %refs_2_.1, f32[1,512]{1,0:T(1,128)} %bitcast.18, f32[1,512]{1,0:T(1,128)} %bitcast.19, ...), custom_call_target="tpu_custom_call" | custom-call | tf_op jit(solution)/shard_map/fused/pallas_call | solution.py:969
  166.5 5.3 %unpack.1 = (f32[4,256,512]{2,1,0:T(8,128)}, f32[4,256,512]{2,1,0:T(8,128)}, f32[1,128]{1,0:T(1,128)}, f32[1,128]{1,0:T(1,128)}, f32[512,128]{1,0:T(8,128)}, /*i...) custom-call(bf16[4,256,512]{2,1,0:T(8,128)(2,1)} %get-tuple-element., ...), custom_call_target="tpu_custom_call" | custom-call | tf_op jit(solution)/shard_map/unpack/pallas_call | solution.py:990

commit v3 on v2

--- a/solution.py
+++ b/solution.py
@@ -255,14 +255,14 @@
     result[...] += dot_nn(hidden[w], weights[2, w])
 
 
-def feed_back(w, g2, weights, n2, hidden, slope, sums, grads, total):
+def feed_back(first, w, g2, weights, n2, hidden, slope, sums, grads, total):
     d_hidden = dot_nt(g2[...], weights[2, w]).astype(BF16).astype(F32)
     d_up = (d_hidden * slope[w]).astype(BF16)
     sums[w, 0:1, :] = jnp.sum(d_up.astype(F32), axis=0, keepdims=True)
     grads[2, w] = dot_tn(hidden[w], g2[...]).astype(BF16)
     grads[1, w] = dot_tn(n2[...], d_up).astype(BF16)
     part = dot_nt(d_up, weights[1, w])
-    total[...] = part if w == 0 else total[...] + part
+    total[...] = part if first else total[...] + part
 
 
 def put_sums(geo, sums, column, row):
@@ -271,14 +271,14 @@
         sums[w, at : at + 1, lanes] = row[:, w * LANES : (w + 1) * LANES]
 
 
-def project_back(geo, w, weights, n1, d_queries, d_table, near_back, far_back, sums, grads, total):
+def project_back(geo, first, w, weights, n1, d_queries, d_table, near_back, far_back, sums, grads, total):
     kv = own_gradients(geo, w, d_table, near_back, far_back).astype(BF16)
     d_qkv = jnp.concatenate([d_queries[w], kv], axis=1)
     sums[w, 1:2, :LANES] = jnp.sum(d_qkv[:, :LANES].astype(F32), axis=0, keepdims=True)
     sums[w, 1:2, LANES : 2 * LANES] = jnp.sum(d_qkv[:, 2 * LANES :].astype(F32), axis=0, keepdims=True)
     grads[0, w, :, : 3 * LANES] = dot_tn(n1[...], d_qkv).astype(BF16)
     part = dot_nt(d_qkv, weights[0, w, :, : 3 * LANES])
-    total[...] = part if w == 0 else total[...] + part
+    total[...] = part if first else total[...] + part
 
 
 def remote(source, target, sent, landed, device):
@@ -329,9 +329,9 @@
         weights, extra, x, g2, o_own, n1, q, own, cells, near_send, far_send, near_in, far_in,
         table, bias, probs, mixed, middle, n2, hidden, slope, result, total, g1, d_mixed, d_queries, d_table,
         near_give, far_give, near_back, far_back, grads, sums, gathered, source_all,
-        from_left, from_right, reduced, sums_in, sums_all, sums_got,
+        from_line, reduced, sums_in, sums_all, sums_got,
         load_sem, store_sem, zw_send, zw_recv, pw_send, pw_recv, ex_send, ex_recv, halo_send, halo_recv,
-        far_s, far_r, back_send, back_recv, farb_s, farb_r, rs_send, rs_recv, zl_send, zl_recv, zr_send, zr_recv,
+        far_s, far_r, back_send, back_recv, farb_s, farb_r, rs_send, rs_recv, zl_send, zl_recv,
         ag_send, ag_recv, out_send, out_recv, sm_send, sm_recv, sc_send, sc_recv,
         *landings,
     ) = refs
@@ -389,22 +389,17 @@
 
     arrivals = [arrival(i) for i in range(W - 1)]
 
-    def weight_hop(k, w, to, side):
+    def weight_line(k, w, to):
         rows = plane.block(order_of(k, w), 0)
-        return remote(weights.at[k, w, rows], weights.at[k, w, rows], zw_send.at[k, w, side], zw_recv.at[k, w], (c, to))
+        return remote(weights.at[k, w, rows], weights.at[k, w, rows], zw_send.at[k, to], zw_recv.at[k, w], (c, to))
 
     def weight_first(k):
-        @pl.when(z > 0)
-        def _():
-            weight_hop(k, z, z - 1, 0).start()
-
-        @pl.when(z < W - 1)
-        def _():
-            weight_hop(k, z, z + 1, 1).start()
-
-    def weight_forward(k, w):
-        to = jnp.where(w < z, z + 1, z - 1)
-        return (to >= 0) & (to < W), weight_hop(k, w, to, 0)
+        for step in (1, 2, 3)[: W - 1]:
+            for to, there in ((z - step, z >= step), (z + step, z + step < W)):
+
+                @pl.when(there)
+                def _():
+                    weight_line(k, z, to).start()
 
     def weight_stage(k, w, s):
         order = order_of(k, w)
@@ -414,39 +409,24 @@
             (plane.partner(order, s), z),
         )
 
-    def weight_arrive(k):
+    def weight_event(k, i, s):
+        w = arrivals[i]
+        if s == 0:
+            weight_line(k, w, lax.rem(z + 1, W)).wait_recv()
+        else:
+            weight_stage(k, w, s - 1).wait_recv()
+        if s < B:
+            weight_stage(k, w, s).start()
+
+    def weight_events(k, s):
+        for i in range(W - 1):
+            weight_event(k, i, s)
+
+    def weight_drain(k):
+        for step in range(1, W):
+            to = lax.rem(z + step, W)
+            weight_line(k, z, to).wait_send()
         for w in arrivals:
-            weight_hop(k, w, lax.rem(z + 1, W), 0).wait_recv()
-            onward, copy = weight_forward(k, w)
-
-            @pl.when(onward)
-            def _():
-                copy.start()
-
-            weight_stage(k, w, 0).start()
-
-    def weight_next(k, s):
-        for w in arrivals:
-            weight_stage(k, w, s).wait_recv()
-            if s + 1 < B:
-                weight_stage(k, w, s + 1).start()
-
-    def weight_drain(k):
-        @pl.when(z > 0)
-        def _():
-            weight_hop(k, z, z - 1, 0).wait_send()
-
-        @pl.when(z < W - 1)
-        def _():
-            weight_hop(k, z, z + 1, 1).wait_send()
-
-        for w in arrivals:
-            onward, copy = weight_forward(k, w)
-
-            @pl.when(onward)
-            def _():
-                copy.wait_send()
-
             for s in range(B):
                 weight_stage(k, w, s).wait_send()
 
@@ -458,34 +438,10 @@
         source = lax.rem(z + W - step, W)
         return remote(extra.at[source], extra.at[source], ex_send.at[step], ex_recv.at[step], (c, source))
 
-    weight_first(0)
-    for step in range(1, W):
-        extra_copy(step).start()
-    loads[4].wait()
-    weight_first(1)
-    loads[5].wait()
-    weight_first(2)
-    loads[6].wait()
-    normed, _ = norm_parts(x[...].astype(F32))
-    n1[...] = (normed * n1g[...] + n1b[...]).astype(BF16)
-    bias[0] = mask_bias(geo, c, segs[pl.ds(z, 1), :], 0)
-    bias[1] = mask_bias(geo, c, segs[pl.ds(z, 1), :], 1)
-    pick = far_matrix(geo, c)
-    weight_arrive(0)
-    for s in range(B):
-        weight_next(0, s)
-        if s == 0:
-            weight_arrive(1)
-    for step in range(1, W):
-        extra_from(step).wait_recv()
-
-    for w in range(W):
-        project(w, n1, weights, extra, q, own, cells, near_send, far_send)
-
-    def halo(back):
+    def halo(w, back):
         if back:
-            return remote(near_give, near_back, back_send, back_recv, (c - 1, z))
-        return remote(near_send, near_in, halo_send, halo_recv, (c + 1, z))
+            return remote(near_give.at[w], near_back.at[w], back_send.at[w], back_recv.at[w], (c - 1, z))
+        return remote(near_send.at[w], near_in.at[w], halo_send.at[w], halo_recv.at[w], (c + 1, z))
 
     def needs(source, target):
         need = jnp.bool_(False)
@@ -494,17 +450,13 @@
             need = need | (target // size == source // size + 1)
         return need
 
-    def far_copy(device):
-        return remote(far_send, far_in.at[c], far_s.at[device], far_r.at[c], (device, z))
-
-    def far_wait(device):
-        return remote(far_send, far_in.at[device], far_s.at[device], far_r.at[device], (device, z))
-
-    def give_copy(device):
-        return remote(far_give.at[device], far_back.at[c], farb_s.at[device], farb_r.at[c], (device, z))
-
-    def give_wait(device):
-        return remote(far_give.at[device], far_back.at[device], farb_s.at[device], farb_r.at[device], (device, z))
+    def far_copy(w, device, source):
+        return remote(far_send.at[w], far_in.at[source, w], far_s.at[device, w], far_r.at[source, w], (device, z))
+
+    def give_copy(w, device, source):
+        return remote(
+            far_give.at[device, w], far_back.at[source, w], farb_s.at[device, w], farb_r.at[source, w], (device, z)
+        )
 
     def each_after(action):
         for step in range(1, C):
@@ -522,33 +474,91 @@
             def _():
                 action(device)
 
-    @pl.when(c < C - 1)
-    def _():
-        halo(False).start()
-
-    each_after(lambda device: far_copy(device).start())
-    weight_next(1, 0)
-    weight_arrive(2)
-    weight_next(1, 1)
-
-    @pl.when(c > 0)
-    def _():
-        halo(False).wait_recv()
-
-    each_before(lambda device: far_wait(device).wait_recv())
-
-    for w in range(W):
+    def halo_start(w):
+        @pl.when(c < C - 1)
+        def _():
+            halo(w, False).start()
+
+        each_after(lambda device: far_copy(w, device, c).start())
+
+    def halo_wait(w):
+        @pl.when(c > 0)
+        def _():
+            halo(w, False).wait_recv()
+
+        each_before(lambda device: far_copy(w, device, device).wait_recv())
+
+    def give_start(w):
+        @pl.when(c > 0)
+        def _():
+            halo(w, True).start()
+
+        each_before(lambda device: give_copy(w, device, c).start())
+
+    def give_wait(w):
+        @pl.when(c < C - 1)
+        def _():
+            halo(w, True).wait_recv()
+
+        each_after(lambda device: give_copy(w, device, device).wait_recv())
+
+    first_three = [z] + arrivals
+
+    def projection(w):
+        project(w, n1, weights, extra, q, own, cells, near_send, far_send)
+        halo_start(w)
+
+    def attention(w):
+        halo_wait(w)
         tables(geo, w, pick, own, cells, near_in, far_in, table)
         for tile in (0, 1):
             attend(geo, w, tile, q, table, bias, probs, mixed)
-        if w == 0:
-            weight_next(2, 0)
-        if w == 1:
-            for s in range(2, B):
-                weight_next(1, s)
-        if w == 2:
-            for s in range(1, B - 1):
-                weight_next(2, s)
+
+    weight_first(0)
+    for step in range(1, W):
+        extra_copy(step).start()
+    loads[6].wait()
+    normed, _ = norm_parts(x[...].astype(F32))
+    n1[...] = (normed * n1g[...] + n1b[...]).astype(BF16)
+    projection(z)
+    bias[0] = mask_bias(geo, c, segs[pl.ds(z, 1), :], 0)
+    bias[1] = mask_bias(geo, c, segs[pl.ds(z, 1), :], 1)
+    pick = far_matrix(geo, c)
+    weight_event(0, 0, 0)
+    weight_event(0, 1, 0)
+    weight_event(0, 0, 1)
+    weight_event(0, 2, 0)
+    loads[4].wait()
+    weight_first(1)
+    attention(z)
+    weight_event(0, 1, 1)
+    for step in range(1, W):
+        extra_from(step).wait_recv()
+    weight_event(0, 0, 2)
+    weight_event(0, 2, 1)
+    weight_events(1, 0)
+    loads[5].wait()
+    weight_first(2)
+    for s in range(3, B + 1):
+        weight_event(0, 0, s)
+    projection(arrivals[0])
+    weight_event(0, 1, 2)
+    for s in range(3, B + 1):
+        weight_event(0, 1, s)
+    projection(arrivals[1])
+    weight_event(0, 2, 2)
+    weight_events(1, 1)
+    for s in range(3, B + 1):
+        weight_event(0, 2, s)
+    projection(arrivals[2])
+    attention(arrivals[0])
+    weight_events(2, 0)
+    attention(arrivals[1])
+    weight_events(1, 2)
+    attention(arrivals[2])
+    weight_events(2, 1)
+    for s in range(3, B + 1):
+        weight_events(1, s)
 
     acc = x[...].astype(F32) + out_bias[...]
     for w in range(W):
@@ -557,52 +567,59 @@
     normed, _ = norm_parts(acc)
     n2[...] = (normed * n2g[...] + n2b[...]).astype(BF16)
     result[...] = acc + down_bias[...]
-    weight_next(2, B - 1)
-    for w in range(W):
-        feed(w, n2, weights, extra, hidden, slope, result)
+    feed(z, n2, weights, extra, hidden, slope, result)
+    weight_events(2, 2)
+    for i in range(W - 1):
+        for s in range(3, B + 1):
+            weight_event(2, i, s)
+        feed(arrivals[i], n2, weights, extra, hidden, slope, result)
     gathered[z] = result[...].astype(BF16)
 
-    def row_hop(at, w, to, side):
+    def row_copy(at, w, to, relayed=False):
         rows = (gathered, source_all)[at]
-        return remote(rows.at[w], rows.at[w], out_send.at[at, w, side], out_recv.at[at, w], (c, to))
+        slot = w if relayed else to
+        return remote(rows.at[w], rows.at[w], out_send.at[at, slot, int(relayed)], out_recv.at[at, w], (c, to))
+
+    relays = W == 4
+    inner = (z > 0) & (z < W - 1) if relays else jnp.bool_(False)
+    across = jnp.where(z < W // 2, z + 2, z - 2)
+    beside = W - 1 - z
+    end = jnp.where(z < W // 2, 0, W - 1)
+
+    def each_direct(action):
+        for step in range(1, W):
+            to = lax.rem(z + step, W)
+            later = (z + to == W - 1) if relays else jnp.bool_(False)
+
+            @pl.when(jnp.logical_not(later))
+            def _():
+                action(to)
 
     def rows_first(at):
-        @pl.when(z > 0)
+        each_direct(lambda to: row_copy(at, z, to).start())
+
+    def rows_relay(at):
+        @pl.when(inner)
         def _():
-            row_hop(at, z, z - 1, 0).start()
-
-        @pl.when(z < W - 1)
+            row_copy(at, across, end).wait_recv()
+            row_copy(at, across, end, True).start()
+            row_copy(at, z, beside).start()
+
+    def rows_wait(at):
+        for step in range(1, W):
+            w = lax.rem(z + step, W)
+
+            @pl.when(jnp.logical_not(inner & (w == across)))
+            def _():
+                row_copy(at, w, w).wait_recv()
+
+    def rows_drain(at):
+        each_direct(lambda to: row_copy(at, z, to).wait_send())
+
+        @pl.when(inner)
         def _():
-            row_hop(at, z, z + 1, 1).start()
-
-    def row_forward(at, w):
-        to = jnp.where(w < z, z + 1, z - 1)
-        return (to >= 0) & (to < W), row_hop(at, w, to, 0)
-
-    def rows_arrive(at, i):
-        w = arrivals[i]
-        row_hop(at, w, lax.rem(z + 1, W), 0).wait_recv()
-        onward, copy = row_forward(at, w)
-
-        @pl.when(onward)
-        def _():
-            copy.start()
-
-    def rows_drain(at):
-        @pl.when(z > 0)
-        def _():
-            row_hop(at, z, z - 1, 0).wait_send()
-
-        @pl.when(z < W - 1)
-        def _():
-            row_hop(at, z, z + 1, 1).wait_send()
-
-        for w in arrivals:
-            onward, copy = row_forward(at, w)
-
-            @pl.when(onward)
-            def _():
-                copy.wait_send()
+            row_copy(at, across, end, True).wait_send()
+            row_copy(at, z, beside).wait_send()
 
     def reduce_copy(k, w, s):
         order = order_of(k, w)
@@ -620,42 +637,22 @@
         grads[k, w, rows] = (grads[k, w, rows].astype(F32) + landings[s][k, w].astype(F32)).astype(BF16)
         if s > 0:
             reduce_copy(k, w, s - 1).start()
-
-    def line_copy(k, w, right):
+        else:
+            line_send(k, w)
+
+    def line_copy(k, w):
         rows = plane.block(order_of(k, w), 0)
-        if right:
-            return remote(grads.at[k, w, rows], from_left.at[k, w], zr_send.at[k, w], zr_recv.at[k, w], (c, z + 1))
-        return remote(grads.at[k, w, rows], from_right.at[k, w], zl_send.at[k, w], zl_recv.at[k, w], (c, z - 1))
+        return remote(grads.at[k, w, rows], from_line.at[k, z], zl_send.at[k, w], zl_recv.at[k, z], (c, w))
 
     def line_send(k, w):
-        rows = plane.block(order_of(k, w), 0)
-
-        @pl.when(w > z)
+        @pl.when(w != z)
         def _():
-            @pl.when(z > 0)
-            def _():
-                line_copy(k, w, True).wait_recv()
-                grads[k, w, rows] = (grads[k, w, rows].astype(F32) + from_left[k, w].astype(F32)).astype(BF16)
-
-            line_copy(k, w, True).start()
-
-        @pl.when(w < z)
+            line_copy(k, w).start()
+
+    def line_drain(k, w):
+        @pl.when(w != z)
         def _():
-            @pl.when(z < W - 1)
-            def _():
-                line_copy(k, w, False).wait_recv()
-                grads[k, w, rows] = (grads[k, w, rows].astype(F32) + from_right[k, w].astype(F32)).astype(BF16)
-
-            line_copy(k, w, False).start()
-
-    def line_drain(k, w):
-        @pl.when(w > z)
-        def _():
-            line_copy(k, w, True).wait_send()
-
-        @pl.when(w < z)
-        def _():
-            line_copy(k, w, False).wait_send()
+            line_copy(k, w).wait_send()
 
     def own_rows(k):
         return plane.block(order_of(k, z), 0)
@@ -663,18 +660,13 @@
     def line_end(k):
         rows = own_rows(k)
         total_now = grads[k, z, rows].astype(F32)
-
-        @pl.when(z > 0)
-        def _():
-            line_copy(k, z, True).wait_recv()
-
-        @pl.when(z < W - 1)
-        def _():
-            line_copy(k, z, False).wait_recv()
-
-        left = jnp.where(z > 0, from_left[k, z].astype(F32), 0.0)
-        right = jnp.where(z < W - 1, from_right[k, z].astype(F32), 0.0)
-        reduced[k, rows] = (total_now + left + right).astype(BF16)
+        for step in range(1, W):
+            source = lax.rem(z + step, W)
+            remote(
+                from_line.at[k, source], from_line.at[k, source], zl_send.at[k, source], zl_recv.at[k, source], (c, source)
+            ).wait_recv()
+            total_now = total_now + from_line[k, source].astype(F32)
+        reduced[k, rows] = total_now.astype(BF16)
         gather_copy(k, 0).start()
 
     def gather_copy(k, s):
@@ -687,67 +679,70 @@
         if s + 1 < B:
             gather_copy(k, s + 1).start()
 
-    line_order = []
-    for step in range((W + 1) // 2):
-        line_order += [W - 1 - step] + ([step] if step != W - 1 - step else [])
-
     rows_first(0)
     loads[7].wait()
     for w in range(W):
-        feed_back(w, g2, weights, n2, hidden, slope, sums, grads, total)
+        feed_back(w == 0, w, g2, weights, n2, hidden, slope, sums, grads, total)
         reduce_copy(2, w, B - 1).start()
         reduce_copy(1, w, B - 1).start()
         if w > 0:
             reduce_add(2, w - 1, B - 1)
             reduce_add(1, w - 1, B - 1)
-    rows_arrive(0, 0)
     normed, inverse = norm_parts(middle[...])
     d_normed = total[...]
     wide = g2[...].astype(F32)
     first = wide + norm_backward(d_normed, normed, inverse, n2g[...])
     g1[...] = first
     low = first.astype(BF16)
-    put_sums(geo, sums, 2, jnp.sum(first, axis=0, keepdims=True))
-    put_sums(geo, sums, 3, jnp.sum(d_normed * normed, axis=0, keepdims=True))
-    put_sums(geo, sums, 4, jnp.sum(d_normed, axis=0, keepdims=True))
-    put_sums(geo, sums, 5, jnp.sum(wide, axis=0, keepdims=True))
     reduce_add(2, W - 1, B - 1)
     reduce_add(1, W - 1, B - 1)
     for w in range(W):
         d_mixed[w] = dot_nn(low, weights[0, w, :, 3 * LANES :]).astype(BF16)
         grads[0, w, :, 3 * LANES :] = dot_tn(low, mixed[w]).astype(BF16)
-    for w in range(W):
+
+    def reduce_both(w, s):
+        reduce_add(2, w, s)
+        reduce_add(1, w, s)
+
+    def give(w):
         for tile in (0, 1):
             attend_back(geo, w, tile, q, table, probs, d_mixed, d_queries, d_table)
         return_cells(geo, w, pick, d_table, near_give, far_give)
-        if w == 1:
-            rows_arrive(0, 1)
-        for s in range(B - 2, 0, -1):
-            reduce_add(2, w, s)
-
-    @pl.when(c > 0)
-    def _():
-        halo(True).start()
-
-    each_before(lambda device: give_copy(device).start())
-    for w in range(W):
-        for s in range(B - 2, 0, -1):
-            reduce_add(1, w, s)
-    rows_arrive(0, 2)
-
-    @pl.when(c < C - 1)
-    def _():
-        halo(True).wait_recv()
-
-    each_after(lambda device: give_wait(device).wait_recv())
-    for w in range(W):
-        project_back(geo, w, weights, n1, d_queries, d_table, near_back, far_back, sums, grads, total)
+        give_start(w)
+
+    def take(w):
+        give_wait(w)
+        project_back(geo, w == 0, w, weights, n1, d_queries, d_table, near_back, far_back, sums, grads, total)
         reduce_copy(0, w, B - 1).start()
-        reduce_add(2, w, 0)
+
+    give(0)
+    give(1)
+    for s in range(B - 2, 0, -1):
+        reduce_both(0, s)
+    give(2)
+    give(3)
+    for s in range(B - 2, 0, -1):
+        reduce_both(1, s)
+    put_sums(geo, sums, 2, jnp.sum(first, axis=0, keepdims=True))
+    put_sums(geo, sums, 3, jnp.sum(d_normed * normed, axis=0, keepdims=True))
+    put_sums(geo, sums, 4, jnp.sum(d_normed, axis=0, keepdims=True))
+    put_sums(geo, sums, 5, jnp.sum(wide, axis=0, keepdims=True))
+    take(0)
+    take(1)
+    for s in range(B - 2, 0, -1):
+        reduce_both(2, s)
+    reduce_both(0, 0)
+    take(2)
+    take(3)
     normed, inverse = norm_parts(x[...].astype(F32))
     d_normed = total[...]
     source_all[z] = (g1[...] + norm_backward(d_normed, normed, inverse, n1g[...])).astype(BF16)
-    rows_first(1)
+    rows_relay(0)
+    for s in range(B - 2, 0, -1):
+        reduce_both(3, s)
+    reduce_both(1, 0)
+    for w in range(W):
+        reduce_add(0, w, B - 1)
     put_sums(geo, sums, 0, jnp.sum(d_normed * normed, axis=0, keepdims=True))
     put_sums(geo, sums, 1, jnp.sum(d_normed, axis=0, keepdims=True))
 
@@ -760,41 +755,31 @@
 
     for step in range(1, W):
         sums_copy(step).start()
+    reduce_both(2, 0)
+    reduce_both(3, 0)
+    rows_first(1)
+    for s in range(B - 2, 0, -1):
+        for w in range(W):
+            reduce_add(0, w, s)
+    line_end(2)
+    line_end(1)
     for w in range(W):
-        reduce_add(0, w, B - 1)
-    for w in line_order:
-        line_send(2, w)
-    for w in range(W):
-        reduce_add(1, w, 0)
-    rows_arrive(1, 0)
-    line_end(2)
-    for w in line_order:
-        line_send(1, w)
+        reduce_add(0, w, 0)
     total_sums = sums[z]
     for step in range(1, W):
         sums_copy(step).wait_recv()
         total_sums = total_sums + sums_in[step]
     sums_all[0] = total_sums
+    sums_stage(0).start()
     for s in range(B):
-        sums_stage(s).start()
         sums_stage(s).wait_recv()
         sums_all[s + 1] = sums_all[s] + sums_got[s]
-    gather_next(2, 0)
-    rows_arrive(1, 1)
-    line_end(1)
-    for w in range(W):
-        for s in range(B - 2, 0, -1):
-            reduce_add(0, w, s)
-    for s in range(1, B):
+        if s + 1 < B:
+            sums_stage(s + 1).start()
         gather_next(2, s)
-    gather_next(1, 0)
-    for w in range(W):
-        reduce_add(0, w, 0)
-    for s in range(1, B):
         gather_next(1, s)
-    for w in line_order:
-        line_send(0, w)
-    rows_arrive(1, 2)
+    rows_wait(0)
+    rows_relay(1)
     line_end(0)
     stores = [
         pltpu.make_async_copy(gathered, out_result, store_sem.at[0]),
@@ -804,11 +789,13 @@
         pltpu.make_async_copy(reduced.at[2], out_grads.at[2], store_sem.at[4]),
         pltpu.make_async_copy(reduced.at[0], out_grads.at[0], store_sem.at[5]),
     ]
-    for copy in stores[:5]:
-        copy.start()
+    for at in (0, 2, 3, 4):
+        stores[at].start()
     for s in range(B):
         gather_next(0, s)
     stores[5].start()
+    rows_wait(1)
+    stores[1].start()
 
     for k in range(3):
         weight_drain(k)
@@ -826,16 +813,18 @@
     for s in range(B):
         sums_stage(s).wait_send()
 
-    @pl.when(c < C - 1)
-    def _():
-        halo(False).wait_send()
-
-    @pl.when(c > 0)
-    def _():
-        halo(True).wait_send()
-
-    each_after(lambda device: far_copy(device).wait_send())
-    each_before(lambda device: give_copy(device).wait_send())
+    for w in range(W):
+
+        @pl.when(c < C - 1)
+        def _():
+            halo(w, False).wait_send()
+
+        @pl.when(c > 0)
+        def _():
+            halo(w, True).wait_send()
+
+        each_after(lambda device: far_copy(w, device, c).wait_send())
+        each_before(lambda device: give_copy(w, device, c).wait_send())
     for copy in stores:
         copy.wait()
 
@@ -929,31 +918,28 @@
         vmem((W, T, width), BF16),
         vmem((W, T, width), BF16),
         vmem((3, W, each, width), BF16),
-        vmem((3, W, each, width), BF16),
         vmem((3, width, width), BF16),
         vmem((W, 8, width), F32),
         vmem((B + 1, 8, width), F32),
         vmem((B, 8, width), F32),
         dma((8,)),
         dma((6,)),
-        dma((3, W, 2)),
+        dma((3, W)),
         dma((3, W)),
         dma((3, W, B)),
         dma((3, W, B)),
         dma((W,)),
         dma((W,)),
-        dma(()),
-        dma(()),
-        dma((C,)),
-        dma((C,)),
-        dma(()),
-        dma(()),
-        dma((C,)),
-        dma((C,)),
+        dma((W,)),
+        dma((W,)),
+        dma((C, W)),
+        dma((C, W)),
+        dma((W,)),
+        dma((W,)),
+        dma((C, W)),
+        dma((C, W)),
         dma((3, W, B)),
         dma((3, W, B)),
-        dma((3, W)),
-        dma((3, W)),
         dma((3, W)),
         dma((3, W)),
         dma((3, B)),

time: 173 us -> 127 us (0.73)
  the two profiles are of different devices: /device:TPU:0 before, /device:TPU:25 now
where the time goes in v3:
time: 127 us; the launch traced here: 126 us
  Pallas kernels  126 us (99%)
    pallas_call x1, Pallas kernels, shards(): pl.pallas_call(functools.partial(fused, geo), name='fused', out_shape=[sd...  120 us
    pallas_call x1, Pallas kernels, shards(): pl.pallas_call(unpack, name='unpack', grid=(W,), out_shape=[o[0] for o in...  5.34 us

profile of v3, /device:TPU:25, one launch (start us, length us, event | category | flops | bytes accessed | tf_op | source)
XLA Modules:
  0.0 126.4 jit_solution(283193251660176725)
XLA Ops:
  0.7 120.2 %fused.1 = (bf16[4,256,512]{2,1,0:T(8,128)(2,1)}, bf16[4,256,512]{2,1,0:T(8,128)(2,1)}, bf16[3,512,512]{2,1,0:T(8,128)(2,1)}, f32[8,512]{1,0:T(8,128)}) custom-call(bf16[4,256,512]{2,1,0:T(8,128)(2,1)} %refs_0_.1, bf16[4,256,512]{2,1,0:T(8,128)(2,1)} %refs_1_.1, s32[4,2048]{1,0:T(4,128)} %refs_2_.1, f32[1,512]{1,0:T(1,128)} %bitcast.18, f32[1,512]{1,0:T(1,128)} %bitcast.19, ...), custom_call_target="tpu_custom_call" | custom-call | tf_op jit(solution)/shard_map/fused/pallas_call | solution.py:955
  120.9 5.3 %unpack.1 = (f32[4,256,512]{2,1,0:T(8,128)}, f32[4,256,512]{2,1,0:T(8,128)}, f32[1,128]{1,0:T(1,128)}, f32[1,128]{1,0:T(1,128)}, f32[512,128]{1,0:T(8,128)}, /*i...) custom-call(bf16[4,256,512]{2,1,0:T(8,128)(2,1)} %get-tuple-element., ...), custom_call_target="tpu_custom_call" | custom-call | tf_op jit(solution)/shard_map/unpack/pallas_call | solution.py:976

commit v4 on v3

--- a/solution.py
+++ b/solution.py
@@ -142,7 +142,7 @@
 
 
 def project(w, n1, weights, extra, q, own, cells, near, far):
-    out = dot_nn(n1[...], weights[0, w, :, : 3 * LANES])
+    out = dot_nn(n1[...], weights[0][w])
     bias = extra[w, 1:2, :]
     q[w] = ((out[:, :LANES] + bias[:, :LANES]).astype(BF16) * 0.125).astype(BF16)
     kv = jnp.concatenate(
@@ -248,20 +248,20 @@
 
 
 def feed(w, n2, weights, extra, hidden, slope, result):
-    pre = dot_nn(n2[...], weights[1, w]) + extra[w, 0:1, :]
+    pre = dot_nn(n2[...], weights[1][w]) + extra[w, 0:1, :]
     gate = jax.nn.sigmoid(pre)
     hidden[w] = (pre * gate).astype(BF16)
     slope[w] = gate * (1.0 + pre * (1.0 - gate))
-    result[...] += dot_nn(hidden[w], weights[2, w])
+    result[...] += dot_nn(hidden[w], weights[2][w])
 
 
 def feed_back(first, w, g2, weights, n2, hidden, slope, sums, grads, total):
-    d_hidden = dot_nt(g2[...], weights[2, w]).astype(BF16).astype(F32)
+    d_hidden = dot_nt(g2[...], weights[2][w]).astype(BF16).astype(F32)
     d_up = (d_hidden * slope[w]).astype(BF16)
     sums[w, 0:1, :] = jnp.sum(d_up.astype(F32), axis=0, keepdims=True)
-    grads[2, w] = dot_tn(hidden[w], g2[...]).astype(BF16)
-    grads[1, w] = dot_tn(n2[...], d_up).astype(BF16)
-    part = dot_nt(d_up, weights[1, w])
+    grads[2][w] = dot_tn(hidden[w], g2[...]).astype(BF16)
+    grads[1][w] = dot_tn(n2[...], d_up).astype(BF16)
+    part = dot_nt(d_up, weights[1][w])
     total[...] = part if first else total[...] + part
 
 
@@ -276,8 +276,8 @@
     d_qkv = jnp.concatenate([d_queries[w], kv], axis=1)
     sums[w, 1:2, :LANES] = jnp.sum(d_qkv[:, :LANES].astype(F32), axis=0, keepdims=True)
     sums[w, 1:2, LANES : 2 * LANES] = jnp.sum(d_qkv[:, 2 * LANES :].astype(F32), axis=0, keepdims=True)
-    grads[0, w, :, : 3 * LANES] = dot_tn(n1[...], d_qkv).astype(BF16)
-    part = dot_nt(d_qkv, weights[0, w, :, : 3 * LANES])
+    grads[0][w] = dot_tn(n1[...], d_qkv).astype(BF16)
+    part = dot_nt(d_qkv, weights[0][w])
     total[...] = part if first else total[...] + part
 
 
@@ -292,18 +292,24 @@
         self.each = rows // ctx
         plane_bits = self.bits - 1
         half = plane_bits // 2
-        plane, core = c // 2, c % 2
-        turned = plane // 2**half + plane % 2**half * 2 ** (plane_bits - half)
-        self.places = (plane + core * 2**plane_bits, turned + core * 2**plane_bits)
+        self.plane_bits, self.half = plane_bits, half
+        self.places = self.places_of(c)
         self.masks = (
             [2 << s for s in range(plane_bits)] + [1],
             [2 << (s + half) % plane_bits for s in range(plane_bits)] + [1],
         )
 
-    def place(self, order):
+    def places_of(self, device):
+        plane, core = device // 2, device % 2
+        turned = plane // 2**self.half + plane % 2**self.half * 2 ** (self.plane_bits - self.half)
+        top = core * 2**self.plane_bits
+        return plane + top, turned + top
+
+    def place(self, order, device=None):
+        places = self.places if device is None else self.places_of(device)
         if isinstance(order, int):
-            return self.places[order]
-        return jnp.where(order == 0, self.places[0], self.places[1])
+            return places[order]
+        return jnp.where(order == 0, places[0], places[1])
 
     def partner(self, order, stage):
         if isinstance(order, int):
@@ -313,40 +319,90 @@
     def flip(self, mask):
         return self.c + mask * (1 - 2 * (self.c // mask % 2))
 
-    def block(self, order, stage, other=False):
-        index = self.place(order) // 2**stage
+    def flips(self, bits):
+        device = self.c
+        for s in range(self.bits):
+            if bits >> s & 1:
+                device = device + (1 << s) * (1 - 2 * (self.c // (1 << s) % 2))
+        return device
+
+    def block(self, order, stage, other=False, device=None):
+        index = self.place(order, device) // 2**stage
         if other:
             index = index + 1 - 2 * (index % 2)
         size = self.each * 2**stage
         return pl.ds(pl.multiple_of(index * size, size), size)
 
 
+SCHEDULE = (
+    ("send_shards", 1), ("masks",), ("send_shards", 0), ("event", 1, 0, 0), ("first_norm",), ("projection", 0),
+    ("send_shards", 3), ("event", 0, 0, 0), ("event", 1, 1, 0), ("event", 0, 0, 1), ("event", 0, 1, 0),
+    ("event", 0, 2, 0), ("send_shards", 2), ("event", 3, 0, 0), ("event", 1, 2, 0), ("event", 1, 1, 1),
+    ("send_biases",), ("event", 0, 2, 1), ("event", 1, 0, 1), ("event", 0, 0, 2), ("event", 0, 1, 1),
+    ("event", 3, 1, 0), ("event", 0, 0, 3), ("event", 2, 0, 0), ("event", 2, 0, 1), ("event", 2, 1, 0),
+    ("event", 2, 1, 1), ("event", 0, 1, 2), ("attention", 0), ("event", 3, 1, 1), ("event", 3, 1, 2),
+    ("wait_biases",), ("event", 3, 0, 1), ("projection", 1), ("event", 0, 2, 2), ("event", 3, 2, 0),
+    ("event", 1, 1, 2), ("event", 3, 1, 3), ("event", 0, 1, 3), ("projection", 2), ("event", 0, 2, 3),
+    ("event", 3, 0, 2), ("event", 2, 0, 2), ("projection", 3), ("event", 1, 0, 2), ("event", 3, 2, 1),
+    ("event", 3, 2, 2), ("event", 3, 0, 3), ("event", 1, 0, 3), ("event", 2, 2, 0), ("event", 2, 1, 2),
+    ("attention", 1), ("event", 2, 2, 1), ("event", 1, 2, 1), ("attention", 2), ("event", 3, 2, 3), ("attention", 3),
+    ("event", 2, 1, 3), ("second_norm",), ("forth", 0), ("back", 0), ("halve", 2, 0), ("halve", 1, 0),
+    ("event", 2, 0, 3), ("forth", 1), ("event", 2, 2, 2), ("back", 1), ("halve", 1, 1), ("event", 1, 2, 2),
+    ("halve", 2, 1), ("add", 1, 0, 2), ("event", 1, 1, 3), ("forth", 2), ("event", 2, 2, 3), ("add", 1, 1, 2),
+    ("event", 1, 2, 3), ("forth", 3), ("layer_rows",), ("add", 2, 1, 2), ("rows_first", 1), ("add", 2, 0, 2),
+    ("back", 3), ("halve", 1, 3), ("back", 2), ("second_back",), ("out_back", 3), ("out_back", 1), ("out_back", 0),
+    ("halve", 3, 0), ("halve", 2, 2), ("give", 1), ("out_back", 2), ("rows_first", 0), ("give", 0), ("halve", 3, 1),
+    ("give", 3), ("halve", 3, 3), ("halve", 2, 3), ("give", 2), ("add", 3, 1, 2), ("halve", 1, 2), ("add", 3, 3, 2),
+    ("take", 1), ("rows_relay", 1, 0), ("add", 2, 2, 2), ("add", 2, 0, 1), ("halve", 0, 1), ("add", 1, 2, 2),
+    ("take", 0), ("halve", 0, 0), ("rows_relay", 1, 1), ("add", 1, 3, 2), ("take", 3), ("halve", 0, 3),
+    ("halve", 3, 2), ("take", 2), ("halve", 0, 2), ("source",), ("rows_first", 2), ("rows_relay", 0, 1),
+    ("add", 2, 2, 1), ("add", 3, 0, 2), ("add", 1, 0, 1), ("add", 3, 2, 2), ("add", 1, 1, 1), ("add", 2, 3, 2),
+    ("add", 1, 3, 1), ("add", 1, 2, 1), ("add", 2, 1, 1), ("rows_relay", 0, 0), ("add", 3, 1, 1), ("send_sums",),
+    ("add", 3, 2, 1), ("rows_relay", 2, 0), ("add", 2, 2, 0), ("add", 1, 1, 0), ("add", 2, 3, 1), ("add", 0, 2, 2),
+    ("add", 0, 0, 2), ("add", 3, 0, 1), ("add", 0, 1, 2), ("add", 1, 2, 0), ("add", 1, 3, 0), ("add", 0, 3, 2),
+    ("add", 3, 2, 0), ("rows_relay", 2, 1), ("add", 3, 3, 1), ("add", 0, 0, 1), ("add", 3, 1, 0), ("add", 3, 0, 0),
+    ("add", 2, 3, 0), ("add", 1, 0, 0), ("line_over", 1), ("add", 2, 1, 0), ("add", 0, 1, 1), ("add", 0, 3, 1),
+    ("add", 3, 3, 0), ("add", 0, 2, 1), ("add", 0, 0, 0), ("add_sums", 0), ("line_over", 3), ("add", 2, 0, 0),
+    ("rows_wait", 1), ("line_over", 2), ("line_pass", 1), ("add", 0, 1, 0), ("add", 0, 3, 0), ("line_end", 1),
+    ("gather", 1, 0), ("add", 0, 2, 0), ("line_pass", 2), ("line_over", 0), ("gather", 1, 1), ("line_pass", 3),
+    ("rows_first", 3), ("add_sums", 1), ("line_end", 3), ("gather", 3, 0), ("line_end", 2), ("gather", 2, 0),
+    ("gather", 1, 2), ("add_sums", 2), ("line_pass", 0), ("line_end", 0), ("gather", 0, 0), ("gather", 3, 1),
+    ("gather", 2, 1), ("gather", 0, 1), ("rows_relay", 3, 0), ("gather", 2, 2), ("rows_wait", 2), ("gather", 1, 3),
+    ("rows_relay", 3, 1), ("gather", 3, 2), ("gather", 2, 3), ("gather", 0, 2), ("gather", 3, 3), ("add_sums", 3),
+    ("store", 2), ("rows_wait", 0), ("store", 6), ("gather", 0, 3), ("rows_wait", 3), ("store", 1), ("store", 5),
+    ("store", 0), ("store", 3), ("store", 4),
+)
+FIRST_STAGE = (0, 0, 1, 1)
+
+
 def fused(geo, *refs):
     (
         x_hbm, g_hbm, segs, n1g, n1b, q_hbm, q_bias, k_hbm, v_hbm, v_bias, o_hbm, out_bias, n2g, n2b,
         up_hbm, up_bias, down_hbm, down_bias,
-        out_result, out_source, out_grads, out_sums,
-        weights, extra, x, g2, o_own, n1, q, own, cells, near_send, far_send, near_in, far_in,
+        out_result, out_source, out_a, out_u, out_d, out_o, out_sums,
+        w_a, w_u, w_d, w_o, extra, x, g2, o_own, n1, q, own, cells, near_send, far_send, near_in, far_in,
         table, bias, probs, mixed, middle, n2, hidden, slope, result, total, g1, d_mixed, d_queries, d_table,
-        near_give, far_give, near_back, far_back, grads, sums, gathered, source_all,
-        from_line, reduced, sums_in, sums_all, sums_got,
+        g1_low, near_give, far_give, near_back, far_back, g_a, g_u, g_d, g_o, sums, gathered, source_all,
+        line_a, line_u, line_d, line_o, end_a, end_u, end_d, end_o, in_a, in_u, in_d, in_o, r_a, r_u, r_d, r_o, sums_in, sums_all, sums_got,
         load_sem, store_sem, zw_send, zw_recv, pw_send, pw_recv, ex_send, ex_recv, halo_send, halo_recv,
-        far_s, far_r, back_send, back_recv, farb_s, farb_r, rs_send, rs_recv, zl_send, zl_recv,
+        far_s, far_r, back_send, back_recv, farb_s, farb_r, rs_send, rs_recv, zl_send, zl_recv, zx_recv, zy_recv,
         ag_send, ag_recv, out_send, out_recv, sm_send, sm_recv, sc_send, sc_recv,
         *landings,
     ) = refs
+    weights, grads, reduced = (w_a, w_u, w_d, w_o), (g_a, g_u, g_d, g_o), (r_a, r_u, r_d, r_o)
+    from_line, from_end, from_inner = (line_a, line_u, line_d, line_o), (end_a, end_u, end_d, end_o), (in_a, in_u, in_d, in_o)
     C, W = geo.ctx, geo.wt
     c, z = lax.axis_index("ctx"), lax.axis_index("wt")
     plane = Plane(C, c, 512)
     B = plane.bits
 
     loads = [
-        pltpu.make_async_copy(q_hbm, weights.at[0, z, :, pl.ds(0, LANES)], load_sem.at[0]),
-        pltpu.make_async_copy(k_hbm, weights.at[0, z, :, pl.ds(LANES, LANES)], load_sem.at[1]),
-        pltpu.make_async_copy(v_hbm, weights.at[0, z, :, pl.ds(2 * LANES, LANES)], load_sem.at[2]),
+        pltpu.make_async_copy(q_hbm, weights[0].at[z, :, pl.ds(0, LANES)], load_sem.at[0]),
+        pltpu.make_async_copy(k_hbm, weights[0].at[z, :, pl.ds(LANES, LANES)], load_sem.at[1]),
+        pltpu.make_async_copy(v_hbm, weights[0].at[z, :, pl.ds(2 * LANES, LANES)], load_sem.at[2]),
         pltpu.make_async_copy(o_hbm, o_own, load_sem.at[3]),
-        pltpu.make_async_copy(up_hbm, weights.at[1, z], load_sem.at[4]),
-        pltpu.make_async_copy(down_hbm, weights.at[2, z], load_sem.at[5]),
+        pltpu.make_async_copy(up_hbm, weights[1].at[z], load_sem.at[4]),
+        pltpu.make_async_copy(down_hbm, weights[2].at[z], load_sem.at[5]),
         pltpu.make_async_copy(x_hbm.at[z], x, load_sem.at[6]),
         pltpu.make_async_copy(g_hbm.at[z], g2, load_sem.at[7]),
     ]
@@ -369,66 +425,105 @@
         pl.semaphore_signal(barrier, inc=1, device_id=(c, lax.rem(z + step, W)), device_id_type=pl.DeviceIdType.MESH)
     for copy in loads[:4]:
         copy.wait()
-    weights[0, z, :, 3 * LANES :] = o_own[...].T
+    weights[3][z] = o_own[...].T
     pl.semaphore_wait(barrier, C + W - 2)
 
     def order_of(k, w):
         return (k + w) % 2
 
-    def arrival(i):
+    relays = W == 4
+    inner = (z > 0) & (z < W - 1) if relays else jnp.bool_(False)
+    across = jnp.where(z < W // 2, z + 2, z - 2)
+    beside = W - 1 - z
+    end = jnp.where(z < W // 2, 0, W - 1)
+    near_inner = jnp.where(z < W // 2, 1, W - 2)
+
+    def arrival(i, relayed):
         table_of = []
         for at in range(W):
             seen = []
             for step in range(1, W):
                 seen += [w for w in (at - step, at + step) if 0 <= w < W]
+            if relayed and 0 < at < W - 1:
+                seen = [at - 1, at + 2, at + 1] if at < W // 2 else [at + 1, at - 2, at - 1]
             table_of.append(seen[i])
         w = jnp.int32(table_of[0])
         for at in range(1, W):
             w = jnp.where(z == at, table_of[at], w)
         return w
 
-    arrivals = [arrival(i) for i in range(W - 1)]
-
-    def weight_line(k, w, to):
-        rows = plane.block(order_of(k, w), 0)
-        return remote(weights.at[k, w, rows], weights.at[k, w, rows], zw_send.at[k, to], zw_recv.at[k, w], (c, to))
+    relayed_of = (False, relays, relays, relays)
+    first_stage = FIRST_STAGE if B > 2 else (0, 0, 0, 0)
+    arrivals_of = [[arrival(i, relayed) for i in range(W - 1)] for relayed in relayed_of]
+    arrivals = arrivals_of[0]
+
+    def each_direct(action, relayed=relays):
+        for step in range(1, W):
+            to = lax.rem(z + step, W)
+            later = (z + to == W - 1) if relayed else jnp.bool_(False)
+
+            @pl.when(jnp.logical_not(later))
+            def _():
+                action(to)
+
+    def weight_line(k, w, to, relayed=False):
+        rows = plane.block(order_of(k, w), first_stage[k])
+        slot = w if relayed else to
+        return remote(
+            weights[k].at[w, rows], weights[k].at[w, rows], zw_send.at[k, slot, int(relayed)], zw_recv.at[k, w], (c, to)
+        )
 
     def weight_first(k):
-        for step in (1, 2, 3)[: W - 1]:
-            for to, there in ((z - step, z >= step), (z + step, z + step < W)):
-
-                @pl.when(there)
-                def _():
-                    weight_line(k, z, to).start()
-
-    def weight_stage(k, w, s):
+        each_direct(lambda to: weight_line(k, z, to).start(), relayed_of[k])
+
+    def weight_copy(k, w, j, s, landing=False):
         order = order_of(k, w)
-        rows = plane.block(order, s)
-        return remote(
-            weights.at[k, w, rows], weights.at[k, w, rows], pw_send.at[k, w, s], pw_recv.at[k, w, s],
-            (plane.partner(order, s), z),
-        )
+        device = plane.partner(order, s)
+        seen = device if landing else None
+        if j < 0:
+            rows = plane.block(order, first_stage[k], device=seen)
+        else:
+            rows = plane.block(order, j, other=True, device=seen)
+        at = s * (s + 1) // 2 + j + 1
+        block = weights[k].at[w, rows]
+        return remote(block, block, pw_send.at[k, w, at], pw_recv.at[k, w, at], (device, z))
+
+    def held_at(k, s):
+        return [-1, *range(first_stage[k], s)] if s >= first_stage[k] else []
 
     def weight_event(k, i, s):
-        w = arrivals[i]
+        w = arrivals_of[k][i]
         if s == 0:
             weight_line(k, w, lax.rem(z + 1, W)).wait_recv()
+            if i == 1 and relayed_of[k]:
+
+                @pl.when(inner)
+                def _():
+                    weight_line(k, w, end, True).start()
+                    weight_line(k, z, beside).start()
+
+            for later in range(first_stage[k], B):
+                weight_copy(k, w, -1, later).start()
         else:
-            weight_stage(k, w, s - 1).wait_recv()
-        if s < B:
-            weight_stage(k, w, s).start()
-
-    def weight_events(k, s):
-        for i in range(W - 1):
-            weight_event(k, i, s)
+            for j in held_at(k, s - 1):
+                weight_copy(k, w, j, s - 1, True).wait_recv()
+            if s > first_stage[k]:
+                for later in range(s, B):
+                    weight_copy(k, w, s - 1, later).start()
 
     def weight_drain(k):
-        for step in range(1, W):
-            to = lax.rem(z + step, W)
-            weight_line(k, z, to).wait_send()
+        each_direct(lambda to: weight_line(k, z, to).wait_send(), relayed_of[k])
+        if relayed_of[k]:
+
+            @pl.when(inner)
+            def _():
+                weight_line(k, across, end, True).wait_send()
+                weight_line(k, z, beside).wait_send()
+
         for w in arrivals:
             for s in range(B):
-                weight_stage(k, w, s).wait_send()
+                for j in held_at(k, s):
+                    weight_copy(k, w, j, s).wait_send()
 
     def extra_copy(step):
         to = lax.rem(z + step, W)
@@ -502,130 +597,55 @@
 
         each_after(lambda device: give_copy(w, device, device).wait_recv())
 
-    first_three = [z] + arrivals
-
-    def projection(w):
-        project(w, n1, weights, extra, q, own, cells, near_send, far_send)
-        halo_start(w)
-
-    def attention(w):
-        halo_wait(w)
-        tables(geo, w, pick, own, cells, near_in, far_in, table)
-        for tile in (0, 1):
-            attend(geo, w, tile, q, table, bias, probs, mixed)
-
-    weight_first(0)
-    for step in range(1, W):
-        extra_copy(step).start()
-    loads[6].wait()
-    normed, _ = norm_parts(x[...].astype(F32))
-    n1[...] = (normed * n1g[...] + n1b[...]).astype(BF16)
-    projection(z)
-    bias[0] = mask_bias(geo, c, segs[pl.ds(z, 1), :], 0)
-    bias[1] = mask_bias(geo, c, segs[pl.ds(z, 1), :], 1)
-    pick = far_matrix(geo, c)
-    weight_event(0, 0, 0)
-    weight_event(0, 1, 0)
-    weight_event(0, 0, 1)
-    weight_event(0, 2, 0)
-    loads[4].wait()
-    weight_first(1)
-    attention(z)
-    weight_event(0, 1, 1)
-    for step in range(1, W):
-        extra_from(step).wait_recv()
-    weight_event(0, 0, 2)
-    weight_event(0, 2, 1)
-    weight_events(1, 0)
-    loads[5].wait()
-    weight_first(2)
-    for s in range(3, B + 1):
-        weight_event(0, 0, s)
-    projection(arrivals[0])
-    weight_event(0, 1, 2)
-    for s in range(3, B + 1):
-        weight_event(0, 1, s)
-    projection(arrivals[1])
-    weight_event(0, 2, 2)
-    weight_events(1, 1)
-    for s in range(3, B + 1):
-        weight_event(0, 2, s)
-    projection(arrivals[2])
-    attention(arrivals[0])
-    weight_events(2, 0)
-    attention(arrivals[1])
-    weight_events(1, 2)
-    attention(arrivals[2])
-    weight_events(2, 1)
-    for s in range(3, B + 1):
-        weight_events(1, s)
-
-    acc = x[...].astype(F32) + out_bias[...]
-    for w in range(W):
-        acc = acc + dot_nt(mixed[w], weights[0, w, :, 3 * LANES :])
-    middle[...] = acc
-    normed, _ = norm_parts(acc)
-    n2[...] = (normed * n2g[...] + n2b[...]).astype(BF16)
-    result[...] = acc + down_bias[...]
-    feed(z, n2, weights, extra, hidden, slope, result)
-    weight_events(2, 2)
-    for i in range(W - 1):
-        for s in range(3, B + 1):
-            weight_event(2, i, s)
-        feed(arrivals[i], n2, weights, extra, hidden, slope, result)
-    gathered[z] = result[...].astype(BF16)
-
-    def row_copy(at, w, to, relayed=False):
-        rows = (gathered, source_all)[at]
+    def row_copy(part, w, to, relayed=False):
+        rows = (gathered, source_all)[part // 2].at[w, pl.ds(part % 2 * geo.tile, geo.tile)]
         slot = w if relayed else to
-        return remote(rows.at[w], rows.at[w], out_send.at[at, slot, int(relayed)], out_recv.at[at, w], (c, to))
-
-    relays = W == 4
-    inner = (z > 0) & (z < W - 1) if relays else jnp.bool_(False)
-    across = jnp.where(z < W // 2, z + 2, z - 2)
-    beside = W - 1 - z
-    end = jnp.where(z < W // 2, 0, W - 1)
-
-    def each_direct(action):
+        return remote(rows, rows, out_send.at[part, slot, int(relayed)], out_recv.at[part, w], (c, to))
+
+    def each_beside(action):
         for step in range(1, W):
             to = lax.rem(z + step, W)
-            later = (z + to == W - 1) if relays else jnp.bool_(False)
-
-            @pl.when(jnp.logical_not(later))
+            if relays:
+                skip = (z + to == W - 1) & jnp.logical_not(inner) | inner & (to == across)
+            else:
+                skip = jnp.bool_(False)
+
+            @pl.when(jnp.logical_not(skip))
             def _():
                 action(to)
 
-    def rows_first(at):
-        each_direct(lambda to: row_copy(at, z, to).start())
-
-    def rows_relay(at):
+    def rows_first(part):
+        each_beside(lambda to: row_copy(part, z, to).start())
+
+    def rows_relay(part, far):
+        w = across if far else beside
+
         @pl.when(inner)
         def _():
-            row_copy(at, across, end).wait_recv()
-            row_copy(at, across, end, True).start()
-            row_copy(at, z, beside).start()
-
-    def rows_wait(at):
+            row_copy(part, w, end).wait_recv()
+            row_copy(part, w, end, True).start()
+
+    def rows_wait(part):
         for step in range(1, W):
             w = lax.rem(z + step, W)
 
-            @pl.when(jnp.logical_not(inner & (w == across)))
+            @pl.when(jnp.logical_not(inner) | (w == end))
             def _():
-                row_copy(at, w, w).wait_recv()
-
-    def rows_drain(at):
-        each_direct(lambda to: row_copy(at, z, to).wait_send())
+                row_copy(part, w, w).wait_recv()
+
+    def rows_drain(part):
+        each_beside(lambda to: row_copy(part, z, to).wait_send())
 
         @pl.when(inner)
         def _():
-            row_copy(at, across, end, True).wait_send()
-            row_copy(at, z, beside).wait_send()
+            row_copy(part, across, end, True).wait_send()
+            row_copy(part, beside, end, True).wait_send()
 
     def reduce_copy(k, w, s):
         order = order_of(k, w)
         return remote(
-            grads.at[k, w, plane.block(order, s, other=True)],
-            landings[s].at[k, w],
+            grads[k].at[w, plane.block(order, s, other=True)],
+            landings[4 * s + k].at[w],
             rs_send.at[k, w, s],
             rs_recv.at[k, w, s],
             (plane.partner(order, s), z),
@@ -634,20 +654,49 @@
     def reduce_add(k, w, s):
         reduce_copy(k, w, s).wait_recv()
         rows = plane.block(order_of(k, w), s)
-        grads[k, w, rows] = (grads[k, w, rows].astype(F32) + landings[s][k, w].astype(F32)).astype(BF16)
+        grads[k][w, rows] = (grads[k][w, rows].astype(F32) + landings[4 * s + k][w].astype(F32)).astype(BF16)
         if s > 0:
             reduce_copy(k, w, s - 1).start()
         else:
             line_send(k, w)
 
-    def line_copy(k, w):
+    def line_copy(k, w, way=None):
         rows = plane.block(order_of(k, w), 0)
-        return remote(grads.at[k, w, rows], from_line.at[k, z], zl_send.at[k, w], zl_recv.at[k, z], (c, w))
+        if way == "end":
+            return remote(grads[k].at[w, rows], from_end[k], zl_send.at[k, w], zx_recv.at[k], (c, near_inner))
+        if way == "inner":
+            return remote(grads[k].at[w, rows], from_inner[k], zl_send.at[k, w], zy_recv.at[k], (c, beside))
+        return remote(grads[k].at[w, rows], from_line[k].at[z], zl_send.at[k, w], zl_recv.at[k, z], (c, w))
 
     def line_send(k, w):
-        @pl.when(w != z)
+        over = jnp.logical_not(inner) & (w == beside) if relays else jnp.bool_(False)
+        waits = inner & ((w == across) | (w == end))
+
+        @pl.when(over)
+        def _():
+            line_copy(k, w, "end").start()
+
+        @pl.when((w != z) & jnp.logical_not(over | waits))
         def _():
             line_copy(k, w).start()
+
+    def line_add(k, w, landed):
+        rows = plane.block(order_of(k, w), 0)
+        grads[k][w, rows] = (grads[k][w, rows].astype(F32) + landed[k][...].astype(F32)).astype(BF16)
+
+    def line_over(k):
+        @pl.when(inner)
+        def _():
+            line_copy(k, across, "end").wait_recv()
+            line_add(k, across, from_end)
+            line_copy(k, across, "inner").start()
+
+    def line_pass(k):
+        @pl.when(inner)
+        def _():
+            line_copy(k, across, "inner").wait_recv()
+            line_add(k, end, from_inner)
+            line_copy(k, end).start()
 
     def line_drain(k, w):
         @pl.when(w != z)
@@ -659,92 +708,159 @@
 
     def line_end(k):
         rows = own_rows(k)
-        total_now = grads[k, z, rows].astype(F32)
+        total_now = grads[k][z, rows].astype(F32)
         for step in range(1, W):
             source = lax.rem(z + step, W)
-            remote(
-                from_line.at[k, source], from_line.at[k, source], zl_send.at[k, source], zl_recv.at[k, source], (c, source)
-            ).wait_recv()
-            total_now = total_now + from_line[k, source].astype(F32)
-        reduced[k, rows] = total_now.astype(BF16)
-        gather_copy(k, 0).start()
-
-    def gather_copy(k, s):
+            block = from_line[k].at[source]
+            comes = inner | (source == near_inner) if relays else jnp.bool_(True)
+
+            @pl.when(comes)
+            def _():
+                remote(block, block, zl_send.at[k, source], zl_recv.at[k, source], (c, source)).wait_recv()
+
+            total_now = total_now + jnp.where(comes, from_line[k][source].astype(F32), 0.0)
+        reduced[k][rows] = total_now.astype(BF16)
+
+    def gather_copy(k, j, s):
         order = order_of(k, z)
-        rows = plane.block(order, s)
-        return remote(reduced.at[k, rows], reduced.at[k, rows], ag_send.at[k, s], ag_recv.at[k, s], (plane.partner(order, s), z))
-
-    def gather_next(k, s):
-        gather_copy(k, s).wait_recv()
-        if s + 1 < B:
-            gather_copy(k, s + 1).start()
-
-    rows_first(0)
-    loads[7].wait()
-    for w in range(W):
-        feed_back(w == 0, w, g2, weights, n2, hidden, slope, sums, grads, total)
-        reduce_copy(2, w, B - 1).start()
-        reduce_copy(1, w, B - 1).start()
-        if w > 0:
-            reduce_add(2, w - 1, B - 1)
-            reduce_add(1, w - 1, B - 1)
-    normed, inverse = norm_parts(middle[...])
-    d_normed = total[...]
-    wide = g2[...].astype(F32)
-    first = wide + norm_backward(d_normed, normed, inverse, n2g[...])
-    g1[...] = first
-    low = first.astype(BF16)
-    reduce_add(2, W - 1, B - 1)
-    reduce_add(1, W - 1, B - 1)
-    for w in range(W):
-        d_mixed[w] = dot_nn(low, weights[0, w, :, 3 * LANES :]).astype(BF16)
-        grads[0, w, :, 3 * LANES :] = dot_tn(low, mixed[w]).astype(BF16)
-
-    def reduce_both(w, s):
-        reduce_add(2, w, s)
-        reduce_add(1, w, s)
-
-    def give(w):
+        rows = plane.block(order, 0) if j < 0 else plane.block(order, j, other=True)
+        at = s * (s + 1) // 2 + j + 1
+        block = reduced[k].at[rows]
+        return remote(block, block, ag_send.at[k, at], ag_recv.at[k, at], (plane.partner(order, s), z))
+
+    def gather_landing(k, j, s):
+        order = order_of(k, z)
+        device = plane.partner(order, s)
+        rows = plane.block(order, 0, device=device) if j < 0 else plane.block(order, j, other=True, device=device)
+        at = s * (s + 1) // 2 + j + 1
+        block = reduced[k].at[rows]
+        return remote(block, block, ag_send.at[k, at], ag_recv.at[k, at], (device, z))
+
+    def gather_event(k, s):
+        if s > 0:
+            for j in range(-1, s - 1):
+                gather_landing(k, j, s - 1).wait_recv()
+        for later in range(s, B):
+            gather_copy(k, s - 1, later).start()
+
+    def gather_drain(k):
+        for s in range(B):
+            for j in range(-1, s):
+                gather_copy(k, j, s).wait_send()
+
+    held = {}
+    shard_of = [z] + arrivals
+    feed_of = [z] + arrivals_of[2]
+    turn = [w for step in range((W + 1) // 2) for w in dict.fromkeys((step, W - 1 - step))]
+
+    def send_shards(k):
+        for at in {1: (4,), 2: (5,)}.get(k, ()):
+            loads[at].wait()
+        weight_first(k)
+
+    def send_biases():
+        for step in range(1, W):
+            extra_copy(step).start()
+
+    def wait_biases():
+        for step in range(1, W):
+            extra_from(step).wait_recv()
+
+    def first_norm():
+        loads[6].wait()
+        normed, _ = norm_parts(x[...].astype(F32))
+        n1[...] = (normed * n1g[...] + n1b[...]).astype(BF16)
+
+    def masks():
+        bias[0] = mask_bias(geo, c, segs[pl.ds(z, 1), :], 0)
+        bias[1] = mask_bias(geo, c, segs[pl.ds(z, 1), :], 1)
+        held["pick"] = far_matrix(geo, c)
+
+    def projection(i):
+        w = shard_of[i]
+        project(w, n1, weights, extra, q, own, cells, near_send, far_send)
+        halo_start(w)
+
+    def attention(i):
+        w = shard_of[i]
+        halo_wait(w)
+        tables(geo, w, held["pick"], own, cells, near_in, far_in, table)
+        for tile in (0, 1):
+            attend(geo, w, tile, q, table, bias, probs, mixed)
+
+    def event(k, i, s):
+        for stage in {0: [0], 1: [1], 2: range(2, B), 3: [B]}[s]:
+            weight_event(k, i, stage)
+
+    def second_norm():
+        loads[7].wait()
+        acc = x[...].astype(F32) + out_bias[...]
+        for w in range(W):
+            acc = acc + dot_nt(mixed[w], weights[3][w])
+        middle[...] = acc
+        normed, _ = norm_parts(acc)
+        n2[...] = (normed * n2g[...] + n2b[...]).astype(BF16)
+        result[...] = acc + down_bias[...]
+
+    def forth(i):
+        feed(feed_of[i], n2, weights, extra, hidden, slope, result)
+
+    def layer_rows():
+        gathered[z] = result[...].astype(BF16)
+
+    def back(i):
+        first = "total" not in held
+        held["total"] = True
+        feed_back(first, feed_of[i], g2, weights, n2, hidden, slope, sums, grads, total)
+
+    def shard(k, i):
+        return feed_of[i] if k in (1, 2) else turn[i]
+
+    def halve(k, i):
+        reduce_copy(k, shard(k, i), B - 1).start()
+
+    def add(k, i, s):
+        for stage in {2: [B - 1], 1: range(B - 2, 0, -1), 0: [0]}[s]:
+            reduce_add(k, shard(k, i), stage)
+
+    def second_back():
+        hat, inverse = norm_parts(middle[...])
+        d_normed = total[...]
+        wide = g2[...].astype(F32)
+        first = wide + norm_backward(d_normed, hat, inverse, n2g[...])
+        g1[...] = first
+        g1_low[...] = first.astype(BF16)
+        put_sums(geo, sums, 2, jnp.sum(first, axis=0, keepdims=True))
+        put_sums(geo, sums, 3, jnp.sum(d_normed * hat, axis=0, keepdims=True))
+        put_sums(geo, sums, 4, jnp.sum(d_normed, axis=0, keepdims=True))
+        put_sums(geo, sums, 5, jnp.sum(wide, axis=0, keepdims=True))
+        del held["total"]
+
+    def out_back(i):
+        w = turn[i]
+        d_mixed[w] = dot_nn(g1_low[...], weights[3][w]).astype(BF16)
+        grads[3][w] = dot_tn(g1_low[...], mixed[w]).astype(BF16)
+
+    def give(i):
+        w = turn[i]
         for tile in (0, 1):
             attend_back(geo, w, tile, q, table, probs, d_mixed, d_queries, d_table)
-        return_cells(geo, w, pick, d_table, near_give, far_give)
+        return_cells(geo, w, held["pick"], d_table, near_give, far_give)
         give_start(w)
 
-    def take(w):
+    def take(i):
+        w = turn[i]
         give_wait(w)
-        project_back(geo, w == 0, w, weights, n1, d_queries, d_table, near_back, far_back, sums, grads, total)
-        reduce_copy(0, w, B - 1).start()
-
-    give(0)
-    give(1)
-    for s in range(B - 2, 0, -1):
-        reduce_both(0, s)
-    give(2)
-    give(3)
-    for s in range(B - 2, 0, -1):
-        reduce_both(1, s)
-    put_sums(geo, sums, 2, jnp.sum(first, axis=0, keepdims=True))
-    put_sums(geo, sums, 3, jnp.sum(d_normed * normed, axis=0, keepdims=True))
-    put_sums(geo, sums, 4, jnp.sum(d_normed, axis=0, keepdims=True))
-    put_sums(geo, sums, 5, jnp.sum(wide, axis=0, keepdims=True))
-    take(0)
-    take(1)
-    for s in range(B - 2, 0, -1):
-        reduce_both(2, s)
-    reduce_both(0, 0)
-    take(2)
-    take(3)
-    normed, inverse = norm_parts(x[...].astype(F32))
-    d_normed = total[...]
-    source_all[z] = (g1[...] + norm_backward(d_normed, normed, inverse, n1g[...])).astype(BF16)
-    rows_relay(0)
-    for s in range(B - 2, 0, -1):
-        reduce_both(3, s)
-    reduce_both(1, 0)
-    for w in range(W):
-        reduce_add(0, w, B - 1)
-    put_sums(geo, sums, 0, jnp.sum(d_normed * normed, axis=0, keepdims=True))
-    put_sums(geo, sums, 1, jnp.sum(d_normed, axis=0, keepdims=True))
+        first = "total" not in held
+        held["total"] = True
+        project_back(geo, first, w, weights, n1, d_queries, d_table, near_back, far_back, sums, grads, total)
+
+    def source():
+        normed, inverse = norm_parts(x[...].astype(F32))
+        d_normed = total[...]
+        source_all[z] = (g1[...] + norm_backward(d_normed, normed, inverse, n1g[...])).astype(BF16)
+        put_sums(geo, sums, 0, jnp.sum(d_normed * normed, axis=0, keepdims=True))
+        put_sums(geo, sums, 1, jnp.sum(d_normed, axis=0, keepdims=True))
 
     def sums_copy(step):
         to = lax.rem(z + step, W)
@@ -753,60 +869,61 @@
     def sums_stage(s):
         return remote(sums_all.at[s], sums_got.at[s], sc_send.at[s], sc_recv.at[s], (plane.flip(1 << s), z))
 
-    for step in range(1, W):
-        sums_copy(step).start()
-    reduce_both(2, 0)
-    reduce_both(3, 0)
-    rows_first(1)
-    for s in range(B - 2, 0, -1):
-        for w in range(W):
-            reduce_add(0, w, s)
-    line_end(2)
-    line_end(1)
-    for w in range(W):
-        reduce_add(0, w, 0)
-    total_sums = sums[z]
-    for step in range(1, W):
-        sums_copy(step).wait_recv()
-        total_sums = total_sums + sums_in[step]
-    sums_all[0] = total_sums
-    sums_stage(0).start()
-    for s in range(B):
-        sums_stage(s).wait_recv()
-        sums_all[s + 1] = sums_all[s] + sums_got[s]
-        if s + 1 < B:
-            sums_stage(s + 1).start()
-        gather_next(2, s)
-        gather_next(1, s)
-    rows_wait(0)
-    rows_relay(1)
-    line_end(0)
+    def send_sums():
+        for step in range(1, W):
+            sums_copy(step).start()
+
+    def add_sums(s):
+        if s == 0:
+            total_sums = sums[z]
+            for step in range(1, W):
+                sums_copy(step).wait_recv()
+                total_sums = total_sums + sums_in[step]
+            sums_all[0] = total_sums
+            sums_stage(0).start()
+        for stage in {0: [], 1: [0], 2: range(1, B - 1), 3: [B - 1]}[s]:
+            sums_stage(stage).wait_recv()
+            sums_all[stage + 1] = sums_all[stage] + sums_got[stage]
+            if stage + 1 < B:
+                sums_stage(stage + 1).start()
+
+    def gather(k, s):
+        for stage in {0: [0], 1: [1], 2: range(2, B), 3: [B]}[s]:
+            gather_event(k, stage)
+
     stores = [
         pltpu.make_async_copy(gathered, out_result, store_sem.at[0]),
         pltpu.make_async_copy(source_all, out_source, store_sem.at[1]),
         pltpu.make_async_copy(sums_all.at[B], out_sums, store_sem.at[2]),
-        pltpu.make_async_copy(reduced.at[1], out_grads.at[1], store_sem.at[3]),
-        pltpu.make_async_copy(reduced.at[2], out_grads.at[2], store_sem.at[4]),
-        pltpu.make_async_copy(reduced.at[0], out_grads.at[0], store_sem.at[5]),
+        pltpu.make_async_copy(r_a, out_a, store_sem.at[3]),
+        pltpu.make_async_copy(r_u, out_u, store_sem.at[4]),
+        pltpu.make_async_copy(r_d, out_d, store_sem.at[5]),
+        pltpu.make_async_copy(r_o, out_o, store_sem.at[6]),
     ]
-    for at in (0, 2, 3, 4):
-        stores[at].start()
-    for s in range(B):
-        gather_next(0, s)
-    stores[5].start()
-    rows_wait(1)
-    stores[1].start()
-
-    for k in range(3):
+
+    def store(i):
+        stores[i].start()
+
+    steps = {
+        step.__name__: step
+        for step in (
+            send_shards, send_biases, wait_biases, first_norm, masks, projection, attention, event, second_norm, forth,
+            layer_rows, back, halve, add, second_back, out_back, give, take, source, send_sums, add_sums, gather, store,
+            rows_first, rows_relay, rows_wait, line_over, line_pass, line_end,
+        )
+    }
+    for name, *args in SCHEDULE:
+        steps[name](*args)
+
+    for k in range(4):
         weight_drain(k)
         for w in range(W):
             for s in range(B):
                 reduce_copy(k, w, s).wait_send()
             line_drain(k, w)
-        for s in range(B):
-            gather_copy(k, s).wait_send()
-    for at in (0, 1):
-        rows_drain(at)
+        gather_drain(k)
+    for part in range(4):
+        rows_drain(part)
     for step in range(1, W):
         extra_copy(step).wait_send()
         sums_copy(step).wait_send()
@@ -829,19 +946,18 @@
         copy.wait()
 
 
-def unpack(result, source, grads, sums, *outs):
+def unpack(result, source, grads_a, grads_u, grads_d, grads_o, sums, *outs):
     (
         layer_out, input_grad, d_n1g, d_n1b, d_q, d_qb, d_k, d_v, d_vb, d_o, d_ob, d_n2g, d_n2b, d_up, d_upb, d_down, d_db,
     ) = outs
     layer_out[...] = result[...].astype(F32)
     input_grad[...] = source[...].astype(F32)
-    wide = grads[0].astype(F32)
-    d_q[...] = wide[:, :LANES]
-    d_k[...] = wide[:, LANES : 2 * LANES]
-    d_v[...] = wide[:, 2 * LANES : 3 * LANES]
-    d_o[...] = wide[:, 3 * LANES :].T
-    d_up[...] = grads[1].astype(F32)
-    d_down[...] = grads[2].astype(F32)
+    d_q[...] = grads_a[:, :LANES].astype(F32)
+    d_k[...] = grads_a[:, LANES : 2 * LANES].astype(F32)
+    d_v[...] = grads_a[:, 2 * LANES :].astype(F32)
+    d_o[...] = grads_o[...].astype(F32).T
+    d_up[...] = grads_u[...].astype(F32)
+    d_down[...] = grads_d[...].astype(F32)
     for at, out in enumerate((d_n1g, d_n1b, d_ob, d_n2g, d_n2b, d_db)):
         row, lane = 2 + at // 4, at % 4 * LANES
         out[...] = sums[row : row + 1, lane : lane + LANES]
@@ -881,8 +997,9 @@
     vmem, dma = pltpu.VMEM, pltpu.SemaphoreType.DMA
     row = lambda v: v.reshape(1, -1)
     pair = 2 * LANES
+    wide_of = (3 * LANES, hidden, width, LANES)
     scratch = [
-        vmem((3, W, width, width), BF16),
+        *[vmem((W, width, n), BF16) for n in wide_of],
         vmem((W, 8, width), F32),
         vmem((T, width), BF16),
         vmem((T, width), BF16),
@@ -909,25 +1026,28 @@
         vmem((W, T, LANES), BF16),
         vmem((W, T, LANES), BF16),
         vmem((W, 2, S, pair), F32),
+        vmem((T, width), BF16),
         vmem((W, 80, pair), BF16),
         vmem((C, W, 16, pair), BF16),
         vmem((W, 80, pair), BF16),
         vmem((C, W, 16, pair), BF16),
-        vmem((3, W, width, width), BF16),
+        *[vmem((W, width, n), BF16) for n in wide_of],
         vmem((W, 8, width), F32),
         vmem((W, T, width), BF16),
         vmem((W, T, width), BF16),
-        vmem((3, W, each, width), BF16),
-        vmem((3, width, width), BF16),
+        *[vmem((W, each, n), BF16) for n in wide_of],
+        *[vmem((each, n), BF16) for n in wide_of],
+        *[vmem((each, n), BF16) for n in wide_of],
+        *[vmem((width, n), BF16) for n in wide_of],
         vmem((W, 8, width), F32),
         vmem((B + 1, 8, width), F32),
         vmem((B, 8, width), F32),
         dma((8,)),
-        dma((6,)),
-        dma((3, W)),
-        dma((3, W)),
-        dma((3, W, B)),
-        dma((3, W, B)),
+        dma((7,)),
+        dma((4, W, 2)),
+        dma((4, W)),
+        dma((4, W, B * (B + 1) // 2)),
+        dma((4, W, B * (B + 1) // 2)),
         dma((W,)),
         dma((W,)),
         dma((W,)),
@@ -938,37 +1058,39 @@
         dma((W,)),
         dma((C, W)),
         dma((C, W)),
-        dma((3, W, B)),
-        dma((3, W, B)),
-        dma((3, W)),
-        dma((3, W)),
-        dma((3, B)),
-        dma((3, B)),
-        dma((2, W, 2)),
-        dma((2, W)),
+        dma((4, W, B)),
+        dma((4, W, B)),
+        dma((4, W)),
+        dma((4, W)),
+        dma((4,)),
+        dma((4,)),
+        dma((4, B * (B + 1) // 2)),
+        dma((4, B * (B + 1) // 2)),
+        dma((4, W, 2)),
+        dma((4, W)),
         dma((W,)),
         dma((W,)),
         dma((B,)),
         dma((B,)),
-    ] + [vmem((3, W, each * 2**s, width), BF16) for s in range(B)]
+    ] + [vmem((W, each * 2**s, n), BF16) for s in range(B) for n in wide_of]
     far, near = pl.BlockSpec(memory_space=pl.ANY), pl.BlockSpec(memory_space=pltpu.VMEM)
-    result, source, grads, sums = pl.pallas_call(
+    result, source, d_a, d_u, d_d, d_o, sums = pl.pallas_call(
         functools.partial(fused, geo),
         name="fused",
-        out_shape=[sds((W, T, width), BF16), sds((W, T, width), BF16), sds((3, width, width), BF16), sds((8, width), F32)],
+        out_shape=[sds((W, T, width), BF16), sds((W, T, width), BF16), *[sds((width, n), BF16) for n in wide_of], sds((8, width), F32)],
         in_specs=[far, far, near, near, near, far, near, far, far, near, far, near, near, near, far, near, far, near],
-        out_specs=[far] * 4,
+        out_specs=[far] * 7,
         scratch_shapes=scratch,
         compiler_params=pltpu.CompilerParams(collective_id=0, has_side_effects=True, vmem_limit_bytes=58 * 2**20),
     )(
         x_in, grad_out, seg_ids, row(norm1_gain), row(norm1_bias), q_weight, row(q_bias), k_weight, v_weight, row(v_bias),
         out_weight, row(out_bias), row(norm2_gain), row(norm2_bias), up_weight, row(up_bias), down_weight, row(down_bias),
     )
-    part = width // W
+    part, half = width // 2, W // 2
     rows = lambda shape: pl.BlockSpec(shape, lambda i: (i, 0))
     still = lambda shape: pl.BlockSpec(shape, lambda i: (0, 0))
     one, wide = (sds((1, LANES), F32), still((1, LANES))), (sds((1, hidden), F32), still((1, hidden)))
-    blocks = (sds((W, T, width), F32), pl.BlockSpec((1, T, width), lambda i: (i, 0, 0)))
+    blocks = (sds((W, T, width), F32), pl.BlockSpec((half, T, width), lambda i: (i, 0, 0)))
     thin = (sds((width, LANES), F32), rows((part, LANES)))
     full = (sds((width, width), F32), rows((part, width)))
     turned = (sds((LANES, width), F32), pl.BlockSpec((LANES, part), lambda i: (0, i)))
@@ -976,11 +1098,11 @@
     values = pl.pallas_call(
         unpack,
         name="unpack",
-        grid=(W,),
+        grid=(2,),
         out_shape=[o[0] for o in outs],
-        in_specs=[blocks[1], blocks[1], pl.BlockSpec((3, part, width), lambda i: (0, i, 0)), still((8, width))],
+        in_specs=[blocks[1], blocks[1], *[rows((part, n)) for n in wide_of], still((8, width))],
         out_specs=[o[1] for o in outs],
-    )(result, source, grads, sums)
+    )(result, source, d_a, d_u, d_d, d_o, sums)
     return tuple(v.reshape(-1) if v.shape[0] == 1 else v for v in values)
 
 

time: 127 us -> 107 us (0.84)
  the two profiles are of different devices: /device:TPU:25 before, /device:TPU:0 now
where the time goes in v4:
time: 107 us; the launch traced here: 106 us
  Pallas kernels  106 us (99%)
    pallas_call x1, Pallas kernels, shards(): pl.pallas_call(functools.partial(fused, geo), name='fused', out_shape=[sd...  101 us
    pallas_call x1, Pallas kernels, shards(): pl.pallas_call(unpack, name='unpack', grid=(2,), out_shape=[o[0] for o in...  4.82 us

profile of v4, /device:TPU:0, one launch (start us, length us, event | category | flops | bytes accessed | tf_op | source)
XLA Modules:
  0.0 106.4 jit_solution(12980991184762705838)
XLA Ops:
  0.7 100.8 %fused.1 = (bf16[4,256,512]{2,1,0:T(8,128)(2,1)}, bf16[4,256,512]{2,1,0:T(8,128)(2,1)}, bf16[512,384]{1,0:T(8,128)(2,1)}, bf16[512,512]{1,0:T(8,128)(2,1)}, bf16...) custom-call(bf16[4,256,512]{2,1,0:T(8,128)(2,1)} %refs_0_.1, bf16[4,256,512]{2,1,0:T(8,128)(2,1)} %refs_1_.1, ...), custom_call_target="tpu_custom_call" | custom-call | tf_op jit(solution)/shard_map/fused/pallas_call | solution.py:1077
  101.5 4.8 %unpack.1 = (f32[4,256,512]{2,1,0:T(8,128)}, f32[4,256,512]{2,1,0:T(8,128)}, f32[1,128]{1,0:T(1,128)}, f32[1,128]{1,0:T(1,128)}, f32[512,128]{1,0:T(8,128)}, /*i...) custom-call(bf16[4,256,512]{2,1,0:T(8,128)(2,1)} %get-tuple-element., ...), custom_call_target="tpu_custom_call" | custom-call | tf_op jit(solution)/shard_map/unpack/pallas_call | solution.py:1098

commit v5 on v4

--- a/solution.py
+++ b/solution.py
@@ -335,58 +335,59 @@
 
 
 SCHEDULE = (
-    ("send_shards", 1), ("masks",), ("send_shards", 0), ("event", 1, 0, 0), ("first_norm",), ("projection", 0),
-    ("send_shards", 3), ("event", 0, 0, 0), ("event", 1, 1, 0), ("event", 0, 0, 1), ("event", 0, 1, 0),
-    ("event", 0, 2, 0), ("send_shards", 2), ("event", 3, 0, 0), ("event", 1, 2, 0), ("event", 1, 1, 1),
-    ("send_biases",), ("event", 0, 2, 1), ("event", 1, 0, 1), ("event", 0, 0, 2), ("event", 0, 1, 1),
-    ("event", 3, 1, 0), ("event", 0, 0, 3), ("event", 2, 0, 0), ("event", 2, 0, 1), ("event", 2, 1, 0),
-    ("event", 2, 1, 1), ("event", 0, 1, 2), ("attention", 0), ("event", 3, 1, 1), ("event", 3, 1, 2),
-    ("wait_biases",), ("event", 3, 0, 1), ("projection", 1), ("event", 0, 2, 2), ("event", 3, 2, 0),
-    ("event", 1, 1, 2), ("event", 3, 1, 3), ("event", 0, 1, 3), ("projection", 2), ("event", 0, 2, 3),
-    ("event", 3, 0, 2), ("event", 2, 0, 2), ("projection", 3), ("event", 1, 0, 2), ("event", 3, 2, 1),
-    ("event", 3, 2, 2), ("event", 3, 0, 3), ("event", 1, 0, 3), ("event", 2, 2, 0), ("event", 2, 1, 2),
-    ("attention", 1), ("event", 2, 2, 1), ("event", 1, 2, 1), ("attention", 2), ("event", 3, 2, 3), ("attention", 3),
-    ("event", 2, 1, 3), ("second_norm",), ("forth", 0), ("back", 0), ("halve", 2, 0), ("halve", 1, 0),
-    ("event", 2, 0, 3), ("forth", 1), ("event", 2, 2, 2), ("back", 1), ("halve", 1, 1), ("event", 1, 2, 2),
-    ("halve", 2, 1), ("add", 1, 0, 2), ("event", 1, 1, 3), ("forth", 2), ("event", 2, 2, 3), ("add", 1, 1, 2),
-    ("event", 1, 2, 3), ("forth", 3), ("layer_rows",), ("add", 2, 1, 2), ("rows_first", 1), ("add", 2, 0, 2),
-    ("back", 3), ("halve", 1, 3), ("back", 2), ("second_back",), ("out_back", 3), ("out_back", 1), ("out_back", 0),
-    ("halve", 3, 0), ("halve", 2, 2), ("give", 1), ("out_back", 2), ("rows_first", 0), ("give", 0), ("halve", 3, 1),
-    ("give", 3), ("halve", 3, 3), ("halve", 2, 3), ("give", 2), ("add", 3, 1, 2), ("halve", 1, 2), ("add", 3, 3, 2),
-    ("take", 1), ("rows_relay", 1, 0), ("add", 2, 2, 2), ("add", 2, 0, 1), ("halve", 0, 1), ("add", 1, 2, 2),
-    ("take", 0), ("halve", 0, 0), ("rows_relay", 1, 1), ("add", 1, 3, 2), ("take", 3), ("halve", 0, 3),
-    ("halve", 3, 2), ("take", 2), ("halve", 0, 2), ("source",), ("rows_first", 2), ("rows_relay", 0, 1),
-    ("add", 2, 2, 1), ("add", 3, 0, 2), ("add", 1, 0, 1), ("add", 3, 2, 2), ("add", 1, 1, 1), ("add", 2, 3, 2),
-    ("add", 1, 3, 1), ("add", 1, 2, 1), ("add", 2, 1, 1), ("rows_relay", 0, 0), ("add", 3, 1, 1), ("send_sums",),
-    ("add", 3, 2, 1), ("rows_relay", 2, 0), ("add", 2, 2, 0), ("add", 1, 1, 0), ("add", 2, 3, 1), ("add", 0, 2, 2),
-    ("add", 0, 0, 2), ("add", 3, 0, 1), ("add", 0, 1, 2), ("add", 1, 2, 0), ("add", 1, 3, 0), ("add", 0, 3, 2),
-    ("add", 3, 2, 0), ("rows_relay", 2, 1), ("add", 3, 3, 1), ("add", 0, 0, 1), ("add", 3, 1, 0), ("add", 3, 0, 0),
-    ("add", 2, 3, 0), ("add", 1, 0, 0), ("line_over", 1), ("add", 2, 1, 0), ("add", 0, 1, 1), ("add", 0, 3, 1),
-    ("add", 3, 3, 0), ("add", 0, 2, 1), ("add", 0, 0, 0), ("add_sums", 0), ("line_over", 3), ("add", 2, 0, 0),
-    ("rows_wait", 1), ("line_over", 2), ("line_pass", 1), ("add", 0, 1, 0), ("add", 0, 3, 0), ("line_end", 1),
-    ("gather", 1, 0), ("add", 0, 2, 0), ("line_pass", 2), ("line_over", 0), ("gather", 1, 1), ("line_pass", 3),
-    ("rows_first", 3), ("add_sums", 1), ("line_end", 3), ("gather", 3, 0), ("line_end", 2), ("gather", 2, 0),
-    ("gather", 1, 2), ("add_sums", 2), ("line_pass", 0), ("line_end", 0), ("gather", 0, 0), ("gather", 3, 1),
-    ("gather", 2, 1), ("gather", 0, 1), ("rows_relay", 3, 0), ("gather", 2, 2), ("rows_wait", 2), ("gather", 1, 3),
-    ("rows_relay", 3, 1), ("gather", 3, 2), ("gather", 2, 3), ("gather", 0, 2), ("gather", 3, 3), ("add_sums", 3),
-    ("store", 2), ("rows_wait", 0), ("store", 6), ("gather", 0, 3), ("rows_wait", 3), ("store", 1), ("store", 5),
-    ("store", 0), ("store", 3), ("store", 4),
+    ("send_shards", 0), ("send_shards", 1), ("first_norm",), ("event", 0, 1, 0), ("send_shards", 3), ("send_biases",),
+    ("projection", 0), ("event", 1, 0, 0), ("event", 0, 0, 0), ("event", 1, 1, 0), ("event", 1, 0, 1),
+    ("event", 0, 0, 1), ("masks",), ("send_shards", 2), ("event", 3, 0, 0), ("event", 3, 0, 1), ("event", 0, 2, 0),
+    ("event", 1, 1, 1), ("event", 3, 1, 0), ("event", 1, 2, 0), ("attention", 0), ("event", 0, 1, 1),
+    ("event", 0, 1, 2), ("event", 0, 2, 1), ("event", 3, 0, 2), ("event", 1, 2, 1), ("wait_biases",),
+    ("event", 2, 0, 0), ("event", 0, 0, 2), ("event", 3, 2, 0), ("event", 0, 0, 3), ("projection", 1),
+    ("event", 3, 2, 1), ("event", 2, 1, 0), ("event", 2, 1, 1), ("event", 0, 1, 3), ("event", 2, 0, 1),
+    ("event", 0, 2, 2), ("event", 0, 2, 3), ("event", 3, 2, 2), ("projection", 3), ("event", 1, 0, 2),
+    ("event", 1, 0, 3), ("projection", 2), ("event", 1, 1, 2), ("event", 3, 1, 1), ("event", 3, 1, 2),
+    ("attention", 1), ("event", 3, 2, 3), ("event", 1, 1, 3), ("event", 3, 1, 3), ("event", 2, 2, 0),
+    ("event", 3, 0, 3), ("event", 1, 2, 2), ("event", 2, 1, 2), ("attention", 3), ("event", 1, 2, 3),
+    ("event", 2, 0, 2), ("attention", 2), ("second_norm",), ("forth", 0), ("event", 2, 1, 3), ("back", 0),
+    ("halve", 1, 0), ("event", 2, 0, 3), ("forth", 1), ("halve", 2, 0), ("forth", 2), ("event", 2, 2, 1),
+    ("event", 2, 2, 2), ("back", 2), ("halve", 2, 2), ("add", 1, 0, 2), ("back", 1), ("event", 2, 2, 3), ("forth", 3),
+    ("layer_rows",), ("add", 2, 0, 2), ("rows_first", 0), ("back", 3), ("second_back",), ("out_back", 0),
+    ("halve", 3, 0), ("out_back", 2), ("halve", 2, 3), ("give", 0), ("rows_first", 1), ("halve", 1, 3),
+    ("out_back", 3), ("halve", 3, 3), ("give", 2), ("give", 3), ("halve", 1, 2), ("out_back", 1), ("give", 1),
+    ("add", 3, 0, 2), ("add", 3, 3, 2), ("take", 0), ("add", 1, 2, 2), ("add", 1, 3, 2), ("rows_relay", 0, 0),
+    ("add", 2, 2, 2), ("halve", 3, 2), ("take", 3), ("halve", 0, 3), ("add", 2, 3, 2), ("add", 2, 0, 1), ("take", 2),
+    ("halve", 1, 1), ("halve", 2, 1), ("take", 1), ("halve", 3, 1), ("rows_relay", 0, 1), ("add", 3, 3, 1),
+    ("source",), ("send_sums",), ("rows_first", 2), ("add", 1, 1, 2), ("halve", 0, 0), ("rows_relay", 1, 0),
+    ("add", 3, 2, 2), ("add", 3, 0, 1), ("add", 1, 2, 1), ("add", 3, 1, 2), ("add", 1, 3, 1), ("add", 2, 3, 1),
+    ("add", 2, 1, 2), ("halve", 0, 1), ("add", 0, 3, 2), ("add", 3, 0, 0), ("add", 0, 1, 2), ("add", 1, 2, 0),
+    ("add", 1, 3, 0), ("add", 3, 2, 1), ("add", 3, 1, 1), ("rows_relay", 2, 0), ("add", 1, 0, 1), ("halve", 0, 2),
+    ("add", 1, 1, 1), ("add", 2, 3, 0), ("add", 2, 1, 1), ("rows_relay", 1, 1), ("add", 3, 2, 0), ("add", 2, 2, 1),
+    ("add", 0, 0, 2), ("add", 1, 0, 0), ("add", 3, 3, 0), ("add", 1, 1, 0), ("line_over", 1), ("add_sums", 0),
+    ("add_sums", 1), ("add", 2, 0, 0), ("rows_relay", 2, 1), ("add", 2, 1, 0), ("add", 0, 3, 1), ("add", 0, 2, 2),
+    ("add", 2, 2, 0), ("add", 3, 1, 0), ("line_over", 2), ("rows_wait", 1), ("add", 0, 0, 1), ("add", 0, 1, 1),
+    ("line_pass", 1), ("rows_first", 3), ("line_pass", 2), ("add", 0, 2, 1), ("add_sums", 2), ("add_sums", 3),
+    ("add", 0, 1, 0), ("add", 0, 0, 0), ("line_end", 1), ("gather", 1, 0), ("store", 2), ("line_end", 2),
+    ("gather", 2, 0), ("line_end", 3), ("add", 0, 2, 0), ("gather", 3, 0), ("add", 0, 3, 0), ("rows_relay", 3, 1),
+    ("gather", 1, 1), ("gather", 2, 1), ("line_end", 0), ("rows_relay", 3, 0), ("gather", 0, 0), ("rows_wait", 0),
+    ("store", 0), ("gather", 3, 1), ("rows_wait", 2), ("gather", 2, 2), ("gather", 2, 3), ("gather", 3, 2),
+    ("gather", 1, 2), ("gather", 0, 1), ("gather", 1, 3), ("store", 6), ("store", 5), ("gather", 0, 2), ("store", 3),
+    ("rows_wait", 3), ("store", 1), ("store", 4),
 )
 FIRST_STAGE = (0, 0, 1, 1)
+WAYS = (1, 1, 1, 1)
 
 
 def fused(geo, *refs):
     (
-        x_hbm, g_hbm, segs, n1g, n1b, q_hbm, q_bias, k_hbm, v_hbm, v_bias, o_hbm, out_bias, n2g, n2b,
-        up_hbm, up_bias, down_hbm, down_bias,
+        x_hbm, g_hbm, segs_hbm, n1g_hbm, n1b_hbm, q_hbm, q_bias_hbm, k_hbm, v_hbm, v_bias_hbm, o_hbm, out_bias_hbm,
+        n2g_hbm, n2b_hbm, up_hbm, up_bias_hbm, down_hbm, down_bias_hbm,
         out_result, out_source, out_a, out_u, out_d, out_o, out_sums,
+        segs, n1g, n1b, q_bias, v_bias, out_bias, n2g, n2b, up_bias, down_bias,
         w_a, w_u, w_d, w_o, extra, x, g2, o_own, n1, q, own, cells, near_send, far_send, near_in, far_in,
         table, bias, probs, mixed, middle, n2, hidden, slope, result, total, g1, d_mixed, d_queries, d_table,
         g1_low, near_give, far_give, near_back, far_back, g_a, g_u, g_d, g_o, sums, gathered, source_all,
         line_a, line_u, line_d, line_o, end_a, end_u, end_d, end_o, in_a, in_u, in_d, in_o, r_a, r_u, r_d, r_o, sums_in, sums_all, sums_got,
-        load_sem, store_sem, zw_send, zw_recv, pw_send, pw_recv, ex_send, ex_recv, halo_send, halo_recv,
+        load_sem, small_sem, store_sem, zw_send, zw_recv, pw_send, pw_recv, ex_send, ex_recv, halo_send, halo_recv,
         far_s, far_r, back_send, back_recv, farb_s, farb_r, rs_send, rs_recv, zl_send, zl_recv, zx_recv, zy_recv,
-        ag_send, ag_recv, out_send, out_recv, sm_send, sm_recv, sc_send, sc_recv,
+        ag_send, ag_recv, gp_send, gp_recv, gc_send, gc_recv, out_send, out_recv, sm_send, sm_recv, sc_send, sc_recv,
         *landings,
     ) = refs
     weights, grads, reduced = (w_a, w_u, w_d, w_o), (g_a, g_u, g_d, g_o), (r_a, r_u, r_d, r_o)
@@ -406,26 +407,30 @@
         pltpu.make_async_copy(x_hbm.at[z], x, load_sem.at[6]),
         pltpu.make_async_copy(g_hbm.at[z], g2, load_sem.at[7]),
     ]
-    for copy in loads:
+    small = [
+        pltpu.make_async_copy(source, target, small_sem.at[at])
+        for at, (source, target) in enumerate(
+            (
+                (q_bias_hbm, q_bias), (v_bias_hbm, v_bias), (up_bias_hbm, up_bias), (n1g_hbm, n1g), (n1b_hbm, n1b),
+                (segs_hbm, segs), (out_bias_hbm, out_bias), (n2g_hbm, n2g), (n2b_hbm, n2b), (down_bias_hbm, down_bias),
+            )
+        )
+    ]
+
+    for copy in loads + small:
         copy.start()
     near_in[...] = jnp.zeros_like(near_in)
     far_in[...] = jnp.zeros_like(far_in)
     near_back[...] = jnp.zeros_like(near_back)
     far_back[...] = jnp.zeros_like(far_back)
-    sums[...] = jnp.zeros_like(sums)
-    extra[z] = jnp.zeros_like(extra[z])
-    extra[z, 0:1, :] = up_bias[...]
-    extra[z, 1:2, :LANES] = q_bias[...]
-    extra[z, 1:2, LANES : 2 * LANES] = v_bias[...]
 
     barrier = pltpu.get_barrier_semaphore()
     for step in range(1, C):
         pl.semaphore_signal(barrier, inc=1, device_id=(lax.rem(c + step, C), z), device_id_type=pl.DeviceIdType.MESH)
     for step in range(1, W):
         pl.semaphore_signal(barrier, inc=1, device_id=(c, lax.rem(z + step, W)), device_id_type=pl.DeviceIdType.MESH)
-    for copy in loads[:4]:
-        copy.wait()
-    weights[3][z] = o_own[...].T
+    sums[...] = jnp.zeros_like(sums)
+    extra[z] = jnp.zeros_like(extra[z])
     pl.semaphore_wait(barrier, C + W - 2)
 
     def order_of(k, w):
@@ -438,43 +443,50 @@
     end = jnp.where(z < W // 2, 0, W - 1)
     near_inner = jnp.where(z < W // 2, 1, W - 2)
 
-    def arrival(i, relayed):
+    def arrival(i, way):
         table_of = []
         for at in range(W):
             seen = []
             for step in range(1, W):
                 seen += [w for w in (at - step, at + step) if 0 <= w < W]
-            if relayed and 0 < at < W - 1:
+            if way == 1 and 0 < at < W - 1:
                 seen = [at - 1, at + 2, at + 1] if at < W // 2 else [at + 1, at - 2, at - 1]
+            if way == 2 and 0 < at < W - 1:
+                seen = [at - 1, at + 1, at + 2] if at < W // 2 else [at + 1, at - 1, at - 2]
             table_of.append(seen[i])
         w = jnp.int32(table_of[0])
         for at in range(1, W):
             w = jnp.where(z == at, table_of[at], w)
         return w
 
-    relayed_of = (False, relays, relays, relays)
+    ways = WAYS if relays else (0, 0, 0, 0)
     first_stage = FIRST_STAGE if B > 2 else (0, 0, 0, 0)
-    arrivals_of = [[arrival(i, relayed) for i in range(W - 1)] for relayed in relayed_of]
+    arrivals_of = [[arrival(i, way) for i in range(W - 1)] for way in ways]
     arrivals = arrivals_of[0]
 
-    def each_direct(action, relayed=relays):
+    def each_direct(action, way):
         for step in range(1, W):
-            to = lax.rem(z + step, W)
-            later = (z + to == W - 1) if relayed else jnp.bool_(False)
-
-            @pl.when(jnp.logical_not(later))
-            def _():
-                action(to)
-
-    def weight_line(k, w, to, relayed=False):
+            for to, there in ((z - step, z >= step), (z + step, z + step < W)):
+                skip = jnp.bool_(False)
+                if way == 1:
+                    skip = z + to == W - 1
+                if way == 2:
+                    skip = (z + to == W - 1) & jnp.logical_not(inner) | inner & (to == across)
+
+                @pl.when(there & jnp.logical_not(skip))
+                def _():
+                    action(to)
+
+    def weight_line(k, w, to, relayed=False, own=False):
         rows = plane.block(order_of(k, w), first_stage[k])
         slot = w if relayed else to
+        mine = {1: up_hbm, 2: down_hbm}.get(k) if own else None
         return remote(
-            weights[k].at[w, rows], weights[k].at[w, rows], zw_send.at[k, slot, int(relayed)], zw_recv.at[k, w], (c, to)
+            weights[k].at[w, rows] if mine is None else mine.at[rows], weights[k].at[w, rows], zw_send.at[k, slot, int(relayed)], zw_recv.at[k, w], (c, to)
         )
 
     def weight_first(k):
-        each_direct(lambda to: weight_line(k, z, to).start(), relayed_of[k])
+        each_direct(lambda to: weight_line(k, z, to, own=True).start(), ways[k])
 
     def weight_copy(k, w, j, s, landing=False):
         order = order_of(k, w)
@@ -495,12 +507,18 @@
         w = arrivals_of[k][i]
         if s == 0:
             weight_line(k, w, lax.rem(z + 1, W)).wait_recv()
-            if i == 1 and relayed_of[k]:
+            if i == 1 and ways[k] == 1:
 
                 @pl.when(inner)
                 def _():
                     weight_line(k, w, end, True).start()
-                    weight_line(k, z, beside).start()
+                    weight_line(k, z, beside, own=True).start()
+
+            if i > 0 and ways[k] == 2:
+
+                @pl.when(inner)
+                def _():
+                    weight_line(k, w, end, True).start()
 
             for later in range(first_stage[k], B):
                 weight_copy(k, w, -1, later).start()
@@ -512,13 +530,16 @@
                     weight_copy(k, w, s - 1, later).start()
 
     def weight_drain(k):
-        each_direct(lambda to: weight_line(k, z, to).wait_send(), relayed_of[k])
-        if relayed_of[k]:
+        each_direct(lambda to: weight_line(k, z, to, own=True).wait_send(), ways[k])
+        if ways[k]:
 
             @pl.when(inner)
             def _():
                 weight_line(k, across, end, True).wait_send()
-                weight_line(k, z, beside).wait_send()
+                if ways[k] == 1:
+                    weight_line(k, z, beside, own=True).wait_send()
+                else:
+                    weight_line(k, beside, end, True).wait_send()
 
         for w in arrivals:
             for s in range(B):
@@ -602,20 +623,8 @@
         slot = w if relayed else to
         return remote(rows, rows, out_send.at[part, slot, int(relayed)], out_recv.at[part, w], (c, to))
 
-    def each_beside(action):
-        for step in range(1, W):
-            to = lax.rem(z + step, W)
-            if relays:
-                skip = (z + to == W - 1) & jnp.logical_not(inner) | inner & (to == across)
-            else:
-                skip = jnp.bool_(False)
-
-            @pl.when(jnp.logical_not(skip))
-            def _():
-                action(to)
-
     def rows_first(part):
-        each_beside(lambda to: row_copy(part, z, to).start())
+        each_direct(lambda to: row_copy(part, z, to).start(), 2 if relays else 0)
 
     def rows_relay(part, far):
         w = across if far else beside
@@ -634,7 +643,7 @@
                 row_copy(part, w, w).wait_recv()
 
     def rows_drain(part):
-        each_beside(lambda to: row_copy(part, z, to).wait_send())
+        each_direct(lambda to: row_copy(part, z, to).wait_send(), 2 if relays else 0)
 
         @pl.when(inner)
         def _():
@@ -668,9 +677,11 @@
             return remote(grads[k].at[w, rows], from_inner[k], zl_send.at[k, w], zy_recv.at[k], (c, beside))
         return remote(grads[k].at[w, rows], from_line[k].at[z], zl_send.at[k, w], zl_recv.at[k, z], (c, w))
 
+    chained = (False, relays, relays, False)
+
     def line_send(k, w):
-        over = jnp.logical_not(inner) & (w == beside) if relays else jnp.bool_(False)
-        waits = inner & ((w == across) | (w == end))
+        over = jnp.logical_not(inner) & (w == beside) if chained[k] else jnp.bool_(False)
+        waits = inner & ((w == across) | (w == end)) if chained[k] else jnp.bool_(False)
 
         @pl.when(over)
         def _():
@@ -712,7 +723,7 @@
         for step in range(1, W):
             source = lax.rem(z + step, W)
             block = from_line[k].at[source]
-            comes = inner | (source == near_inner) if relays else jnp.bool_(True)
+            comes = inner | (source == near_inner) if chained[k] else jnp.bool_(True)
 
             @pl.when(comes)
             def _():
@@ -736,7 +747,31 @@
         block = reduced[k].at[rows]
         return remote(block, block, ag_send.at[k, at], ag_recv.at[k, at], (device, z))
 
+    def gather_plane(k, offset, landing=False):
+        device = plane.flips(2 * offset)
+        block = reduced[k].at[plane.block(order_of(k, z), 0, device=device if landing else None)]
+        return remote(block, block, gp_send.at[k, offset], gp_recv.at[k, offset], (device, z))
+
+    def gather_core(k, offset, landing=False):
+        block = reduced[k].at[plane.block(order_of(k, z), 0, device=plane.flips(2 * offset + int(landing)))]
+        return remote(block, block, gc_send.at[k, offset], gc_recv.at[k, offset], (plane.flips(1), z))
+
+    straight = (True, False, False, True)
+
     def gather_event(k, s):
+        if straight[k]:
+            offsets = range(1, C // 2) if s < 2 else range(C // 2)
+            for offset in offsets:
+                if s == 0:
+                    gather_plane(k, offset).start()
+                elif s == 1:
+                    gather_plane(k, offset, True).wait_recv()
+                    gather_core(k, offset).start()
+                elif s == 2:
+                    gather_core(k, offset, True).wait_recv()
+            if s == 0:
+                gather_core(k, 0).start()
+            return
         if s > 0:
             for j in range(-1, s - 1):
                 gather_landing(k, j, s - 1).wait_recv()
@@ -744,6 +779,12 @@
             gather_copy(k, s - 1, later).start()
 
     def gather_drain(k):
+        if straight[k]:
+            for offset in range(C // 2):
+                if offset:
+                    gather_plane(k, offset).wait_send()
+                gather_core(k, offset).wait_send()
+            return
         for s in range(B):
             for j in range(-1, s):
                 gather_copy(k, j, s).wait_send()
@@ -754,11 +795,18 @@
     turn = [w for step in range((W + 1) // 2) for w in dict.fromkeys((step, W - 1 - step))]
 
     def send_shards(k):
-        for at in {1: (4,), 2: (5,)}.get(k, ()):
+        for at in {0: (0, 1, 2), 3: (3,)}.get(k, ()):
             loads[at].wait()
+        if k == 3:
+            weights[3][z] = o_own[...].T
         weight_first(k)
 
     def send_biases():
+        for at in (0, 1, 2):
+            small[at].wait()
+        extra[z, 0:1, :] = up_bias[...]
+        extra[z, 1:2, :LANES] = q_bias[...]
+        extra[z, 1:2, LANES : 2 * LANES] = v_bias[...]
         for step in range(1, W):
             extra_copy(step).start()
 
@@ -768,10 +816,13 @@
 
     def first_norm():
         loads[6].wait()
+        small[3].wait()
+        small[4].wait()
         normed, _ = norm_parts(x[...].astype(F32))
         n1[...] = (normed * n1g[...] + n1b[...]).astype(BF16)
 
     def masks():
+        small[5].wait()
         bias[0] = mask_bias(geo, c, segs[pl.ds(z, 1), :], 0)
         bias[1] = mask_bias(geo, c, segs[pl.ds(z, 1), :], 1)
         held["pick"] = far_matrix(geo, c)
@@ -793,7 +844,10 @@
             weight_event(k, i, stage)
 
     def second_norm():
-        loads[7].wait()
+        for at in (4, 5, 7):
+            loads[at].wait()
+        for at in range(6, 10):
+            small[at].wait()
         acc = x[...].astype(F32) + out_bias[...]
         for w in range(W):
             acc = acc + dot_nt(mixed[w], weights[3][w])
@@ -946,24 +1000,57 @@
         copy.wait()
 
 
-def unpack(result, source, grads_a, grads_u, grads_d, grads_o, sums, *outs):
-    (
-        layer_out, input_grad, d_n1g, d_n1b, d_q, d_qb, d_k, d_v, d_vb, d_o, d_ob, d_n2g, d_n2b, d_up, d_upb, d_down, d_db,
-    ) = outs
-    layer_out[...] = result[...].astype(F32)
-    input_grad[...] = source[...].astype(F32)
-    d_q[...] = grads_a[:, :LANES].astype(F32)
-    d_k[...] = grads_a[:, LANES : 2 * LANES].astype(F32)
-    d_v[...] = grads_a[:, 2 * LANES :].astype(F32)
-    d_o[...] = grads_o[...].astype(F32).T
-    d_up[...] = grads_u[...].astype(F32)
-    d_down[...] = grads_d[...].astype(F32)
-    for at, out in enumerate((d_n1g, d_n1b, d_ob, d_n2g, d_n2b, d_db)):
+def unpack(
+    result_in, source_in, a_in, u_in, d_in, o_in, sums_in,
+    result_out, source_out, d_n1g, d_n1b, d_q, d_qb, d_k, d_v, d_vb, d_o, d_ob, d_n2g, d_n2b, d_up, d_upb, d_down, d_db,
+    result, source, a, u, d, o, sums, result_f, source_f, a_f, o_f, u_f, d_f, row_f, load_sem, store_sem,
+):
+    runs = result.shape[0]
+    pairs = [(result_in.at[m], result.at[m]) for m in range(runs)] + [(source_in.at[m], source.at[m]) for m in range(runs)]
+    pairs += [(a_in, a), (u_in, u), (d_in, d), (o_in, o), (sums_in, sums)]
+    loads = [pltpu.make_async_copy(*pair, load_sem.at[at]) for at, pair in enumerate(pairs)]
+    for copy in loads:
+        copy.start()
+    stores = []
+
+    def put(held, target):
+        copy = pltpu.make_async_copy(held, target, store_sem.at[len(stores)])
+        copy.start()
+        stores.append(copy)
+
+    for m in range(runs):
+        loads[m].wait()
+        result_f[m] = result[m].astype(F32)
+        put(result_f.at[m], result_out.at[m])
+    for m in range(runs):
+        loads[runs + m].wait()
+        source_f[m] = source[m].astype(F32)
+        put(source_f.at[m], source_out.at[m])
+    loads[2 * runs].wait()
+    for at, target in enumerate((d_q, d_k, d_v)):
+        a_f[at] = a[:, at * LANES : (at + 1) * LANES].astype(F32)
+        put(a_f.at[at], target)
+    loads[2 * runs + 1].wait()
+    u_f[...] = u[...].astype(F32)
+    put(u_f, d_up)
+    loads[2 * runs + 2].wait()
+    d_f[...] = d[...].astype(F32)
+    put(d_f, d_down)
+    loads[2 * runs + 3].wait()
+    o_f[...] = o[...].astype(F32).T
+    put(o_f, d_o)
+    loads[2 * runs + 4].wait()
+    for at, target in enumerate((d_n1g, d_n1b, d_ob, d_n2g, d_n2b, d_db)):
         row, lane = 2 + at // 4, at % 4 * LANES
-        out[...] = sums[row : row + 1, lane : lane + LANES]
-    d_qb[...] = sums[1:2, :LANES]
-    d_vb[...] = sums[1:2, LANES : 2 * LANES]
-    d_upb[...] = sums[0:1, :]
+        row_f[at, :, :LANES] = sums[row : row + 1, lane : lane + LANES]
+        put(row_f.at[at, :, pl.ds(0, LANES)], target)
+    for at, target in ((6, d_qb), (7, d_vb)):
+        row_f[at, :, :LANES] = sums[1:2, (at - 6) * LANES : (at - 5) * LANES]
+        put(row_f.at[at, :, pl.ds(0, LANES)], target)
+    row_f[8] = sums[0:1, :]
+    put(row_f.at[8], d_upb)
+    for copy in stores:
+        copy.wait()
 
 
 def shards(
@@ -999,6 +1086,8 @@
     pair = 2 * LANES
     wide_of = (3 * LANES, hidden, width, LANES)
     scratch = [
+        vmem(seg_ids.shape, jnp.int32),
+        *[vmem((1, n), F32) for n in (width, width, LANES, LANES, width, width, width, hidden, width)],
         *[vmem((W, width, n), BF16) for n in wide_of],
         vmem((W, 8, width), F32),
         vmem((T, width), BF16),
@@ -1043,6 +1132,7 @@
         vmem((B + 1, 8, width), F32),
         vmem((B, 8, width), F32),
         dma((8,)),
+        dma((10,)),
         dma((7,)),
         dma((4, W, 2)),
         dma((4, W)),
@@ -1066,6 +1156,10 @@
         dma((4,)),
         dma((4, B * (B + 1) // 2)),
         dma((4, B * (B + 1) // 2)),
+        dma((4, C // 2)),
+        dma((4, C // 2)),
+        dma((4, C // 2)),
+        dma((4, C // 2)),
         dma((4, W, 2)),
         dma((4, W)),
         dma((W,)),
@@ -1073,12 +1167,12 @@
         dma((B,)),
         dma((B,)),
     ] + [vmem((W, each * 2**s, n), BF16) for s in range(B) for n in wide_of]
-    far, near = pl.BlockSpec(memory_space=pl.ANY), pl.BlockSpec(memory_space=pltpu.VMEM)
+    far = pl.BlockSpec(memory_space=pl.ANY)
     result, source, d_a, d_u, d_d, d_o, sums = pl.pallas_call(
         functools.partial(fused, geo),
         name="fused",
         out_shape=[sds((W, T, width), BF16), sds((W, T, width), BF16), *[sds((width, n), BF16) for n in wide_of], sds((8, width), F32)],
-        in_specs=[far, far, near, near, near, far, near, far, far, near, far, near, near, near, far, near, far, near],
+        in_specs=[far] * 18,
         out_specs=[far] * 7,
         scratch_shapes=scratch,
         compiler_params=pltpu.CompilerParams(collective_id=0, has_side_effects=True, vmem_limit_bytes=58 * 2**20),
@@ -1086,22 +1180,30 @@
         x_in, grad_out, seg_ids, row(norm1_gain), row(norm1_bias), q_weight, row(q_bias), k_weight, v_weight, row(v_bias),
         out_weight, row(out_bias), row(norm2_gain), row(norm2_bias), up_weight, row(up_bias), down_weight, row(down_bias),
     )
-    part, half = width // 2, W // 2
-    rows = lambda shape: pl.BlockSpec(shape, lambda i: (i, 0))
-    still = lambda shape: pl.BlockSpec(shape, lambda i: (0, 0))
-    one, wide = (sds((1, LANES), F32), still((1, LANES))), (sds((1, hidden), F32), still((1, hidden)))
-    blocks = (sds((W, T, width), F32), pl.BlockSpec((half, T, width), lambda i: (i, 0, 0)))
-    thin = (sds((width, LANES), F32), rows((part, LANES)))
-    full = (sds((width, width), F32), rows((part, width)))
-    turned = (sds((LANES, width), F32), pl.BlockSpec((LANES, part), lambda i: (0, i)))
-    outs = [blocks, blocks, one, one, thin, one, thin, thin, one, turned, one, one, one, full, wide, full, one]
+    one, thin, full = (1, LANES), (width, LANES), (width, width)
+    shapes = [(W, T, width)] * 2 + [one, one, thin, one, thin, thin, one, (LANES, width), one, one, one, full, (1, hidden), full, one]
     values = pl.pallas_call(
         unpack,
         name="unpack",
-        grid=(2,),
-        out_shape=[o[0] for o in outs],
-        in_specs=[blocks[1], blocks[1], *[rows((part, n)) for n in wide_of], still((8, width))],
-        out_specs=[o[1] for o in outs],
+        out_shape=[sds(shape, F32) for shape in shapes],
+        in_specs=[far] * 7,
+        out_specs=[far] * 17,
+        scratch_shapes=[
+            vmem((W, T, width), BF16),
+            vmem((W, T, width), BF16),
+            *[vmem((width, n), BF16) for n in wide_of],
+            vmem((8, width), F32),
+            vmem((W, T, width), F32),
+            vmem((W, T, width), F32),
+            vmem((3, width, LANES), F32),
+            vmem((LANES, width), F32),
+            vmem(full, F32),
+            vmem(full, F32),
+            vmem((9, 1, hidden), F32),
+            dma((2 * W + 5,)),
+            dma((2 * W + 15,)),
+        ],
+        compiler_params=pltpu.CompilerParams(vmem_limit_bytes=58 * 2**20),
     )(result, source, d_a, d_u, d_d, d_o, sums)
     return tuple(v.reshape(-1) if v.shape[0] == 1 else v for v in values)
 

time: 107 us -> 101 us (0.944)
  Pallas kernels: 106 us -> 99.3 us
    pallas_call x1, Pallas kernels: 101 us -> 95.1 us  [shards(): pl.pallas_call(functools.partial(fused, geo), name='fused', out_shape=[sd...]
where the time goes in v5:
time: 101 us; the launch traced here: 100 us
  Pallas kernels  99.3 us (98%)
    pallas_call x1, Pallas kernels, shards(): pl.pallas_call(functools.partial(fused, geo), name='fused', out_shape=[sd...  95.1 us
    pallas_call x1, Pallas kernels, shards(): pl.pallas_call(unpack, name='unpack', out_shape=[sds(shape, F32) for shap...  4.28 us

profile of v5, /device:TPU:0, one launch (start us, length us, event | category | flops | bytes accessed | tf_op | source)
XLA Modules:
  0.0 100.2 jit_solution(568548326105712430)
XLA Ops:
  0.7 95.1 %fused.1 = (bf16[4,256,512]{2,1,0:T(8,128)(2,1)}, bf16[4,256,512]{2,1,0:T(8,128)(2,1)}, bf16[512,384]{1,0:T(8,128)(2,1)}, bf16[512,512]{1,0:T(8,128)(2,1)}, bf16...) custom-call(bf16[4,256,512]{2,1,0:T(8,128)(2,1)} %refs_0_.1, bf16[4,256,512]{2,1,0:T(8,128)(2,1)} %refs_1_.1, ...), custom_call_target="tpu_custom_call" | custom-call | tf_op jit(solution)/shard_map/fused/pallas_call | solution.py:1171
  95.7 4.3 %unpack.1 = (f32[4,256,512]{2,1,0:T(8,128)}, f32[4,256,512]{2,1,0:T(8,128)}, f32[1,128]{1,0:T(1,128)}, f32[1,128]{1,0:T(1,128)}, f32[512,128]{1,0:T(8,128)}, /*i...) custom-call(bf16[4,256,512]{2,1,0:T(8,128)(2,1)} %get-tuple-element., ...), custom_call_target="tpu_custom_call" | custom-call | tf_op jit(solution)/shard_map/unpack/pallas_call | solution.py:1185

commit v6 on v5

--- a/solution.py
+++ b/solution.py
@@ -335,41 +335,44 @@
 
 
 SCHEDULE = (
-    ("send_shards", 0), ("send_shards", 1), ("first_norm",), ("event", 0, 1, 0), ("send_shards", 3), ("send_biases",),
-    ("projection", 0), ("event", 1, 0, 0), ("event", 0, 0, 0), ("event", 1, 1, 0), ("event", 1, 0, 1),
-    ("event", 0, 0, 1), ("masks",), ("send_shards", 2), ("event", 3, 0, 0), ("event", 3, 0, 1), ("event", 0, 2, 0),
-    ("event", 1, 1, 1), ("event", 3, 1, 0), ("event", 1, 2, 0), ("attention", 0), ("event", 0, 1, 1),
-    ("event", 0, 1, 2), ("event", 0, 2, 1), ("event", 3, 0, 2), ("event", 1, 2, 1), ("wait_biases",),
-    ("event", 2, 0, 0), ("event", 0, 0, 2), ("event", 3, 2, 0), ("event", 0, 0, 3), ("projection", 1),
-    ("event", 3, 2, 1), ("event", 2, 1, 0), ("event", 2, 1, 1), ("event", 0, 1, 3), ("event", 2, 0, 1),
-    ("event", 0, 2, 2), ("event", 0, 2, 3), ("event", 3, 2, 2), ("projection", 3), ("event", 1, 0, 2),
-    ("event", 1, 0, 3), ("projection", 2), ("event", 1, 1, 2), ("event", 3, 1, 1), ("event", 3, 1, 2),
-    ("attention", 1), ("event", 3, 2, 3), ("event", 1, 1, 3), ("event", 3, 1, 3), ("event", 2, 2, 0),
-    ("event", 3, 0, 3), ("event", 1, 2, 2), ("event", 2, 1, 2), ("attention", 3), ("event", 1, 2, 3),
-    ("event", 2, 0, 2), ("attention", 2), ("second_norm",), ("forth", 0), ("event", 2, 1, 3), ("back", 0),
-    ("halve", 1, 0), ("event", 2, 0, 3), ("forth", 1), ("halve", 2, 0), ("forth", 2), ("event", 2, 2, 1),
-    ("event", 2, 2, 2), ("back", 2), ("halve", 2, 2), ("add", 1, 0, 2), ("back", 1), ("event", 2, 2, 3), ("forth", 3),
-    ("layer_rows",), ("add", 2, 0, 2), ("rows_first", 0), ("back", 3), ("second_back",), ("out_back", 0),
-    ("halve", 3, 0), ("out_back", 2), ("halve", 2, 3), ("give", 0), ("rows_first", 1), ("halve", 1, 3),
-    ("out_back", 3), ("halve", 3, 3), ("give", 2), ("give", 3), ("halve", 1, 2), ("out_back", 1), ("give", 1),
-    ("add", 3, 0, 2), ("add", 3, 3, 2), ("take", 0), ("add", 1, 2, 2), ("add", 1, 3, 2), ("rows_relay", 0, 0),
-    ("add", 2, 2, 2), ("halve", 3, 2), ("take", 3), ("halve", 0, 3), ("add", 2, 3, 2), ("add", 2, 0, 1), ("take", 2),
-    ("halve", 1, 1), ("halve", 2, 1), ("take", 1), ("halve", 3, 1), ("rows_relay", 0, 1), ("add", 3, 3, 1),
-    ("source",), ("send_sums",), ("rows_first", 2), ("add", 1, 1, 2), ("halve", 0, 0), ("rows_relay", 1, 0),
-    ("add", 3, 2, 2), ("add", 3, 0, 1), ("add", 1, 2, 1), ("add", 3, 1, 2), ("add", 1, 3, 1), ("add", 2, 3, 1),
-    ("add", 2, 1, 2), ("halve", 0, 1), ("add", 0, 3, 2), ("add", 3, 0, 0), ("add", 0, 1, 2), ("add", 1, 2, 0),
-    ("add", 1, 3, 0), ("add", 3, 2, 1), ("add", 3, 1, 1), ("rows_relay", 2, 0), ("add", 1, 0, 1), ("halve", 0, 2),
-    ("add", 1, 1, 1), ("add", 2, 3, 0), ("add", 2, 1, 1), ("rows_relay", 1, 1), ("add", 3, 2, 0), ("add", 2, 2, 1),
-    ("add", 0, 0, 2), ("add", 1, 0, 0), ("add", 3, 3, 0), ("add", 1, 1, 0), ("line_over", 1), ("add_sums", 0),
-    ("add_sums", 1), ("add", 2, 0, 0), ("rows_relay", 2, 1), ("add", 2, 1, 0), ("add", 0, 3, 1), ("add", 0, 2, 2),
-    ("add", 2, 2, 0), ("add", 3, 1, 0), ("line_over", 2), ("rows_wait", 1), ("add", 0, 0, 1), ("add", 0, 1, 1),
-    ("line_pass", 1), ("rows_first", 3), ("line_pass", 2), ("add", 0, 2, 1), ("add_sums", 2), ("add_sums", 3),
-    ("add", 0, 1, 0), ("add", 0, 0, 0), ("line_end", 1), ("gather", 1, 0), ("store", 2), ("line_end", 2),
-    ("gather", 2, 0), ("line_end", 3), ("add", 0, 2, 0), ("gather", 3, 0), ("add", 0, 3, 0), ("rows_relay", 3, 1),
-    ("gather", 1, 1), ("gather", 2, 1), ("line_end", 0), ("rows_relay", 3, 0), ("gather", 0, 0), ("rows_wait", 0),
-    ("store", 0), ("gather", 3, 1), ("rows_wait", 2), ("gather", 2, 2), ("gather", 2, 3), ("gather", 3, 2),
-    ("gather", 1, 2), ("gather", 0, 1), ("gather", 1, 3), ("store", 6), ("store", 5), ("gather", 0, 2), ("store", 3),
-    ("rows_wait", 3), ("store", 1), ("store", 4),
+    ("send_shards", 0), ("first_norm",), ("send_shards", 1), ("send_shards", 3), ("event", 0, 0, 0),
+    ("event", 0, 1, 0), ("event", 1, 0, 0), ("event", 0, 0, 1), ("event", 3, 0, 0), ("send_biases",),
+    ("projection", 0), ("event", 1, 1, 0), ("event", 0, 2, 0), ("event", 3, 1, 0), ("event", 3, 1, 1), ("masks",),
+    ("event", 1, 0, 1), ("send_shards", 2), ("event", 0, 0, 2), ("event", 1, 2, 0), ("event", 0, 1, 1),
+    ("event", 3, 1, 2), ("event", 0, 2, 1), ("event", 1, 1, 1), ("wait_biases",), ("attention", 0),
+    ("event", 0, 0, 3), ("projection", 1), ("event", 3, 2, 0), ("event", 1, 1, 2), ("event", 2, 0, 0),
+    ("event", 2, 0, 1), ("event", 2, 1, 0), ("event", 2, 1, 1), ("event", 0, 1, 2), ("event", 0, 2, 2),
+    ("event", 1, 0, 2), ("event", 1, 0, 3), ("event", 0, 2, 3), ("projection", 3), ("event", 3, 0, 1),
+    ("event", 0, 1, 3), ("event", 3, 2, 1), ("event", 3, 2, 2), ("event", 1, 2, 1), ("projection", 2),
+    ("event", 2, 1, 2), ("event", 2, 2, 0), ("event", 2, 0, 2), ("event", 3, 0, 2), ("event", 3, 0, 3),
+    ("event", 3, 1, 3), ("attention", 1), ("attention", 3), ("event", 3, 2, 3), ("attention", 2), ("second_norm",),
+    ("event", 2, 0, 3), ("forth", 1), ("event", 2, 2, 1), ("event", 2, 2, 2), ("event", 2, 1, 3), ("event", 1, 2, 2),
+    ("forth", 0), ("back", 0), ("halve", 1, 0), ("halve", 2, 0), ("event", 2, 2, 3), ("event", 1, 1, 3),
+    ("event", 1, 2, 3), ("forth", 2), ("back", 2), ("halve", 1, 2), ("forth", 3), ("layer_rows",), ("rows_first", 0),
+    ("back", 1), ("add", 1, 0, 2), ("add", 2, 0, 2), ("back", 3), ("second_back",), ("halve", 2, 3), ("out_back", 1),
+    ("rows_first", 1), ("halve", 2, 1), ("out_back", 0), ("give", 0), ("out_back", 2), ("give", 2), ("out_back", 3),
+    ("give", 1), ("give", 3), ("halve", 3, 0), ("halve", 1, 1), ("add", 3, 0, 2), ("add", 1, 1, 2), ("halve", 1, 3),
+    ("add", 1, 2, 2), ("add", 2, 3, 2), ("rows_relay", 0, 0), ("take", 0), ("add", 1, 3, 2), ("add", 2, 1, 2),
+    ("take", 1), ("take", 2), ("take", 3), ("add", 1, 2, 1), ("rows_relay", 1, 0), ("halve", 0, 2), ("halve", 2, 2),
+    ("source",), ("rows_first", 2), ("settle", 0), ("settle", 3), ("settle", 20), ("add", 2, 3, 1), ("add", 3, 0, 1),
+    ("add", 1, 3, 1), ("add", 1, 0, 1), ("rows_relay", 0, 1), ("send_sums",), ("halve", 3, 1), ("add", 3, 1, 2),
+    ("add", 2, 0, 1), ("add", 0, 2, 2), ("settle", 1), ("add", 3, 0, 0), ("rows_relay", 1, 1), ("halve", 3, 2),
+    ("add", 2, 2, 2), ("add", 2, 3, 0), ("halve", 0, 0), ("add", 1, 3, 0), ("add", 3, 2, 2), ("halve", 0, 1),
+    ("add", 3, 1, 1), ("add", 1, 1, 1), ("halve", 3, 3), ("add", 3, 3, 2), ("add", 1, 0, 0), ("halve", 0, 3),
+    ("add", 2, 1, 1), ("add", 0, 0, 2), ("add", 1, 2, 0), ("add", 2, 0, 0), ("settle", 2), ("settle", 23),
+    ("add", 2, 2, 1), ("rows_relay", 2, 1), ("add", 3, 1, 0), ("add", 1, 1, 0), ("line_over", 1), ("add", 3, 3, 1),
+    ("add_sums", 0), ("add", 0, 1, 2), ("add", 0, 2, 1), ("add", 2, 1, 0), ("settle", 22), ("add", 2, 2, 0),
+    ("line_over", 2), ("add_sums", 1), ("add", 3, 2, 1), ("rows_first", 3), ("add", 0, 2, 0), ("line_pass", 1),
+    ("line_pass", 2), ("add", 0, 3, 2), ("add", 0, 1, 1), ("add", 0, 0, 1), ("rows_relay", 2, 0), ("add_sums", 2),
+    ("settle", 5), ("settle", 6), ("settle", 16), ("settle", 17), ("add", 0, 1, 0), ("add", 0, 3, 1),
+    ("add", 0, 0, 0), ("add", 3, 3, 0), ("line_end", 1), ("gather", 1, 0), ("add", 3, 2, 0), ("line_end", 2),
+    ("gather", 2, 0), ("add", 0, 3, 0), ("settle", 9), ("settle", 10), ("settle", 7), ("gather", 2, 1),
+    ("gather", 1, 1), ("rows_relay", 3, 0), ("rows_wait", 2), ("line_end", 3), ("gather", 3, 0), ("rows_relay", 3, 1),
+    ("settle", 4), ("line_end", 0), ("gather", 0, 0), ("gather", 2, 2), ("gather", 1, 2), ("gather", 3, 1),
+    ("settle", 18), ("settle", 11), ("gather", 0, 1), ("rows_wait", 0), ("settle", 21), ("settle", 8),
+    ("gather", 3, 2), ("add_sums", 3), ("store", 2), ("gather", 1, 3), ("rows_wait", 1), ("store", 0),
+    ("rows_wait", 3), ("store", 1), ("store", 6), ("gather", 2, 3), ("store", 5), ("store", 4), ("settle", 13),
+    ("settle", 14), ("gather", 0, 2), ("store", 3), ("settle", 12), ("settle", 15), ("settle", 19),
 )
 FIRST_STAGE = (0, 0, 1, 1)
 WAYS = (1, 1, 1, 1)
@@ -386,7 +389,7 @@
         g1_low, near_give, far_give, near_back, far_back, g_a, g_u, g_d, g_o, sums, gathered, source_all,
         line_a, line_u, line_d, line_o, end_a, end_u, end_d, end_o, in_a, in_u, in_d, in_o, r_a, r_u, r_d, r_o, sums_in, sums_all, sums_got,
         load_sem, small_sem, store_sem, zw_send, zw_recv, pw_send, pw_recv, ex_send, ex_recv, halo_send, halo_recv,
-        far_s, far_r, back_send, back_recv, farb_s, farb_r, rs_send, rs_recv, zl_send, zl_recv, zx_recv, zy_recv,
+        far_s, far_r, back_send, back_recv, rs_send, rs_recv, zl_send, zl_recv, zx_recv, zy_recv,
         ag_send, ag_recv, gp_send, gp_recv, gc_send, gc_recv, out_send, out_recv, sm_send, sm_recv, sc_send, sc_recv,
         *landings,
     ) = refs
@@ -479,14 +482,23 @@
 
     def weight_line(k, w, to, relayed=False, own=False):
         rows = plane.block(order_of(k, w), first_stage[k])
-        slot = w if relayed else to
+        slot = jnp.where(w == across, z, across) if relayed else to
         mine = {1: up_hbm, 2: down_hbm}.get(k) if own else None
         return remote(
-            weights[k].at[w, rows] if mine is None else mine.at[rows], weights[k].at[w, rows], zw_send.at[k, slot, int(relayed)], zw_recv.at[k, w], (c, to)
+            weights[k].at[w, rows] if mine is None else mine.at[rows], weights[k].at[w, rows], zw_send.at[k, slot], zw_recv.at[k, w], (c, to)
         )
 
     def weight_first(k):
         each_direct(lambda to: weight_line(k, z, to, own=True).start(), ways[k])
+
+    def held_at(k, s):
+        return [-1, *range(first_stage[k], s)] if s >= first_stage[k] else []
+
+    plane_slots = {}
+    for k in range(4):
+        for s in range(B):
+            for j in held_at(k, s):
+                plane_slots[k, j, s] = len(plane_slots)
 
     def weight_copy(k, w, j, s, landing=False):
         order = order_of(k, w)
@@ -496,12 +508,9 @@
             rows = plane.block(order, first_stage[k], device=seen)
         else:
             rows = plane.block(order, j, other=True, device=seen)
-        at = s * (s + 1) // 2 + j + 1
+        at, rank = plane_slots[k, j, s], lax.rem(w - z + W, W) - 1
         block = weights[k].at[w, rows]
-        return remote(block, block, pw_send.at[k, w, at], pw_recv.at[k, w, at], (device, z))
-
-    def held_at(k, s):
-        return [-1, *range(first_stage[k], s)] if s >= first_stage[k] else []
+        return remote(block, block, pw_send.at[at, rank], pw_recv.at[at, rank], (device, z))
 
     def weight_event(k, i, s):
         w = arrivals_of[k][i]
@@ -571,7 +580,7 @@
 
     def give_copy(w, device, source):
         return remote(
-            far_give.at[device, w], far_back.at[source, w], farb_s.at[device, w], farb_r.at[source, w], (device, z)
+            far_give.at[device, w], far_back.at[source, w], far_s.at[device, w], far_r.at[source, w], (device, z)
         )
 
     def each_after(action):
@@ -620,8 +629,8 @@
 
     def row_copy(part, w, to, relayed=False):
         rows = (gathered, source_all)[part // 2].at[w, pl.ds(part % 2 * geo.tile, geo.tile)]
-        slot = w if relayed else to
-        return remote(rows, rows, out_send.at[part, slot, int(relayed)], out_recv.at[part, w], (c, to))
+        slot = jnp.where(w == across, across, z) if relayed else to
+        return remote(rows, rows, out_send.at[part, slot], out_recv.at[part, w], (c, to))
 
     def rows_first(part):
         each_direct(lambda to: row_copy(part, z, to).start(), 2 if relays else 0)
@@ -737,7 +746,7 @@
         rows = plane.block(order, 0) if j < 0 else plane.block(order, j, other=True)
         at = s * (s + 1) // 2 + j + 1
         block = reduced[k].at[rows]
-        return remote(block, block, ag_send.at[k, at], ag_recv.at[k, at], (plane.partner(order, s), z))
+        return remote(block, block, ag_send.at[k - 1, at], ag_recv.at[k - 1, at], (plane.partner(order, s), z))
 
     def gather_landing(k, j, s):
         order = order_of(k, z)
@@ -745,16 +754,16 @@
         rows = plane.block(order, 0, device=device) if j < 0 else plane.block(order, j, other=True, device=device)
         at = s * (s + 1) // 2 + j + 1
         block = reduced[k].at[rows]
-        return remote(block, block, ag_send.at[k, at], ag_recv.at[k, at], (device, z))
+        return remote(block, block, ag_send.at[k - 1, at], ag_recv.at[k - 1, at], (device, z))
 
     def gather_plane(k, offset, landing=False):
         device = plane.flips(2 * offset)
         block = reduced[k].at[plane.block(order_of(k, z), 0, device=device if landing else None)]
-        return remote(block, block, gp_send.at[k, offset], gp_recv.at[k, offset], (device, z))
+        return remote(block, block, gp_send.at[k // 3, offset], gp_recv.at[k // 3, offset], (device, z))
 
     def gather_core(k, offset, landing=False):
         block = reduced[k].at[plane.block(order_of(k, z), 0, device=plane.flips(2 * offset + int(landing)))]
-        return remote(block, block, gc_send.at[k, offset], gc_recv.at[k, offset], (plane.flips(1), z))
+        return remote(block, block, gc_send.at[k // 3, offset], gc_recv.at[k // 3, offset], (plane.flips(1), z))
 
     straight = (True, False, False, True)
 
@@ -958,44 +967,62 @@
     def store(i):
         stores[i].start()
 
+    def reduce_drain(k):
+        for w in range(W):
+            for s in range(B):
+                reduce_copy(k, w, s).wait_send()
+
+    def lines_drain(k):
+        for w in range(W):
+            line_drain(k, w)
+
+    def settle(group):
+        if group < 4:
+            weight_drain(group)
+        elif group < 8:
+            reduce_drain(group - 4)
+        elif group < 12:
+            lines_drain(group - 8)
+        elif group < 16:
+            gather_drain(group - 12)
+        elif group < 20:
+            rows_drain(group - 16)
+        elif group == 20:
+            for step in range(1, W):
+                extra_copy(step).wait_send()
+        elif group == 21:
+            for step in range(1, W):
+                sums_copy(step).wait_send()
+            for s in range(B):
+                sums_stage(s).wait_send()
+        else:
+            for w in range(W):
+                if group == 22:
+
+                    @pl.when(c < C - 1)
+                    def _():
+                        halo(w, False).wait_send()
+
+                    each_after(lambda device: far_copy(w, device, c).wait_send())
+                else:
+
+                    @pl.when(c > 0)
+                    def _():
+                        halo(w, True).wait_send()
+
+                    each_before(lambda device: give_copy(w, device, c).wait_send())
+
     steps = {
         step.__name__: step
         for step in (
             send_shards, send_biases, wait_biases, first_norm, masks, projection, attention, event, second_norm, forth,
             layer_rows, back, halve, add, second_back, out_back, give, take, source, send_sums, add_sums, gather, store,
-            rows_first, rows_relay, rows_wait, line_over, line_pass, line_end,
+            rows_first, rows_relay, rows_wait, line_over, line_pass, line_end, settle,
         )
     }
     for name, *args in SCHEDULE:
         steps[name](*args)
 
-    for k in range(4):
-        weight_drain(k)
-        for w in range(W):
-            for s in range(B):
-                reduce_copy(k, w, s).wait_send()
-            line_drain(k, w)
-        gather_drain(k)
-    for part in range(4):
-        rows_drain(part)
-    for step in range(1, W):
-        extra_copy(step).wait_send()
-        sums_copy(step).wait_send()
-    for s in range(B):
-        sums_stage(s).wait_send()
-
-    for w in range(W):
-
-        @pl.when(c < C - 1)
-        def _():
-            halo(w, False).wait_send()
-
-        @pl.when(c > 0)
-        def _():
-            halo(w, True).wait_send()
-
-        each_after(lambda device: far_copy(w, device, c).wait_send())
-        each_before(lambda device: give_copy(w, device, c).wait_send())
     for copy in stores:
         copy.wait()
 
@@ -1085,6 +1112,7 @@
     row = lambda v: v.reshape(1, -1)
     pair = 2 * LANES
     wide_of = (3 * LANES, hidden, width, LANES)
+    slots = sum(1 + s - f for f in (FIRST_STAGE if B > 2 else (0,) * 4) for s in range(f, B))
     scratch = [
         vmem(seg_ids.shape, jnp.int32),
         *[vmem((1, n), F32) for n in (width, width, LANES, LANES, width, width, width, hidden, width)],
@@ -1134,10 +1162,10 @@
         dma((8,)),
         dma((10,)),
         dma((7,)),
-        dma((4, W, 2)),
         dma((4, W)),
-        dma((4, W, B * (B + 1) // 2)),
-        dma((4, W, B * (B + 1) // 2)),
+        dma((4, W)),
+        dma((slots, W - 1)),
+        dma((slots, W - 1)),
         dma((W,)),
         dma((W,)),
         dma((W,)),
@@ -1146,21 +1174,19 @@
         dma((C, W)),
         dma((W,)),
         dma((W,)),
-        dma((C, W)),
-        dma((C, W)),
         dma((4, W, B)),
         dma((4, W, B)),
         dma((4, W)),
         dma((4, W)),
         dma((4,)),
         dma((4,)),
-        dma((4, B * (B + 1) // 2)),
-        dma((4, B * (B + 1) // 2)),
-        dma((4, C // 2)),
-        dma((4, C // 2)),
-        dma((4, C // 2)),
-        dma((4, C // 2)),
-        dma((4, W, 2)),
+        dma((2, B * (B + 1) // 2)),
+        dma((2, B * (B + 1) // 2)),
+        dma((2, C // 2)),
+        dma((2, C // 2)),
+        dma((2, C // 2)),
+        dma((2, C // 2)),
+        dma((4, W)),
         dma((4, W)),
         dma((W,)),
         dma((W,)),

time: 101 us -> 96.7 us (0.957)
  Pallas kernels: 99.3 us -> 95.7 us
    pallas_call x1, Pallas kernels: 95.1 us -> 91.4 us  [shards(): pl.pallas_call(functools.partial(fused, geo), name='fused', out_shape=[sd...]
where the time goes in v6:
time: 96.7 us; the launch traced here: 96.5 us
  Pallas kernels  95.7 us (99%)
    pallas_call x1, Pallas kernels, shards(): pl.pallas_call(functools.partial(fused, geo), name='fused', out_shape=[sd...  91.4 us
    pallas_call x1, Pallas kernels, shards(): pl.pallas_call(unpack, name='unpack', out_shape=[sds(shape, F32) for shap...  4.28 us

profile of v6, /device:TPU:0, one launch (start us, length us, event | category | flops | bytes accessed | tf_op | source)
XLA Modules:
  0.0 96.5 jit_solution(17214520726386524118)
XLA Ops:
  0.7 91.4 %fused.1 = (bf16[4,256,512]{2,1,0:T(8,128)(2,1)}, bf16[4,256,512]{2,1,0:T(8,128)(2,1)}, bf16[512,384]{1,0:T(8,128)(2,1)}, bf16[512,512]{1,0:T(8,128)(2,1)}, bf16...) custom-call(bf16[4,256,512]{2,1,0:T(8,128)(2,1)} %refs_0_.1, bf16[4,256,512]{2,1,0:T(8,128)(2,1)} %refs_1_.1, ...), custom_call_target="tpu_custom_call" | custom-call | tf_op jit(solution)/shard_map/fused/pallas_call | solution.py:1197
  92.1 4.3 %unpack.1 = (f32[4,256,512]{2,1,0:T(8,128)}, f32[4,256,512]{2,1,0:T(8,128)}, f32[1,128]{1,0:T(1,128)}, f32[1,128]{1,0:T(1,128)}, f32[512,128]{1,0:T(8,128)}, /*i...) custom-call(bf16[4,256,512]{2,1,0:T(8,128)(2,1)} %get-tuple-element., ...), custom_call_target="tpu_custom_call" | custom-call | tf_op jit(solution)/shard_map/unpack/pallas_call | solution.py:1211

commit v7 on v6

--- a/solution.py
+++ b/solution.py
@@ -439,6 +439,9 @@
     def order_of(k, w):
         return (k + w) % 2
 
+    def sent(block, semaphore):
+        pltpu.make_async_copy(block, block, semaphore).wait()
+
     relays = W == 4
     inner = (z > 0) & (z < W - 1) if relays else jnp.bool_(False)
     across = jnp.where(z < W // 2, z + 2, z - 2)
@@ -510,7 +513,7 @@
             rows = plane.block(order, j, other=True, device=seen)
         at, rank = plane_slots[k, j, s], lax.rem(w - z + W, W) - 1
         block = weights[k].at[w, rows]
-        return remote(block, block, pw_send.at[at, rank], pw_recv.at[at, rank], (device, z))
+        return remote(block, block, pw_send.at[k], pw_recv.at[at, rank], (device, z))
 
     def weight_event(k, i, s):
         w = arrivals_of[k][i]
@@ -550,10 +553,7 @@
                 else:
                     weight_line(k, beside, end, True).wait_send()
 
-        for w in arrivals:
-            for s in range(B):
-                for j in held_at(k, s):
-                    weight_copy(k, w, j, s).wait_send()
+        sent(weights[k].at[pl.ds(0, W - 1), pl.ds(0, plane.each * (C - 2 ** first_stage[k]))], pw_send.at[k])
 
     def extra_copy(step):
         to = lax.rem(z + step, W)
@@ -664,7 +664,7 @@
         return remote(
             grads[k].at[w, plane.block(order, s, other=True)],
             landings[4 * s + k].at[w],
-            rs_send.at[k, w, s],
+            rs_send.at[k],
             rs_recv.at[k, w, s],
             (plane.partner(order, s), z),
         )
@@ -681,10 +681,10 @@
     def line_copy(k, w, way=None):
         rows = plane.block(order_of(k, w), 0)
         if way == "end":
-            return remote(grads[k].at[w, rows], from_end[k], zl_send.at[k, w], zx_recv.at[k], (c, near_inner))
+            return remote(grads[k].at[w, rows], from_end[k], zl_send.at[k], zx_recv.at[k], (c, near_inner))
         if way == "inner":
-            return remote(grads[k].at[w, rows], from_inner[k], zl_send.at[k, w], zy_recv.at[k], (c, beside))
-        return remote(grads[k].at[w, rows], from_line[k].at[z], zl_send.at[k, w], zl_recv.at[k, z], (c, w))
+            return remote(grads[k].at[w, rows], from_inner[k], zl_send.at[k], zy_recv.at[k], (c, beside))
+        return remote(grads[k].at[w, rows], from_line[k].at[z], zl_send.at[k], zl_recv.at[k, z], (c, w))
 
     chained = (False, relays, relays, False)
 
@@ -717,11 +717,6 @@
             line_copy(k, across, "inner").wait_recv()
             line_add(k, end, from_inner)
             line_copy(k, end).start()
-
-    def line_drain(k, w):
-        @pl.when(w != z)
-        def _():
-            line_copy(k, w).wait_send()
 
     def own_rows(k):
         return plane.block(order_of(k, z), 0)
@@ -736,7 +731,7 @@
 
             @pl.when(comes)
             def _():
-                remote(block, block, zl_send.at[k, source], zl_recv.at[k, source], (c, source)).wait_recv()
+                remote(block, block, zl_send.at[k], zl_recv.at[k, source], (c, source)).wait_recv()
 
             total_now = total_now + jnp.where(comes, from_line[k][source].astype(F32), 0.0)
         reduced[k][rows] = total_now.astype(BF16)
@@ -746,7 +741,7 @@
         rows = plane.block(order, 0) if j < 0 else plane.block(order, j, other=True)
         at = s * (s + 1) // 2 + j + 1
         block = reduced[k].at[rows]
-        return remote(block, block, ag_send.at[k - 1, at], ag_recv.at[k - 1, at], (plane.partner(order, s), z))
+        return remote(block, block, ag_send.at[k - 1], ag_recv.at[k - 1, at], (plane.partner(order, s), z))
 
     def gather_landing(k, j, s):
         order = order_of(k, z)
@@ -754,16 +749,16 @@
         rows = plane.block(order, 0, device=device) if j < 0 else plane.block(order, j, other=True, device=device)
         at = s * (s + 1) // 2 + j + 1
         block = reduced[k].at[rows]
-        return remote(block, block, ag_send.at[k - 1, at], ag_recv.at[k - 1, at], (device, z))
+        return remote(block, block, ag_send.at[k - 1], ag_recv.at[k - 1, at], (device, z))
 
     def gather_plane(k, offset, landing=False):
         device = plane.flips(2 * offset)
         block = reduced[k].at[plane.block(order_of(k, z), 0, device=device if landing else None)]
-        return remote(block, block, gp_send.at[k // 3, offset], gp_recv.at[k // 3, offset], (device, z))
+        return remote(block, block, gp_send.at[k // 3], gp_recv.at[k // 3, offset], (device, z))
 
     def gather_core(k, offset, landing=False):
         block = reduced[k].at[plane.block(order_of(k, z), 0, device=plane.flips(2 * offset + int(landing)))]
-        return remote(block, block, gc_send.at[k // 3, offset], gc_recv.at[k // 3, offset], (plane.flips(1), z))
+        return remote(block, block, gc_send.at[k // 3], gc_recv.at[k // 3, offset], (plane.flips(1), z))
 
     straight = (True, False, False, True)
 
@@ -789,14 +784,10 @@
 
     def gather_drain(k):
         if straight[k]:
-            for offset in range(C // 2):
-                if offset:
-                    gather_plane(k, offset).wait_send()
-                gather_core(k, offset).wait_send()
-            return
-        for s in range(B):
-            for j in range(-1, s):
-                gather_copy(k, j, s).wait_send()
+            sent(reduced[k].at[pl.ds(0, plane.each * (C // 2 - 1))], gp_send.at[k // 3])
+            sent(reduced[k].at[pl.ds(0, plane.each * (C // 2))], gc_send.at[k // 3])
+        else:
+            sent(reduced[k].at[pl.ds(0, plane.each * (C - 1))], ag_send.at[k - 1])
 
     held = {}
     shard_of = [z] + arrivals
@@ -968,13 +959,10 @@
         stores[i].start()
 
     def reduce_drain(k):
-        for w in range(W):
-            for s in range(B):
-                reduce_copy(k, w, s).wait_send()
+        sent(grads[k].at[:, pl.ds(0, plane.each * (C - 1))], rs_send.at[k])
 
     def lines_drain(k):
-        for w in range(W):
-            line_drain(k, w)
+        sent(reduced[k].at[pl.ds(0, plane.each * (W - 1))], zl_send.at[k])
 
     def settle(group):
         if group < 4:
@@ -1164,7 +1152,7 @@
         dma((7,)),
         dma((4, W)),
         dma((4, W)),
-        dma((slots, W - 1)),
+        dma((4,)),
         dma((slots, W - 1)),
         dma((W,)),
         dma((W,)),
@@ -1174,17 +1162,17 @@
         dma((C, W)),
         dma((W,)),
         dma((W,)),
+        dma((4,)),
         dma((4, W, B)),
-        dma((4, W, B)),
-        dma((4, W)),
+        dma((4,)),
         dma((4, W)),
         dma((4,)),
         dma((4,)),
+        dma((2,)),
         dma((2, B * (B + 1) // 2)),
-        dma((2, B * (B + 1) // 2)),
+        dma((2,)),
         dma((2, C // 2)),
-        dma((2, C // 2)),
-        dma((2, C // 2)),
+        dma((2,)),
         dma((2, C // 2)),
         dma((4, W)),
         dma((4, W)),

time: 96.7 us -> 95.5 us (0.988)
  Pallas kernels: 95.7 us -> 94.5 us
    pallas_call x1, Pallas kernels: 91.4 us -> 90.2 us  [shards(): pl.pallas_call(functools.partial(fused, geo), name='fused', out_shape=[sd...]
where the time goes in v7:
time: 95.5 us; the launch traced here: 95.3 us
  Pallas kernels  94.5 us (99%)
    pallas_call x1, Pallas kernels, shards(): pl.pallas_call(functools.partial(fused, geo), name='fused', out_shape=[sd...  90.2 us
    pallas_call x1, Pallas kernels, shards(): pl.pallas_call(unpack, name='unpack', out_shape=[sds(shape, F32) for shap...  4.28 us

profile of v7, /device:TPU:0, one launch (start us, length us, event | category | flops | bytes accessed | tf_op | source)
XLA Modules:
  0.0 95.3 jit_solution(1957674791361134211)
XLA Ops:
  0.7 90.2 %fused.1 = (bf16[4,256,512]{2,1,0:T(8,128)(2,1)}, bf16[4,256,512]{2,1,0:T(8,128)(2,1)}, bf16[512,384]{1,0:T(8,128)(2,1)}, bf16[512,512]{1,0:T(8,128)(2,1)}, bf16...) custom-call(bf16[4,256,512]{2,1,0:T(8,128)(2,1)} %refs_0_.1, bf16[4,256,512]{2,1,0:T(8,128)(2,1)} %refs_1_.1, ...), custom_call_target="tpu_custom_call" | custom-call | tf_op jit(solution)/shard_map/fused/pallas_call | solution.py:1185
  90.9 4.3 %unpack.1 = (f32[4,256,512]{2,1,0:T(8,128)}, f32[4,256,512]{2,1,0:T(8,128)}, f32[1,128]{1,0:T(1,128)}, f32[1,128]{1,0:T(1,128)}, f32[512,128]{1,0:T(8,128)}, /*i...) custom-call(bf16[4,256,512]{2,1,0:T(8,128)(2,1)} %get-tuple-element., ...), custom_call_target="tpu_custom_call" | custom-call | tf_op jit(solution)/shard_map/unpack/pallas_call | solution.py:1199

commit v8 on v7

--- a/solution.py
+++ b/solution.py
@@ -500,8 +500,8 @@
     plane_slots = {}
     for k in range(4):
         for s in range(B):
-            for j in held_at(k, s):
-                plane_slots[k, j, s] = len(plane_slots)
+            if s >= first_stage[k]:
+                plane_slots[k, s] = len(plane_slots)
 
     def weight_copy(k, w, j, s, landing=False):
         order = order_of(k, w)
@@ -511,7 +511,7 @@
             rows = plane.block(order, first_stage[k], device=seen)
         else:
             rows = plane.block(order, j, other=True, device=seen)
-        at, rank = plane_slots[k, j, s], lax.rem(w - z + W, W) - 1
+        at, rank = plane_slots[k, s], lax.rem(w - z + W, W) - 1
         block = weights[k].at[w, rows]
         return remote(block, block, pw_send.at[k], pw_recv.at[at, rank], (device, z))
 
@@ -535,8 +535,9 @@
             for later in range(first_stage[k], B):
                 weight_copy(k, w, -1, later).start()
         else:
-            for j in held_at(k, s - 1):
-                weight_copy(k, w, j, s - 1, True).wait_recv()
+            if s > first_stage[k]:
+                at, rank = plane_slots[k, s - 1], lax.rem(w - z + W, W) - 1
+                sent(weights[k].at[w, plane.block(order_of(k, w), s - 1, other=True)], pw_recv.at[at, rank])
             if s > first_stage[k]:
                 for later in range(s, B):
                     weight_copy(k, w, s - 1, later).start()
@@ -741,7 +742,7 @@
         rows = plane.block(order, 0) if j < 0 else plane.block(order, j, other=True)
         at = s * (s + 1) // 2 + j + 1
         block = reduced[k].at[rows]
-        return remote(block, block, ag_send.at[k - 1], ag_recv.at[k - 1, at], (plane.partner(order, s), z))
+        return remote(block, block, ag_send.at[k - 1], ag_recv.at[k - 1, s], (plane.partner(order, s), z))
 
     def gather_landing(k, j, s):
         order = order_of(k, z)
@@ -749,7 +750,7 @@
         rows = plane.block(order, 0, device=device) if j < 0 else plane.block(order, j, other=True, device=device)
         at = s * (s + 1) // 2 + j + 1
         block = reduced[k].at[rows]
-        return remote(block, block, ag_send.at[k - 1], ag_recv.at[k - 1, at], (device, z))
+        return remote(block, block, ag_send.at[k - 1], ag_recv.at[k - 1, s], (device, z))
 
     def gather_plane(k, offset, landing=False):
         device = plane.flips(2 * offset)
@@ -777,8 +778,7 @@
                 gather_core(k, 0).start()
             return
         if s > 0:
-            for j in range(-1, s - 1):
-                gather_landing(k, j, s - 1).wait_recv()
+            sent(reduced[k].at[plane.block(order_of(k, z), s - 1, other=True)], ag_recv.at[k - 1, s - 1])
         for later in range(s, B):
             gather_copy(k, s - 1, later).start()
 
@@ -1100,7 +1100,7 @@
     row = lambda v: v.reshape(1, -1)
     pair = 2 * LANES
     wide_of = (3 * LANES, hidden, width, LANES)
-    slots = sum(1 + s - f for f in (FIRST_STAGE if B > 2 else (0,) * 4) for s in range(f, B))
+    slots = sum(B - f for f in (FIRST_STAGE if B > 2 else (0,) * 4))
     scratch = [
         vmem(seg_ids.shape, jnp.int32),
         *[vmem((1, n), F32) for n in (width, width, LANES, LANES, width, width, width, hidden, width)],
@@ -1169,7 +1169,7 @@
         dma((4,)),
         dma((4,)),
         dma((2,)),
-        dma((2, B * (B + 1) // 2)),
+        dma((2, B)),
         dma((2,)),
         dma((2, C // 2)),
         dma((2,)),

time: 95.5 us -> 95.2 us (level)
  no operation moved by 1% of the time
where the time goes in v8:
time: 95.2 us; the launch traced here: 95 us
  Pallas kernels  94.2 us (99%)
    pallas_call x1, Pallas kernels, shards(): pl.pallas_call(functools.partial(fused, geo), name='fused', out_shape=[sd...  89.9 us
    pallas_call x1, Pallas kernels, shards(): pl.pallas_call(unpack, name='unpack', out_shape=[sds(shape, F32) for shap...  4.28 us

profile of v8, /device:TPU:0, one launch (start us, length us, event | category | flops | bytes accessed | tf_op | source)
XLA Modules:
  0.0 95.0 jit_solution(16080631509286386250)
XLA Ops:
  0.7 89.9 %fused.1 = (bf16[4,256,512]{2,1,0:T(8,128)(2,1)}, bf16[4,256,512]{2,1,0:T(8,128)(2,1)}, bf16[512,384]{1,0:T(8,128)(2,1)}, bf16[512,512]{1,0:T(8,128)(2,1)}, bf16...) custom-call(bf16[4,256,512]{2,1,0:T(8,128)(2,1)} %refs_0_.1, bf16[4,256,512]{2,1,0:T(8,128)(2,1)} %refs_1_.1, ...), custom_call_target="tpu_custom_call" | custom-call | tf_op jit(solution)/shard_map/fused/pallas_call | solution.py:1185
  90.6 4.3 %unpack.1 = (f32[4,256,512]{2,1,0:T(8,128)}, f32[4,256,512]{2,1,0:T(8,128)}, f32[1,128]{1,0:T(1,128)}, f32[1,128]{1,0:T(1,128)}, f32[512,128]{1,0:T(8,128)}, /*i...) custom-call(bf16[4,256,512]{2,1,0:T(8,128)(2,1)} %get-tuple-element., ...), custom_call_target="tpu_custom_call" | custom-call | tf_op jit(solution)/shard_map/unpack/pallas_call | solution.py:1199
